TPU v7x, 256 devices: a whole 4x4x8 slice. The times are simulated.
256 devices in a mesh: dp: 64 (over y, z, x_hi), seq: 4 (over x_lo, core).
Axes of the slice: x: 4 (x_hi: 2, x_lo: 2; x = x_hi * 2 + x_lo), y: 4, z: 8, core: 2. Of those that a mesh axis runs over, the one named last changes fastest.
Arguments:
- layer_inputs: bfloat16 [65536, 4096], P(('dp', 'seq')), may hold values from -6 to 6
- output_grads: bfloat16 [65536, 14336], P(('dp', 'seq')), may hold values from -6 to 6
- query_inputs: bfloat16 [64, 8, 4096], P('dp', None, 'seq'), may hold values from -0.09375 to 0.09375
- query_grads: bfloat16 [64, 8, 14336], P('dp', None, 'seq'), may hold values from -0.046875 to 0.046875
- input_eigen: float32 [4096], P('seq'), may hold values from 0.1 to 3
- output_eigen: float32 [14336], P('seq'), may hold values from 0.1 to 3
- doc_index: int32 [64, 1024], P('dp', 'seq'), may hold values from 0 to 7, never falling along the last dimension, each value on 1 to 256 neighbouring positions
- kept_counts: int32 [64, 8], P('dp'), may hold values from 1 to 256
Outputs:
- influence: float32 [64, 512], P('seq', 'dp')
Inputs may be any that keep to these rules, and one draw needn't show every extreme that they name: `doc_index`: in each row document numbers never fall, every document 0 to 7 holds 1 to 256 tokens, and some document holds exactly 256.
All inputs are finite; a program needn't handle non-finite values.
Results may differ from a plain program's by a relative error of at most 0.0041.
Values may be sent and summed in bfloat16 or wider, within the bound.
No kernel may reach another device: no remote copies, remote signals or barrier semaphores. Data moves between devices by JAX's collectives and lax.ppermute only.
A program may use at most 128 MiB of HBM per device.

v0:
```python
import jax
import jax.numpy as jnp
from jax import lax
from jax.sharding import PartitionSpec as P

RANK = 8
DOCS = 8


damping = 0.1


def doc_weights(row_ids, row_kept, length, offset_first):
    positions = offset_first + jnp.arange(row_ids.shape[0], dtype=jnp.int32)
    onehot = (row_ids[:, None] == jnp.arange(DOCS, dtype=jnp.int32)[None, :]).astype(jnp.int32)
    first = jnp.cumsum(length) - length
    offset = positions - jnp.sum(onehot * first[None, :], axis=1)
    limit = jnp.sum(onehot * row_kept[None, :], axis=1)
    used = jnp.minimum(length, row_kept).astype(jnp.float32)
    counted = (offset < limit).astype(jnp.float32)
    return onehot.astype(jnp.float32) * counted[:, None] / jnp.sqrt(used)[None, :]


def shards(
    layer_inputs,
    output_grads,
    query_inputs,
    query_grads,
    input_eigen,
    output_eigen,
    doc_index,
    kept_counts,
):
    pre_in = (query_inputs.astype(jnp.float32) / (input_eigen + damping)[None, None, :]).astype(
        jnp.bfloat16
    )
    pre_out = (query_grads.astype(jnp.float32) / (output_eigen + damping)[None, None, :]).astype(
        jnp.bfloat16
    )
    own_tokens = layer_inputs.shape[0]
    full_in, full_out = (
        lax.all_gather(pre_in, "seq", axis=2, tiled=True),
        lax.all_gather(pre_out, "seq", axis=2, tiled=True),
    )
    width_in = full_in.shape[2]
    factors = jnp.concatenate([full_in, full_out], axis=2)
    piece = lax.all_gather(factors, "dp", axis=0, tiled=True)
    count_queries = piece.shape[0]
    flat = piece.reshape(count_queries * RANK, piece.shape[2])
    in_proj = jnp.einsum(
        "td,kd->tk", layer_inputs, flat[:, :width_in], preferred_element_type=jnp.float32
    )
    out_proj = jnp.einsum(
        "tf,kf->tk", output_grads, flat[:, width_in:], preferred_element_type=jnp.float32
    )
    product = (in_proj * out_proj).reshape(own_tokens, count_queries, RANK)
    scores = jnp.sum(product, axis=2)
    row_kept = kept_counts[0]
    own_ids = doc_index[0]
    onehot = (own_ids[:, None] == jnp.arange(DOCS, dtype=jnp.int32)[None, :]).astype(jnp.float32)
    length = lax.psum(jnp.sum(onehot, axis=0), "seq").astype(jnp.int32)
    offset_first = lax.axis_index("seq") * own_tokens
    weights = doc_weights(own_ids, row_kept, length, offset_first)
    sums = jnp.dot(scores.T, weights, precision=lax.Precision.HIGHEST)
    return lax.psum_scatter(sums, "seq", scatter_dimension=0, tiled=True)


def solution(mesh):
    placed = (
        P(("dp", "seq"), None),
        P(("dp", "seq"), None),
        P("dp", None, "seq"),
        P("dp", None, "seq"),
        P("seq"),
        P("seq"),
        P("dp", "seq"),
        P("dp", None),
    )
    return jax.shard_map(
        shards, mesh=mesh, in_specs=placed, out_specs=P("seq", "dp"), check_vma=False
    )
```

profile of v0, /device:TPU:1, one launch (start us, length us, event | category | flops | bytes accessed | tf_op | source)
XLA Modules:
  0.0 290.9 jit_solution(2930839085340960285)
XLA Ops:
  6.5 0.0 copy-start
  6.5 0.0 all-gather.2.cloned.1.call-start
  6.5 0.9 broadcast_add_fusion
  7.4 0.8 divide_convert_fusion
  8.3 8.8 %all_gather.10 = bf16[1,8,14336]{2,1,0:T(8,128)(2,1)S(1)} all-gather(bf16[1,8,3584]{2,1,0:T(8,128)(2,1)S(1)} %divide_convert_fusion), channel_id=1, replica_groups=mesh['dp'=64,'seq'=4] {'seq'}, dimensions={2}, use_global_device_ids=true | all-gather | bytes 286720 | tf_op jit(solution)/shard_map/all_gather | solution.py:43
  17.0 0.7 broadcast_add_fusion.1
  17.7 0.7 divide_convert_fusion.1
  18.4 5.2 %all_gather.9 = bf16[1,8,4096]{2,1,0:T(8,128)(2,1)S(1)} all-gather(bf16[1,8,1024]{2,1,0:T(8,128)(2,1)S(1)} %divide_convert_fusion.1), channel_id=1, replica_groups=mesh['dp'=64,'seq'=4] {'seq'}, dimensions={2}, use_global_device_ids=true | all-gather | bytes 81920 | tf_op jit(solution)/shard_map/all_gather | solution.py:42
  23.7 0.8 pad_maximum_fusion
  24.4 0.0 all-gather.2.cloned.1.call-update
  24.5 0.0 reduce-scatter.4.cloned.1.call-start
  24.5 0.8 convert_reduce_fusion
  25.3 5.2 %psum.7 = f32[8]{0:T(128)S(1)} all-reduce(f32[8]{0:T(128)S(1)} %convert_reduce_fusion), channel_id=1, replica_groups=mesh['dp'=64,'seq'=4] {'seq'}, use_global_device_ids=true, to_apply=%region_2.0 | all-reduce | flops 8 | bytes 64 | tf_op jit(solution)/shard_map/psum | solution.py:61
  30.5 0.7 convert_bitcast_fusion
  31.2 0.2 reduce-window.9
  31.3 0.8 select_reduce_fusion.1
  32.1 217.8 %all-gather.2.cloned.1.call-done = bf16[64,8,18432]{2,1,0:T(8,128)(2,1)} async-done(((bf16[1,8,18432]{2,1,0:T(8,128)(2,1)}), bf16[64,8,18432]{2,1,0:T(8,128)(2,1)}) %all-gather.2.cloned.1.call-update) | async-done | bytes 18874384 | tf_op jit(solution)/shard_map/all_gather | solution.py:47
  249.9 0.0 copy-done
  249.9 3.5 %fusion.2 = f32[512,256]{1,0:T(8,128)S(1)} fusion(bf16[256,4096]{1,0:T(8,128)(2,1)S(1)} %copy-done, bf16[512,18432]{1,0:T(8,128)(2,1)} %bitcast.22), kind=kOutput, calls=%fused_computation.2 | convolution fusion | flops 1073741824 | bytes 6815744 | tf_op jit(solution)/shard_map/td,kd->tk/dot_general | solution.py:50
  253.4 0.0 copy-start.1
  253.4 11.3 %fusion.10 = f32[256,64]{0,1:T(8,128)S(1)} fusion(f32[512,256]{1,0:T(8,128)S(1)} %fusion.2, bf16[256,14336]{1,0:T(8,128)(2,1)} %param.9, bf16[512,18432]{1,0:T(8,128)(2,1)} %bitcast.23), kind=kOutput, calls=%fused_computation.6 | convolution fusion | flops 3758342144 | bytes 22609920 | tf_op jit(solution)/shard_map/tf,kf->tk/dot_general | solution.py:53
  264.7 0.0 copy-done.1
  264.7 0.9 fusion.13
  265.6 0.0 reduce-scatter.4.cloned.1.call-update
  265.6 17.1 %reduce-scatter.4.cloned.1.call-done = f32[16,8]{1,0:T(8,128)} async-done(((f32[64,8]{1,0:T(8,128)}), f32[16,8]{1,0:T(8,128)}) %reduce-scatter.4.cloned.1.call-update) | async-done | bytes 528
  282.7 1.4 copy.10
  (2 shorter events, 0.0 us)
Async XLA Ops:
  6.5 243.4 %copy-start = (bf16[256,4096]{1,0:T(8,128)(2,1)S(1)}, bf16[256,4096]{1,0:T(8,128)(2,1)}, u32[]{:S(2)}) copy-start(bf16[256,4096]{1,0:T(8,128)(2,1)} %param.8) | copy-start | bytes 6291460
  6.5 243.4 %all-gather.2.cloned.1.call-start = ((), (), s32[]{:S(2)}) async-start(), calls=%async_computation.1 | async-start | bytes 19169280 | tf_op jit(solution)/shard_map/all_gather | solution.py:47
  24.5 258.2 %reduce-scatter.4.cloned.1.call-start = ((), (), s32[]{:S(2)}) async-start(), calls=%async_computation.2 | async-start | bytes 40960
  253.4 11.3 %copy-start.1 = (s32[1,256]{1,0:T(1,128)S(1)}, s32[1,256]{1,0:T(1,128)}, u32[]{:S(2)}) copy-start(s32[1,256]{1,0:T(1,128)} %param.14) | copy-start | bytes 3076
Sparse Core Ops, SparseCore 0:
  24.6 225.2 all-gather.1
  265.7 16.9 reduce-scatter.3
where the time goes:
time: 291 us
  waiting for transfers between devices  235 us (81%)
  blocking collectives  19.2 us (7%)
  matrix products  15.6 us (5%)
  between operations  13.4 us (5%)
  other arithmetic  6.31 us (2%)
    all_gather x1, waiting for transfers between devices, shards(): piece = lax.all_gather(factors, 'dp', axis=0, tiled=True)  218 us
    unnamed x3, waiting for transfers between devices  17.1 us
    dot_general x1, matrix products, shards(): jnp.einsum('tf,kf->tk', output_grads, flat[:, width_in:], preferred_eleme...  11.3 us
    all_gather x1, blocking collectives, shards(): lax.all_gather(pre_out, 'seq', axis=2, tiled=True)  8.77 us
  transfers between devices with their start and end apart: 2, of which 2 were waited for; matrix products, arithmetic and copies ran while one was open for 1% of the time, Pallas kernels for 0%

commit v1 on v0

v1 whole, which is shorter than its diff:
```python
import functools

import jax
import jax.numpy as jnp
from jax import lax
from jax.experimental import pallas as pl
from jax.experimental.pallas import tpu as pltpu
from jax.sharding import Mesh
from jax.sharding import PartitionSpec as P

RANK = 8
DOCS = 8
NY, NZ, NX = 4, 8, 4
AXES = ("y", "z", "xh", "xl", "core")
SIZE = {"y": NY, "z": NZ, "x": NX}
damping = 0.1

ROWS = 256
HALF_IN, HALF_OUT = 512, 1792
CHUNK = HALF_IN + HALF_OUT
NT = (((1,), (1,)), ((), ()))


def device_at(y, z, x, core):
    return ((y * NZ + z) * NX + x) * 2 + core


def shift(value, axis, step0, step1):
    pairs = []
    for y in range(NY):
        for z in range(NZ):
            for x in range(NX):
                for core in range(2):
                    at = {"y": y, "z": z, "x": x}
                    at[axis] = (at[axis] + (step1 if core else step0)) % SIZE[axis]
                    pairs.append((device_at(y, z, x, core), device_at(at["y"], at["z"], at["x"], core)))
    return lax.ppermute(value, AXES, pairs)


def swap_cores(value):
    return lax.ppermute(value, "core", [(0, 1), (1, 0)])


def direct(own, axis):
    return [own, shift(own, axis, 1, -1), shift(own, axis, 2, -2), shift(own, axis, -1, 1)]


def gather_z(own):
    a = shift(own, "z", 1, -1)
    b = shift(own, "z", -1, 1)
    a2 = shift(own, "z", 2, -2)
    b2 = shift(own, "z", -2, 2)
    c = shift(jnp.concatenate([a, a2], axis=0), "z", 2, -2)
    d = shift(b, "z", -2, 2)
    return jnp.concatenate([own, a, a2, c, d, b2, b], axis=0), a


def doc_weights(row_ids, row_kept):
    positions = jnp.arange(row_ids.shape[0], dtype=jnp.int32)
    onehot = (row_ids[None, :] == jnp.arange(DOCS, dtype=jnp.int32)[:, None]).astype(jnp.int32)
    length = jnp.sum(onehot, axis=1)
    first = jnp.cumsum(length) - length
    used = jnp.minimum(length, row_kept).astype(jnp.float32)
    counted = (positions[None, :] - first[:, None] < row_kept[:, None]).astype(jnp.float32)
    return onehot.astype(jnp.float32) * counted / jnp.sqrt(used)[:, None]


def project(odd, where, tokens, first, second, acc_in, acc_out, xs, gs, ws, sems):
    def copies(piece):
        half, quarter = divmod(piece, 2)
        at = (where[3] ^ odd) * 4 + quarter * 2 + half
        of_x = pl.ds(pl.multiple_of(at * HALF_IN, 128), HALF_IN)
        of_g = pl.ds(pl.multiple_of(at * HALF_OUT, 128), HALF_OUT)
        of_w = pl.ds(quarter * CHUNK, CHUNK)
        x_own, x_other, g_own, g_other = tokens
        moves = [
            (x_own.at[:, of_x], xs.at[piece, pl.ds(0, 256)]),
            (x_other.at[:, of_x], xs.at[piece, pl.ds(256, 256)]),
            (g_own.at[:, of_g], gs.at[piece, pl.ds(0, 256)]),
            (g_other.at[:, of_g], gs.at[piece, pl.ds(256, 256)]),
        ]
        if half == 0:
            moves += [(v.at[:, of_w], ws.at[piece, pl.ds(64 * i, 64)]) for i, v in enumerate(first)]
        else:
            moves += [
                (second[y].at[pl.ds(32 * k, 32), of_w], ws.at[piece, pl.ds(128 * k + 32 * y, 32)])
                for k in range(2)
                for y in range(4)
            ]
        return [pltpu.make_async_copy(src, dst, sems.at[piece, i]) for i, (src, dst) in enumerate(moves)]

    for piece in range(4):
        for copy in copies(piece):
            copy.start()
    for piece in range(4):
        for copy in copies(piece):
            copy.wait()
        p = lax.dot_general(xs[piece], ws[piece, :, :HALF_IN], NT, preferred_element_type=jnp.float32)
        q = lax.dot_general(gs[piece], ws[piece, :, HALF_IN:], NT, preferred_element_type=jnp.float32)
        if piece == 0:
            acc_in[...] = p
            acc_out[...] = q
        else:
            acc_in[...] += p
            acc_out[...] += q


def even_kernel(where, *refs):
    project(0, where, refs[:4], refs[4:8], refs[8:12], *refs[12:])


def odd_kernel(where, *refs):
    w_own, w_other, even_in, even_out = refs[12:16]
    outs, (acc_in, acc_out, *scratch) = refs[16:20], refs[20:]
    project(1, where, refs[:4], refs[4:8], refs[8:12], acc_in, acc_out, *scratch)
    y, z, xh, xl, core = (where[i] for i in range(5))
    swapped = xl == core

    def total(even, acc):
        odd = acc[...]
        turned = jnp.concatenate([odd[:, 128:], odd[:, :128]], axis=1)
        return even[...] + jnp.where(swapped, turned, odd)

    prod = total(even_in, acc_in) * total(even_out, acc_out)
    weights = jnp.concatenate([w_own[...], w_other[...]], axis=1)
    sums = jnp.dot(weights, prod, precision=lax.Precision.HIGHEST, preferred_element_type=jnp.float32)
    row = lax.broadcasted_iota(jnp.int32, (16, ROWS), 1)
    slot = lax.broadcasted_iota(jnp.int32, (16, ROWS), 0)
    sign = 2 * core - 1
    row_z = (z + sign * ((row >> 2) & 7)) & 7
    row_y = (y + sign * ((row >> 5) & 3)) & 3
    row_xh = xh ^ (row >> 7)
    row_query = (row_y * 8 + row_z) * 2 + row_xh
    seq = xl * 2 + core
    for away in range(4):
        pick = (row_query == (seq ^ away) * 16 + slot).astype(jnp.float32)
        outs[away][...] = lax.dot_general(
            sums, pick, NT, precision=lax.Precision.HIGHEST, preferred_element_type=jnp.float32
        )


def score(where, tokens, first, second, extra=()):
    last = bool(extra)
    proj = (512, ROWS)
    vmem = pl.BlockSpec(memory_space=pltpu.VMEM)
    shapes = [(DOCS, 16)] * 4 if last else [proj] * 2
    return pl.pallas_call(
        odd_kernel if last else even_kernel,
        in_specs=[pl.BlockSpec(memory_space=pltpu.SMEM)]
        + [pl.BlockSpec(memory_space=pl.ANY)] * 12
        + [vmem] * len(extra),
        out_specs=[vmem] * len(shapes),
        out_shape=[jax.ShapeDtypeStruct(shape, jnp.float32) for shape in shapes],
        scratch_shapes=([pltpu.VMEM(proj, jnp.float32)] * 2 if last else [])
        + [
            pltpu.VMEM((4, 512, HALF_IN), jnp.bfloat16),
            pltpu.VMEM((4, 512, HALF_OUT), jnp.bfloat16),
            pltpu.VMEM((4, ROWS, CHUNK), jnp.bfloat16),
            pltpu.SemaphoreType.DMA((4, 12)),
        ],
        compiler_params=pltpu.CompilerParams(vmem_limit_bytes=60 * 1024 * 1024),
        cost_estimate=pl.CostEstimate(
            flops=2 * 512 * ROWS * 4 * CHUNK, bytes_accessed=2 * 768 * 4 * CHUNK, transcendentals=0
        ),
    )(where, *tokens, *first, *second, *extra)


def shards(
    layer_inputs,
    output_grads,
    query_inputs,
    query_grads,
    input_eigen,
    output_eigen,
    doc_index,
    kept_counts,
):
    y, z, xh, xl, core = (lax.axis_index(a) for a in AXES)
    pre_in = (query_inputs[0].astype(jnp.float32) / (input_eigen + damping)[None, :]).astype(jnp.bfloat16)
    pre_out = (query_grads[0].astype(jnp.float32) / (output_eigen + damping)[None, :]).astype(jnp.bfloat16)
    pre = jnp.concatenate(
        [pre_in[:, :HALF_IN], pre_out[:, :HALF_OUT], pre_in[:, HALF_IN:], pre_out[:, HALF_OUT:]], axis=1
    )
    low, high = pre[:4], pre[4:]
    kept = jnp.where(core == 0, low, high)
    came = swap_cores(jnp.where(core == 0, high, low))
    both = jnp.where(core == 0, jnp.stack([kept, came], axis=1), jnp.stack([came, kept], axis=1))
    own = both.reshape(8, 2 * CHUNK)

    own, output_grads = lax.optimization_barrier((own, output_grads))
    g_other = swap_cores(output_grads)
    slots, first_came = gather_z(own)
    first_came, layer_inputs, own_ids = lax.optimization_barrier((first_came, layer_inputs, doc_index[0]))
    x_other = swap_cores(layer_inputs)
    ids = lax.all_gather(own_ids, ("xl", "core"), axis=0, tiled=True)

    halves = [slots[:, :CHUNK].reshape(32, 2 * CHUNK), slots[:, CHUNK:].reshape(32, 2 * CHUNK)]
    halves, x_other, g_other, ids = lax.optimization_barrier((halves, x_other, g_other, ids))

    first, second = direct(halves[0], "y"), direct(halves[1], "x")

    def go_round(one, two, axis):
        pair = [jnp.concatenate([one, two], axis=0)]
        for _ in range(3):
            pair.append(shift(pair[-1], axis, 1, -1))
        return pair

    even_second = go_round(second[0], second[2], "y")
    near_first = go_round(first[0], first[1], "x")
    far_first = go_round(first[2], first[3], "x")
    odd_second = go_round(second[1], second[3], "y")

    weights = doc_weights(ids, kept_counts[0])
    seq = xl * 2 + core
    w_own = lax.dynamic_slice(weights, (0, seq * 256), (DOCS, 256))
    w_other = lax.dynamic_slice(weights, (0, (seq ^ 1) * 256), (DOCS, 256))

    where = jnp.stack([y, z, xh, xl, core]).astype(jnp.int32)
    tokens = (layer_inputs, x_other, output_grads, g_other)
    even = score(where, tokens, [near_first[0], far_first[0], near_first[2], far_first[2]], even_second)
    pieces = score(
        where,
        tokens,
        [near_first[1], far_first[1], near_first[3], far_first[3]],
        odd_second,
        (w_own, w_other, *even),
    )
    total = pieces[0]
    for away in (1, 2, 3):
        total = total + lax.ppermute(pieces[away], ("xl", "core"), [(i, i ^ away) for i in range(4)])
    return total.T


def solution(mesh):
    fine = Mesh(mesh.devices.reshape(NY, NZ, 2, 2, 2), AXES)
    dp, seq = ("y", "z", "xh"), ("xl", "core")
    placed = (
        P(dp + seq, None),
        P(dp + seq, None),
        P(dp, None, seq),
        P(dp, None, seq),
        P(seq),
        P(seq),
        P(dp, seq),
        P(dp, None),
    )
    return jax.shard_map(shards, mesh=fine, in_specs=placed, out_specs=P(seq, dp), check_vma=False)
```

time: 291 us -> 110 us (0.38)
  waiting for transfers between devices: 235 us -> 31.6 us
  starting transfers between devices: 0.04 us -> 45.2 us
  Pallas kernels: 0 us -> 17.4 us
  matrix products: 15.6 us -> 0 us
  blocking collectives: 19.2 us -> 5.02 us
  between operations: 13.4 us -> 0.3 us
  local copies, waits for them, and re-layouts: 1.37 us -> 5.33 us
    all_gather x1 -> x0, waiting for transfers between devices: 218 us -> none  [shards(): piece = lax.all_gather(factors, 'dp', axis=0, tiled=True)]
    ppermute x0 -> x30, starting transfers between devices: none -> 45.2 us  [the longest x24 38.2 us: shift(): return lax.ppermute(value, AXES, pairs)]
    ppermute x0 -> x30, waiting for transfers between devices: none -> 31.6 us  [the longest x24 29 us: shift(): return lax.ppermute(value, AXES, pairs)]
    pallas_call x0 -> x2, Pallas kernels: none -> 17.4 us  [score(): pl.pallas_call(odd_kernel if last else even_kernel, in_specs=[pl.BlockSpe...]
    unnamed x3 -> x0, waiting for transfers between devices: 17.1 us -> none
    dot_general x2 -> x0, matrix products: 14.8 us -> none  [the longest x1 11.3 us: shards(): jnp.einsum('tf,kf->tk', output_grads, flat[:, width_in:], preferred_eleme...]
    all_gather x2 -> x1, blocking collectives: 14 us -> 5.02 us  [shards(): ids = lax.all_gather(own_ids, ('xl', 'core'), axis=0, tiled=True)]
    psum x1 -> x0, blocking collectives: 5.18 us -> none  [shards(): length = lax.psum(jnp.sum(onehot, axis=0), 'seq').astype(jnp.int32)]
  transfers between devices with their start and end apart: 2 -> 30, of which waited for: 2 -> 14; matrix products, arithmetic and copies ran while one was open for 1% -> 4% of each run, Pallas kernels for 0% -> 7%
where the time goes in v1:
time: 110 us
  starting transfers between devices  45.2 us (41%)
  waiting for transfers between devices  31.6 us (29%)
  Pallas kernels  17.4 us (16%)
  local copies, waits for them, and re-layouts  5.33 us (5%)
  blocking collectives  5.02 us (5%)
  other arithmetic  4.8 us (4%)
    ppermute x24, starting transfers between devices, shift(): return lax.ppermute(value, AXES, pairs)  38.2 us
    ppermute x24, waiting for transfers between devices, shift(): return lax.ppermute(value, AXES, pairs)  29 us
    pallas_call x2, Pallas kernels, score(): pl.pallas_call(odd_kernel if last else even_kernel, in_specs=[pl.BlockSpe...  17.4 us
    all_gather x1, blocking collectives, shards(): ids = lax.all_gather(own_ids, ('xl', 'core'), axis=0, tiled=True)  5.02 us
    ppermute x3, starting transfers between devices, swap_cores(): return lax.ppermute(value, 'core', [(0, 1), (1, 0)])  3.77 us
    ppermute x3, starting transfers between devices, shards(): lax.ppermute(pieces[away], ('xl', 'core'), [(i, i ^ away) for i in range(...  3.27 us
    unnamed x22, local copies, waits for them, and re-layouts  2.26 us
  transfers between devices with their start and end apart: 30, of which 14 were waited for; matrix products, arithmetic and copies ran while one was open for 4% of the time, Pallas kernels for 7%

profile of v1, /device:TPU:1, one launch (start us, length us, event | category | flops | bytes accessed | tf_op | source)
XLA Modules:
  0.0 109.8 jit_solution(8168057157598934757)
XLA Ops:
  0.0 0.7 broadcast_add_fusion
  0.7 0.8 fusion
  1.6 0.7 broadcast_add_fusion.1
  2.3 0.7 fusion.3
  3.1 3.3 %collective-permute-start = (bf16[4,4608]{1,0:T(4,128)(2,1)S(1)}, bf16[4,4608]{1,0:T(4,128)(2,1)S(1)}, u32[]{:S(2)}, u32[]{:S(2)}) collective-permute-start(bf16[4,4608]{1,0:T(4,128)(2,1)S(1)} %get-tuple-element.38), channel_id=1, source_target_pairs={{0,1},{1,0},{2,3},{3,2},{4,5},{5,4},{6,7},{7,6},{8,9},{9,8},{10,11... | collective-permute-start | bytes 110600 | tf_op jit(solution)/shard_map/ppermute | solution.py:41
  6.4 0.9 collective-permute-done
  7.9 3.8 %collective-permute-start.1 = (bf16[8,4608]{1,0:T(8,128)(2,1)S(1)}, bf16[8,4608]{1,0:T(8,128)(2,1)S(1)}, u32[]{:S(2)}, u32[]{:S(2)}) collective-permute-start(bf16[8,4608]{1,0:T(8,128)(2,1)S(1)} %select_n.35), channel_id=1, source_target_pairs={{0,8},{1,57},{2,10},{3,59},{4,12},{5,61},{6,14},{7,63},{8,16},{9,1... | collective-permute-start | bytes 221192 | tf_op jit(solution)/shard_map/ppermute | solution.py:37
  11.7 1.2 %collective-permute-start.2 = (bf16[8,4608]{1,0:T(8,128)(2,1)S(1)}, bf16[8,4608]{1,0:T(8,128)(2,1)S(1)}, u32[]{:S(2)}, u32[]{:S(2)}) collective-permute-start(bf16[8,4608]{1,0:T(8,128)(2,1)S(1)} %select_n.35), channel_id=1, source_target_pairs={{0,16},{1,49},{2,18},{3,51},{4,20},{5,53},{6,22},{7,55},{8,24},{9,... | collective-permute-start | bytes 221192 | tf_op jit(solution)/shard_map/ppermute | solution.py:37
  12.9 0.7 collective-permute-start.4
  13.7 0.5 collective-permute-start.6
  14.2 1.9 %collective-permute-done.2 = bf16[8,4608]{1,0:T(8,128)(2,1)S(1)} collective-permute-done((bf16[8,4608]{1,0:T(8,128)(2,1)S(1)}, bf16[8,4608]{1,0:T(8,128)(2,1)S(1)}, u32[]{:S(2)}, u32[]{:S(2)}) %collective-permute-start.2) | collective-permute-done | bytes 73760 | tf_op jit(solution)/shard_map/ppermute | solution.py:37
  16.2 3.6 %collective-permute-start.3 = (bf16[16,4608]{1,0:T(8,128)(2,1)S(1)}, bf16[16,4608]{1,0:T(8,128)(2,1)S(1)}, u32[]{:S(2)}, u32[]{:S(2)}) collective-permute-start(bf16[16,4608]{1,0:T(8,128)(2,1)S(1)} %pad_maximum_fusion), channel_id=1, source_target_pairs={{0,16},{1,49},{2,18},{3,51},{4,20},{5,53},{6,22},{7,55},{8,24},{9,... | collective-permute-start | bytes 442376 | tf_op jit(solution)/shard_map/ppermute | solution.py:37
  19.8 3.0 %collective-permute-start.5 = (bf16[8,4608]{1,0:T(8,128)(2,1)S(1)}, bf16[8,4608]{1,0:T(8,128)(2,1)S(1)}, u32[]{:S(2)}, u32[]{:S(2)}) collective-permute-start(bf16[8,4608]{1,0:T(8,128)(2,1)S(1)} %collective-permute-done.4), channel_id=1, source_target_pairs={{0,48},{1,17},{2,50},{3,19},{4,52},{5,21},{6,54},{7,23},{8,56},{9,... | collective-permute-start | bytes 221192 | tf_op jit(solution)/shard_map/ppermute | solution.py:37
  22.8 5.0 %all-gather = s32[4,1,256]{2,1,0:T(1,128)S(1)} all-gather(s32[1,1,256]{2,1,0:T(1,128)} %bitcast.27), channel_id=1, replica_groups=mesh['y'=4,'z'=8,'xh'=2,'xl'=2,'core'=2] {'xl','core'}, dimensions={0}, use_global_device_ids=true | all-gather | bytes 5120 | tf_op jit(solution)/shard_map/all_gather | solution.py:195
  27.9 0.8 reshape.54
  28.8 0.8 reshape.55
  29.6 1.2 %constant_dynamic-update-slice_fusion.14 = bf16[64,4608]{1,0:T(8,128)(2,1)S(1)} fusion(bf16[32,4608]{1,0:T(8,128)(2,1)} %reshape.55), kind=kLoop, calls=%fused_computation.25 | loop fusion | bytes 589824
  30.7 2.5 %collective-permute-start.23 = (bf16[32,4608]{1,0:T(8,128)(2,1)}, bf16[32,4608]{1,0:T(8,128)(2,1)S(1)}, u32[]{:S(2)}, u32[]{:S(2)}) collective-permute-start(bf16[32,4608]{1,0:T(8,128)(2,1)} %reshape.55), channel_id=1, source_target_pairs={{0,4},{1,5},{2,6},{3,7},{4,0},{5,1},{6,2},{7,3},{8,12},{9,13},{10,... | collective-permute-start | bytes 884744 | tf_op jit(solution)/shard_map/ppermute | solution.py:37
  33.3 2.9 %collective-permute-start.11 = (bf16[32,4608]{1,0:T(8,128)(2,1)}, bf16[32,4608]{1,0:T(8,128)(2,1)S(1)}, u32[]{:S(2)}, u32[]{:S(2)}) collective-permute-start(bf16[32,4608]{1,0:T(8,128)(2,1)} %reshape.54), channel_id=1, source_target_pairs={{0,128},{1,129},{2,130},{3,131},{4,132},{5,133},{6,134},{7,135},{8... | collective-permute-start | bytes 884744 | tf_op jit(solution)/shard_map/ppermute | solution.py:37
  36.6 2.3 %collective-permute-start.9 = (bf16[32,4608]{1,0:T(8,128)(2,1)}, bf16[32,4608]{1,0:T(8,128)(2,1)S(1)}, u32[]{:S(2)}, u32[]{:S(2)}) collective-permute-start(bf16[32,4608]{1,0:T(8,128)(2,1)} %reshape.54), channel_id=1, source_target_pairs={{0,64},{1,193},{2,66},{3,195},{4,68},{5,197},{6,70},{7,199},{8,72}... | collective-permute-start | bytes 884744 | tf_op jit(solution)/shard_map/ppermute | solution.py:37
  39.1 1.0 constant_dynamic-update-slice_fusion.8
  40.1 0.9 collective-permute-done.23
  41.4 1.7 %collective-permute-done.11 = bf16[32,4608]{1,0:T(8,128)(2,1)S(1)} collective-permute-done((bf16[32,4608]{1,0:T(8,128)(2,1)}, bf16[32,4608]{1,0:T(8,128)(2,1)S(1)}, u32[]{:S(2)}, u32[]{:S(2)}) %collective-permute-start.11) | collective-permute-done | bytes 294944 | tf_op jit(solution)/shard_map/ppermute | solution.py:37
  43.2 2.7 %collective-permute-start.24 = (bf16[64,4608]{1,0:T(8,128)(2,1)S(1)}, bf16[64,4608]{1,0:T(8,128)(2,1)}, u32[]{:S(2)}, u32[]{:S(2)}) collective-permute-start(bf16[64,4608]{1,0:T(8,128)(2,1)S(1)} %constant_dynamic-update-slice_fusion.13.refs_8_), channel_id=1, source_target_pairs={{0,64},{1,193},{2,66},{3,195},{4,68},{5,197},{6,70},{7,199},{8,72}... | collective-permute-start | bytes 1769480 | tf_op jit(solution)/shard_map/ppermute | solution.py:37
  45.9 4.3 %collective-permute-done.12 = bf16[32,4608]{1,0:T(8,128)(2,1)S(1)} collective-permute-done((bf16[32,4608]{1,0:T(8,128)(2,1)}, bf16[32,4608]{1,0:T(8,128)(2,1)S(1)}, u32[]{:S(2)}, u32[]{:S(2)}) %collective-permute-start.12) | collective-permute-done | bytes 294944 | tf_op jit(solution)/shard_map/ppermute | solution.py:37
  50.3 0.5 collective-permute-start.13
  50.9 1.1 %collective-permute-start.20 = (bf16[64,4608]{1,0:T(8,128)(2,1)S(1)}, bf16[64,4608]{1,0:T(8,128)(2,1)}, u32[]{:S(2)}, u32[]{:S(2)}) collective-permute-start(bf16[64,4608]{1,0:T(8,128)(2,1)S(1)} %constant_dynamic-update-slice_fusion.11.refs_8_), channel_id=1, source_target_pairs={{0,64},{1,193},{2,66},{3,195},{4,68},{5,197},{6,70},{7,199},{8,72}... | collective-permute-start | bytes 1769480 | tf_op jit(solution)/shard_map/ppermute | solution.py:37
  52.1 5.0 %collective-permute-done.24.refs_9_ = bf16[64,4608]{1,0:T(8,128)(2,1)} collective-permute-done((bf16[64,4608]{1,0:T(8,128)(2,1)S(1)}, bf16[64,4608]{1,0:T(8,128)(2,1)}, u32[]{:S(2)}, u32[]{:S(2)}) %collective-permute-start.24) | collective-permute-done | bytes 589856 | tf_op jit(solution)/shard_map/ppermute | solution.py:37
  57.2 2.3 %collective-permute-start.25 = (bf16[64,4608]{1,0:T(8,128)(2,1)}, bf16[64,4608]{1,0:T(8,128)(2,1)}, u32[]{:S(2)}, u32[]{:S(2)}) collective-permute-start(bf16[64,4608]{1,0:T(8,128)(2,1)} %collective-permute-done.24.refs_9_), channel_id=1, source_target_pairs={{0,64},{1,193},{2,66},{3,195},{4,68},{5,197},{6,70},{7,199},{8,72}... | collective-permute-start | bytes 1769480 | tf_op jit(solution)/shard_map/ppermute | solution.py:37
  59.5 4.0 %collective-permute-done.20.refs_9_ = bf16[64,4608]{1,0:T(8,128)(2,1)} collective-permute-done((bf16[64,4608]{1,0:T(8,128)(2,1)S(1)}, bf16[64,4608]{1,0:T(8,128)(2,1)}, u32[]{:S(2)}, u32[]{:S(2)}) %collective-permute-start.20) | collective-permute-done | bytes 589856 | tf_op jit(solution)/shard_map/ppermute | solution.py:37
  63.5 2.3 %collective-permute-start.21 = (bf16[64,4608]{1,0:T(8,128)(2,1)}, bf16[64,4608]{1,0:T(8,128)(2,1)}, u32[]{:S(2)}, u32[]{:S(2)}) collective-permute-start(bf16[64,4608]{1,0:T(8,128)(2,1)} %collective-permute-done.20.refs_9_), channel_id=1, source_target_pairs={{0,64},{1,193},{2,66},{3,195},{4,68},{5,197},{6,70},{7,199},{8,72}... | collective-permute-start | bytes 1769480 | tf_op jit(solution)/shard_map/ppermute | solution.py:37
  66.0 1.5 %collective-permute-start.14 = (bf16[64,4608]{1,0:T(8,128)(2,1)}, bf16[64,4608]{1,0:T(8,128)(2,1)}, u32[]{:S(2)}, u32[]{:S(2)}) collective-permute-start(bf16[64,4608]{1,0:T(8,128)(2,1)} %collective-permute-done.10.refs_4_), channel_id=1, source_target_pairs={{0,2},{1,7},{2,4},{3,1},{4,6},{5,3},{6,0},{7,5},{8,10},{9,15},{10,... | collective-permute-start | bytes 1769480 | tf_op jit(solution)/shard_map/ppermute | solution.py:37
  67.5 0.6 stack.37.where
  68.4 1.4 %collective-permute-done.25.refs_10_ = bf16[64,4608]{1,0:T(8,128)(2,1)} collective-permute-done((bf16[64,4608]{1,0:T(8,128)(2,1)}, bf16[64,4608]{1,0:T(8,128)(2,1)}, u32[]{:S(2)}, u32[]{:S(2)}) %collective-permute-start.25) | collective-permute-done | bytes 589856 | tf_op jit(solution)/shard_map/ppermute | solution.py:37
  69.8 2.3 %collective-permute-start.26 = (bf16[64,4608]{1,0:T(8,128)(2,1)}, bf16[64,4608]{1,0:T(8,128)(2,1)}, u32[]{:S(2)}, u32[]{:S(2)}) collective-permute-start(bf16[64,4608]{1,0:T(8,128)(2,1)} %collective-permute-done.25.refs_10_), channel_id=1, source_target_pairs={{0,64},{1,193},{2,66},{3,195},{4,68},{5,197},{6,70},{7,199},{8,72}... | collective-permute-start | bytes 1769480 | tf_op jit(solution)/shard_map/ppermute | solution.py:37
  72.2 4.0 %collective-permute-done.21.refs_10_ = bf16[64,4608]{1,0:T(8,128)(2,1)} collective-permute-done((bf16[64,4608]{1,0:T(8,128)(2,1)}, bf16[64,4608]{1,0:T(8,128)(2,1)}, u32[]{:S(2)}, u32[]{:S(2)}) %collective-permute-start.21) | collective-permute-done | bytes 589856 | tf_op jit(solution)/shard_map/ppermute | solution.py:37
  76.1 2.3 %collective-permute-start.22 = (bf16[64,4608]{1,0:T(8,128)(2,1)}, bf16[64,4608]{1,0:T(8,128)(2,1)}, u32[]{:S(2)}, u32[]{:S(2)}) collective-permute-start(bf16[64,4608]{1,0:T(8,128)(2,1)} %collective-permute-done.21.refs_10_), channel_id=1, source_target_pairs={{0,64},{1,193},{2,66},{3,195},{4,68},{5,197},{6,70},{7,199},{8,72}... | collective-permute-start | bytes 1769480 | tf_op jit(solution)/shard_map/ppermute | solution.py:37
  78.5 3.0 %collective-permute-done.14.refs_6_ = bf16[64,4608]{1,0:T(8,128)(2,1)} collective-permute-done((bf16[64,4608]{1,0:T(8,128)(2,1)}, bf16[64,4608]{1,0:T(8,128)(2,1)}, u32[]{:S(2)}, u32[]{:S(2)}) %collective-permute-start.14) | collective-permute-done | bytes 589856 | tf_op jit(solution)/shard_map/ppermute | solution.py:37
  81.5 1.2 %collective-permute-start.15 = (bf16[64,4608]{1,0:T(8,128)(2,1)}, bf16[64,4608]{1,0:T(8,128)(2,1)}, u32[]{:S(2)}, u32[]{:S(2)}) collective-permute-start(bf16[64,4608]{1,0:T(8,128)(2,1)} %collective-permute-done.14.refs_6_), channel_id=1, source_target_pairs={{0,2},{1,7},{2,4},{3,1},{4,6},{5,3},{6,0},{7,5},{8,10},{9,15},{10,... | collective-permute-start | bytes 1769480 | tf_op jit(solution)/shard_map/ppermute | solution.py:37
  82.8 0.6 constant_dynamic-slice_fusion
  83.4 8.2 %shard_map.82 = (f32[512,256]{1,0:T(8,128)}, f32[512,256]{1,0:T(8,128)}) custom-call(s32[5]{0:T(128)} %stack.37.where, bf16[256,4096]{1,0:T(8,128)(2,1)} %refs_0_.1, bf16[256,4096]{1,0:T(8,128)(2,1)} %copy-done, bf16[256,14336]{1,0:T(8,128)(2,1)} %refs_2_.1, bf16[256,14336]{1,0:T(8,128)(2,1)} %collective-permute-done.8.refs_3_, bf16[64,4608]{1,0:T(8,128)(2,1)} %copy-done.1, ...), custom_call_target="tpu_custom_call" | custom-call | flops 2415919104 | bytes 14155776 | tf_op jit(solution)/shard_map/pallas_call | solution.py:147
  91.6 2.5 %collective-permute-done.15.refs_6_ = bf16[64,4608]{1,0:T(8,128)(2,1)} collective-permute-done((bf16[64,4608]{1,0:T(8,128)(2,1)}, bf16[64,4608]{1,0:T(8,128)(2,1)}, u32[]{:S(2)}, u32[]{:S(2)}) %collective-permute-start.15) | collective-permute-done | bytes 589856 | tf_op jit(solution)/shard_map/ppermute | solution.py:37
  94.1 9.3 %shard_map.83 = (f32[8,16]{1,0:T(8,128)}, f32[8,16]{1,0:T(8,128)}, f32[8,16]{1,0:T(8,128)}, f32[8,16]{1,0:T(8,128)}) custom-call(s32[5]{0:T(128)} %stack.37.where, bf16[256,4096]{1,0:T(8,128)(2,1)} %refs_0_.1, bf16[256,4096]{1,0:T(8,128)(2,1)} %copy-done, bf16[256,14336]{1,0:T(8,128)(2,1)} %refs_2_.1, bf16[256,14336]{1,0:T(8,128)(2,1)} %collective-permute-done.8.refs_3_, ...), custom_call_target="tpu_custom_call" | custom-call | flops 2415919104 | bytes 14155776 | tf_op jit(solution)/shard_map/pallas_call | solution.py:147
  103.4 1.5 %collective-permute-start.27 = (f32[8,16]{1,0:T(8,128)}, f32[8,16]{1,0:T(8,128)S(1)}, u32[]{:S(2)}, u32[]{:S(2)}) collective-permute-start(f32[8,16]{1,0:T(8,128)} %get-tuple-element.32), channel_id=1, source_target_pairs={{0,1},{1,0},{2,3},{3,2},{4,5},{5,4},{6,7},{7,6},{8,9},{9,8},{10,11... | collective-permute-start | bytes 1544 | tf_op jit(solution)/shard_map/ppermute | solution.py:230
  105.0 1.7 %collective-permute-start.29 = (f32[8,16]{1,0:T(8,128)}, f32[8,16]{1,0:T(8,128)S(1)}, u32[]{:S(2)}, u32[]{:S(2)}) collective-permute-start(f32[8,16]{1,0:T(8,128)} %get-tuple-element.34), channel_id=1, source_target_pairs={{0,3},{1,2},{2,1},{3,0},{4,7},{5,6},{6,5},{7,4},{8,11},{9,10},{10,... | collective-permute-start | bytes 1544 | tf_op jit(solution)/shard_map/ppermute | solution.py:230
  106.7 1.0 collective-permute-done.28
  107.6 0.8 collective-permute-done.29
  108.5 1.3 %add_bitcast_fusion = f32[16,8]{0,1:T(8,128)} fusion(f32[8,16]{1,0:T(8,128)S(1)} %collective-permute-done.29, f32[8,16]{1,0:T(8,128)S(1)} %collective-permute-done.28, f32[8,16]{1,0:T(8,128)} %get-tuple-element.31, f32[8,16]{1,0:T(8,128)S(1)} %collective-permute-done.27), kind=kLoop, calls=%fused_computation.31 | loop fusion | flops 384 | bytes 2560 | tf_op jit(solution)/shard_map/transpose | solution.py:231
  (65 shorter events, 2.7 us)
Async XLA Ops:
  0.0 82.7 %copy-start.5 = (s32[1,8]{1,0:T(1,128)S(1)}, s32[1,8]{1,0:T(1,128)}, u32[]{:S(2)}) copy-start(s32[1,8]{1,0:T(1,128)} %param.15) | copy-start | bytes 100
  3.1 4.2 %collective-permute-start = (bf16[4,4608]{1,0:T(4,128)(2,1)S(1)}, bf16[4,4608]{1,0:T(4,128)(2,1)S(1)}, u32[]{:S(2)}, u32[]{:S(2)}) collective-permute-start(bf16[4,4608]{1,0:T(4,128)(2,1)S(1)} %get-tuple-element.38), channel_id=1, source_target_pairs={{0,1},{1,0},{2,3},{3,2},{4,5},{5,4},{6,7},{7,6},{8,9},{9,8},{10,11... | collective-permute-start | bytes 110600 | tf_op jit(solution)/shard_map/ppermute | solution.py:41
  7.5 22.1 %collective-permute-start.8 = (bf16[256,14336]{1,0:T(8,128)(2,1)}, bf16[256,14336]{1,0:T(8,128)(2,1)}, u32[]{:S(2)}, u32[]{:S(2)}) collective-permute-start(bf16[256,14336]{1,0:T(8,128)(2,1)} %refs_2_.1), channel_id=1, source_target_pairs={{0,1},{1,0},{2,3},{3,2},{4,5},{5,4},{6,7},{7,6},{8,9},{9,8},{10,11... | collective-permute-start | bytes 22020104 | tf_op jit(solution)/shard_map/ppermute | solution.py:41
  7.9 6.3 %collective-permute-start.1 = (bf16[8,4608]{1,0:T(8,128)(2,1)S(1)}, bf16[8,4608]{1,0:T(8,128)(2,1)S(1)}, u32[]{:S(2)}, u32[]{:S(2)}) collective-permute-start(bf16[8,4608]{1,0:T(8,128)(2,1)S(1)} %select_n.35), channel_id=1, source_target_pairs={{0,8},{1,57},{2,10},{3,59},{4,12},{5,61},{6,14},{7,63},{8,16},{9,1... | collective-permute-start | bytes 221192 | tf_op jit(solution)/shard_map/ppermute | solution.py:37
  11.7 4.4 %collective-permute-start.2 = (bf16[8,4608]{1,0:T(8,128)(2,1)S(1)}, bf16[8,4608]{1,0:T(8,128)(2,1)S(1)}, u32[]{:S(2)}, u32[]{:S(2)}) collective-permute-start(bf16[8,4608]{1,0:T(8,128)(2,1)S(1)} %select_n.35), channel_id=1, source_target_pairs={{0,16},{1,49},{2,18},{3,51},{4,20},{5,53},{6,22},{7,55},{8,24},{9,... | collective-permute-start | bytes 221192 | tf_op jit(solution)/shard_map/ppermute | solution.py:37
  12.9 6.9 %collective-permute-start.4 = (bf16[8,4608]{1,0:T(8,128)(2,1)S(1)}, bf16[8,4608]{1,0:T(8,128)(2,1)S(1)}, u32[]{:S(2)}, u32[]{:S(2)}) collective-permute-start(bf16[8,4608]{1,0:T(8,128)(2,1)S(1)} %select_n.35), channel_id=1, source_target_pairs={{0,56},{1,9},{2,58},{3,11},{4,60},{5,13},{6,62},{7,15},{8,0},{9,17... | collective-permute-start | bytes 221192 | tf_op jit(solution)/shard_map/ppermute | solution.py:37
  13.7 14.2 %collective-permute-start.6 = (bf16[8,4608]{1,0:T(8,128)(2,1)S(1)}, bf16[8,4608]{1,0:T(8,128)(2,1)S(1)}, u32[]{:S(2)}, u32[]{:S(2)}) collective-permute-start(bf16[8,4608]{1,0:T(8,128)(2,1)S(1)} %select_n.35), channel_id=1, source_target_pairs={{0,48},{1,17},{2,50},{3,19},{4,52},{5,21},{6,54},{7,23},{8,56},{9,... | collective-permute-start | bytes 221192 | tf_op jit(solution)/shard_map/ppermute | solution.py:37
  16.2 11.7 %collective-permute-start.3 = (bf16[16,4608]{1,0:T(8,128)(2,1)S(1)}, bf16[16,4608]{1,0:T(8,128)(2,1)S(1)}, u32[]{:S(2)}, u32[]{:S(2)}) collective-permute-start(bf16[16,4608]{1,0:T(8,128)(2,1)S(1)} %pad_maximum_fusion), channel_id=1, source_target_pairs={{0,16},{1,49},{2,18},{3,51},{4,20},{5,53},{6,22},{7,55},{8,24},{9,... | collective-permute-start | bytes 442376 | tf_op jit(solution)/shard_map/ppermute | solution.py:37
  19.8 9.8 %collective-permute-start.7 = (bf16[256,4096]{1,0:T(8,128)(2,1)}, bf16[256,4096]{1,0:T(8,128)(2,1)S(1)}, u32[]{:S(2)}, u32[]{:S(2)}) collective-permute-start(bf16[256,4096]{1,0:T(8,128)(2,1)} %refs_0_.1), channel_id=1, source_target_pairs={{0,1},{1,0},{2,3},{3,2},{4,5},{5,4},{6,7},{7,6},{8,9},{9,8},{10,11... | collective-permute-start | bytes 6291464 | tf_op jit(solution)/shard_map/ppermute | solution.py:41
  19.8 8.0 %collective-permute-start.5 = (bf16[8,4608]{1,0:T(8,128)(2,1)S(1)}, bf16[8,4608]{1,0:T(8,128)(2,1)S(1)}, u32[]{:S(2)}, u32[]{:S(2)}) collective-permute-start(bf16[8,4608]{1,0:T(8,128)(2,1)S(1)} %collective-permute-done.4), channel_id=1, source_target_pairs={{0,48},{1,17},{2,50},{3,19},{4,52},{5,21},{6,54},{7,23},{8,56},{9,... | collective-permute-start | bytes 221192 | tf_op jit(solution)/shard_map/ppermute | solution.py:37
  29.6 53.8 %copy-start = (bf16[256,4096]{1,0:T(8,128)(2,1)}, bf16[256,4096]{1,0:T(8,128)(2,1)S(1)}, u32[]{:S(2)}) copy-start(bf16[256,4096]{1,0:T(8,128)(2,1)S(1)} %collective-permute-done.7.refs_1_) | copy-start | bytes 6291460
  30.7 10.2 %collective-permute-start.23 = (bf16[32,4608]{1,0:T(8,128)(2,1)}, bf16[32,4608]{1,0:T(8,128)(2,1)S(1)}, u32[]{:S(2)}, u32[]{:S(2)}) collective-permute-start(bf16[32,4608]{1,0:T(8,128)(2,1)} %reshape.55), channel_id=1, source_target_pairs={{0,4},{1,5},{2,6},{3,7},{4,0},{5,1},{6,2},{7,3},{8,12},{9,13},{10,... | collective-permute-start | bytes 884744 | tf_op jit(solution)/shard_map/ppermute | solution.py:37
  33.3 9.9 %collective-permute-start.11 = (bf16[32,4608]{1,0:T(8,128)(2,1)}, bf16[32,4608]{1,0:T(8,128)(2,1)S(1)}, u32[]{:S(2)}, u32[]{:S(2)}) collective-permute-start(bf16[32,4608]{1,0:T(8,128)(2,1)} %reshape.54), channel_id=1, source_target_pairs={{0,128},{1,129},{2,130},{3,131},{4,132},{5,133},{6,134},{7,135},{8... | collective-permute-start | bytes 884744 | tf_op jit(solution)/shard_map/ppermute | solution.py:37
  36.2 14.1 %collective-permute-start.12 = (bf16[32,4608]{1,0:T(8,128)(2,1)}, bf16[32,4608]{1,0:T(8,128)(2,1)S(1)}, u32[]{:S(2)}, u32[]{:S(2)}) collective-permute-start(bf16[32,4608]{1,0:T(8,128)(2,1)} %reshape.54), channel_id=1, source_target_pairs={{0,192},{1,65},{2,194},{3,67},{4,196},{5,69},{6,198},{7,71},{8,200... | collective-permute-start | bytes 884744 | tf_op jit(solution)/shard_map/ppermute | solution.py:37
  36.6 15.4 %collective-permute-start.9 = (bf16[32,4608]{1,0:T(8,128)(2,1)}, bf16[32,4608]{1,0:T(8,128)(2,1)S(1)}, u32[]{:S(2)}, u32[]{:S(2)}) collective-permute-start(bf16[32,4608]{1,0:T(8,128)(2,1)} %reshape.54), channel_id=1, source_target_pairs={{0,64},{1,193},{2,66},{3,195},{4,68},{5,197},{6,70},{7,199},{8,72}... | collective-permute-start | bytes 884744 | tf_op jit(solution)/shard_map/ppermute | solution.py:37
  38.9 11.9 %collective-permute-start.18 = (bf16[32,4608]{1,0:T(8,128)(2,1)}, bf16[32,4608]{1,0:T(8,128)(2,1)S(1)}, u32[]{:S(2)}, u32[]{:S(2)}) collective-permute-start(bf16[32,4608]{1,0:T(8,128)(2,1)} %reshape.55), channel_id=1, source_target_pairs={{0,2},{1,7},{2,4},{3,1},{4,6},{5,3},{6,0},{7,5},{8,10},{9,15},{10,... | collective-permute-start | bytes 884744 | tf_op jit(solution)/shard_map/ppermute | solution.py:37
  41.0 9.8 %collective-permute-start.19 = (bf16[32,4608]{1,0:T(8,128)(2,1)}, bf16[32,4608]{1,0:T(8,128)(2,1)S(1)}, u32[]{:S(2)}, u32[]{:S(2)}) collective-permute-start(bf16[32,4608]{1,0:T(8,128)(2,1)} %reshape.55), channel_id=1, source_target_pairs={{0,6},{1,3},{2,0},{3,5},{4,2},{5,7},{6,4},{7,1},{8,14},{9,11},{10,... | collective-permute-start | bytes 884744 | tf_op jit(solution)/shard_map/ppermute | solution.py:37
  41.4 42.0 %copy-start.2 = (bf16[64,4608]{1,0:T(8,128)(2,1)}, bf16[64,4608]{1,0:T(8,128)(2,1)S(1)}, u32[]{:S(2)}) copy-start(bf16[64,4608]{1,0:T(8,128)(2,1)S(1)} %constant_dynamic-update-slice_fusion.13.refs_8_) | copy-start | bytes 1769476
  43.2 14.0 %collective-permute-start.24 = (bf16[64,4608]{1,0:T(8,128)(2,1)S(1)}, bf16[64,4608]{1,0:T(8,128)(2,1)}, u32[]{:S(2)}, u32[]{:S(2)}) collective-permute-start(bf16[64,4608]{1,0:T(8,128)(2,1)S(1)} %constant_dynamic-update-slice_fusion.13.refs_8_), channel_id=1, source_target_pairs={{0,64},{1,193},{2,66},{3,195},{4,68},{5,197},{6,70},{7,199},{8,72}... | collective-permute-start | bytes 1769480 | tf_op jit(solution)/shard_map/ppermute | solution.py:37
  50.3 15.7 %copy-start.4 = (bf16[64,4608]{1,0:T(8,128)(2,1)}, bf16[64,4608]{1,0:T(8,128)(2,1)S(1)}, u32[]{:S(2)}) copy-start(bf16[64,4608]{1,0:T(8,128)(2,1)S(1)} %constant_dynamic-update-slice_fusion.9.refs_5_) | copy-start | bytes 1769476
  50.3 15.5 %collective-permute-start.13 = (bf16[64,4608]{1,0:T(8,128)(2,1)S(1)}, bf16[64,4608]{1,0:T(8,128)(2,1)}, u32[]{:S(2)}, u32[]{:S(2)}) collective-permute-start(bf16[64,4608]{1,0:T(8,128)(2,1)S(1)} %constant_dynamic-update-slice_fusion.9.refs_5_), channel_id=1, source_target_pairs={{0,2},{1,7},{2,4},{3,1},{4,6},{5,3},{6,0},{7,5},{8,10},{9,15},{10,... | collective-permute-start | bytes 1769480 | tf_op jit(solution)/shard_map/ppermute | solution.py:37
  50.9 15.1 %copy-start.3 = (bf16[64,4608]{1,0:T(8,128)(2,1)}, bf16[64,4608]{1,0:T(8,128)(2,1)S(1)}, u32[]{:S(2)}) copy-start(bf16[64,4608]{1,0:T(8,128)(2,1)S(1)} %constant_dynamic-update-slice_fusion.11.refs_8_) | copy-start | bytes 1769476
  50.9 12.6 %collective-permute-start.20 = (bf16[64,4608]{1,0:T(8,128)(2,1)S(1)}, bf16[64,4608]{1,0:T(8,128)(2,1)}, u32[]{:S(2)}, u32[]{:S(2)}) collective-permute-start(bf16[64,4608]{1,0:T(8,128)(2,1)S(1)} %constant_dynamic-update-slice_fusion.11.refs_8_), channel_id=1, source_target_pairs={{0,64},{1,193},{2,66},{3,195},{4,68},{5,197},{6,70},{7,199},{8,72}... | collective-permute-start | bytes 1769480 | tf_op jit(solution)/shard_map/ppermute | solution.py:37
  52.0 31.4 %copy-start.1 = (bf16[64,4608]{1,0:T(8,128)(2,1)}, bf16[64,4608]{1,0:T(8,128)(2,1)S(1)}, u32[]{:S(2)}) copy-start(bf16[64,4608]{1,0:T(8,128)(2,1)S(1)} %constant_dynamic-update-slice_fusion.7.refs_4_) | copy-start | bytes 1769476
  52.0 14.0 %collective-permute-start.10 = (bf16[64,4608]{1,0:T(8,128)(2,1)S(1)}, bf16[64,4608]{1,0:T(8,128)(2,1)}, u32[]{:S(2)}, u32[]{:S(2)}) collective-permute-start(bf16[64,4608]{1,0:T(8,128)(2,1)S(1)} %constant_dynamic-update-slice_fusion.7.refs_4_), channel_id=1, source_target_pairs={{0,2},{1,7},{2,4},{3,1},{4,6},{5,3},{6,0},{7,5},{8,10},{9,15},{10,... | collective-permute-start | bytes 1769480 | tf_op jit(solution)/shard_map/ppermute | solution.py:37
  57.2 12.6 %collective-permute-start.25 = (bf16[64,4608]{1,0:T(8,128)(2,1)}, bf16[64,4608]{1,0:T(8,128)(2,1)}, u32[]{:S(2)}, u32[]{:S(2)}) collective-permute-start(bf16[64,4608]{1,0:T(8,128)(2,1)} %collective-permute-done.24.refs_9_), channel_id=1, source_target_pairs={{0,64},{1,193},{2,66},{3,195},{4,68},{5,197},{6,70},{7,199},{8,72}... | collective-permute-start | bytes 1769480 | tf_op jit(solution)/shard_map/ppermute | solution.py:37
  63.5 12.6 %collective-permute-start.21 = (bf16[64,4608]{1,0:T(8,128)(2,1)}, bf16[64,4608]{1,0:T(8,128)(2,1)}, u32[]{:S(2)}, u32[]{:S(2)}) collective-permute-start(bf16[64,4608]{1,0:T(8,128)(2,1)} %collective-permute-done.20.refs_9_), channel_id=1, source_target_pairs={{0,64},{1,193},{2,66},{3,195},{4,68},{5,197},{6,70},{7,199},{8,72}... | collective-permute-start | bytes 1769480 | tf_op jit(solution)/shard_map/ppermute | solution.py:37
  65.8 12.6 %collective-permute-start.16 = (bf16[64,4608]{1,0:T(8,128)(2,1)}, bf16[64,4608]{1,0:T(8,128)(2,1)}, u32[]{:S(2)}, u32[]{:S(2)}) collective-permute-start(bf16[64,4608]{1,0:T(8,128)(2,1)} %collective-permute-done.13.refs_5_), channel_id=1, source_target_pairs={{0,2},{1,7},{2,4},{3,1},{4,6},{5,3},{6,0},{7,5},{8,10},{9,15},{10,... | collective-permute-start | bytes 1769480 | tf_op jit(solution)/shard_map/ppermute | solution.py:37
  66.0 15.5 %collective-permute-start.14 = (bf16[64,4608]{1,0:T(8,128)(2,1)}, bf16[64,4608]{1,0:T(8,128)(2,1)}, u32[]{:S(2)}, u32[]{:S(2)}) collective-permute-start(bf16[64,4608]{1,0:T(8,128)(2,1)} %collective-permute-done.10.refs_4_), channel_id=1, source_target_pairs={{0,2},{1,7},{2,4},{3,1},{4,6},{5,3},{6,0},{7,5},{8,10},{9,15},{10,... | collective-permute-start | bytes 1769480 | tf_op jit(solution)/shard_map/ppermute | solution.py:37
  69.8 13.6 %collective-permute-start.26 = (bf16[64,4608]{1,0:T(8,128)(2,1)}, bf16[64,4608]{1,0:T(8,128)(2,1)}, u32[]{:S(2)}, u32[]{:S(2)}) collective-permute-start(bf16[64,4608]{1,0:T(8,128)(2,1)} %collective-permute-done.25.refs_10_), channel_id=1, source_target_pairs={{0,64},{1,193},{2,66},{3,195},{4,68},{5,197},{6,70},{7,199},{8,72}... | collective-permute-start | bytes 1769480 | tf_op jit(solution)/shard_map/ppermute | solution.py:37
  76.1 15.5 %collective-permute-start.22 = (bf16[64,4608]{1,0:T(8,128)(2,1)}, bf16[64,4608]{1,0:T(8,128)(2,1)}, u32[]{:S(2)}, u32[]{:S(2)}) collective-permute-start(bf16[64,4608]{1,0:T(8,128)(2,1)} %collective-permute-done.21.refs_10_), channel_id=1, source_target_pairs={{0,64},{1,193},{2,66},{3,195},{4,68},{5,197},{6,70},{7,199},{8,72}... | collective-permute-start | bytes 1769480 | tf_op jit(solution)/shard_map/ppermute | solution.py:37
  78.5 13.2 %collective-permute-start.17 = (bf16[64,4608]{1,0:T(8,128)(2,1)}, bf16[64,4608]{1,0:T(8,128)(2,1)}, u32[]{:S(2)}, u32[]{:S(2)}) collective-permute-start(bf16[64,4608]{1,0:T(8,128)(2,1)} %collective-permute-done.16.refs_7_), channel_id=1, source_target_pairs={{0,2},{1,7},{2,4},{3,1},{4,6},{5,3},{6,0},{7,5},{8,10},{9,15},{10,... | collective-permute-start | bytes 1769480 | tf_op jit(solution)/shard_map/ppermute | solution.py:37
  81.5 12.6 %collective-permute-start.15 = (bf16[64,4608]{1,0:T(8,128)(2,1)}, bf16[64,4608]{1,0:T(8,128)(2,1)}, u32[]{:S(2)}, u32[]{:S(2)}) collective-permute-start(bf16[64,4608]{1,0:T(8,128)(2,1)} %collective-permute-done.14.refs_6_), channel_id=1, source_target_pairs={{0,2},{1,7},{2,4},{3,1},{4,6},{5,3},{6,0},{7,5},{8,10},{9,15},{10,... | collective-permute-start | bytes 1769480 | tf_op jit(solution)/shard_map/ppermute | solution.py:37
  103.4 3.3 %collective-permute-start.27 = (f32[8,16]{1,0:T(8,128)}, f32[8,16]{1,0:T(8,128)S(1)}, u32[]{:S(2)}, u32[]{:S(2)}) collective-permute-start(f32[8,16]{1,0:T(8,128)} %get-tuple-element.32), channel_id=1, source_target_pairs={{0,1},{1,0},{2,3},{3,2},{4,5},{5,4},{6,7},{7,6},{8,9},{9,8},{10,11... | collective-permute-start | bytes 1544 | tf_op jit(solution)/shard_map/ppermute | solution.py:230
  105.0 2.7 %collective-permute-start.28 = (f32[8,16]{1,0:T(8,128)}, f32[8,16]{1,0:T(8,128)S(1)}, u32[]{:S(2)}, u32[]{:S(2)}) collective-permute-start(f32[8,16]{1,0:T(8,128)} %get-tuple-element.33), channel_id=1, source_target_pairs={{0,2},{1,3},{2,0},{3,1},{4,6},{5,7},{6,4},{7,5},{8,10},{9,11},{10,... | collective-permute-start | bytes 1544 | tf_op jit(solution)/shard_map/ppermute | solution.py:230
  105.0 3.5 %collective-permute-start.29 = (f32[8,16]{1,0:T(8,128)}, f32[8,16]{1,0:T(8,128)S(1)}, u32[]{:S(2)}, u32[]{:S(2)}) collective-permute-start(f32[8,16]{1,0:T(8,128)} %get-tuple-element.34), channel_id=1, source_target_pairs={{0,3},{1,2},{2,1},{3,0},{4,7},{5,6},{6,5},{7,4},{8,11},{9,10},{10,... | collective-permute-start | bytes 1544 | tf_op jit(solution)/shard_map/ppermute | solution.py:230

commit v2 on v1

--- a/solution.py
+++ b/solution.py
@@ -19,6 +19,7 @@
 HALF_IN, HALF_OUT = 512, 1792
 CHUNK = HALF_IN + HALF_OUT
 NT = (((1,), (1,)), ((), ()))
+LIMIT = 32 * 1024 * 1024
 
 
 def device_at(y, z, x, core):
@@ -158,7 +159,7 @@
             pltpu.VMEM((4, ROWS, CHUNK), jnp.bfloat16),
             pltpu.SemaphoreType.DMA((4, 12)),
         ],
-        compiler_params=pltpu.CompilerParams(vmem_limit_bytes=60 * 1024 * 1024),
+        compiler_params=pltpu.CompilerParams(vmem_limit_bytes=LIMIT),
         cost_estimate=pl.CostEstimate(
             flops=2 * 512 * ROWS * 4 * CHUNK, bytes_accessed=2 * 768 * 4 * CHUNK, transcendentals=0
         ),
@@ -184,18 +185,20 @@
     low, high = pre[:4], pre[4:]
     kept = jnp.where(core == 0, low, high)
     came = swap_cores(jnp.where(core == 0, high, low))
+    ids_came = swap_cores(doc_index[0])
     both = jnp.where(core == 0, jnp.stack([kept, came], axis=1), jnp.stack([came, kept], axis=1))
     own = both.reshape(8, 2 * CHUNK)
 
-    own, output_grads = lax.optimization_barrier((own, output_grads))
+    chip_ids = jnp.where(core == 0, jnp.stack([doc_index[0], ids_came]), jnp.stack([ids_came, doc_index[0]]))
+    own, output_grads, chip_ids = lax.optimization_barrier((own, output_grads, chip_ids))
+    mate_ids = lax.ppermute(chip_ids, "xl", [(0, 1), (1, 0)])
     g_other = swap_cores(output_grads)
     slots, first_came = gather_z(own)
-    first_came, layer_inputs, own_ids = lax.optimization_barrier((first_came, layer_inputs, doc_index[0]))
+    first_came, layer_inputs, mate_ids = lax.optimization_barrier((first_came, layer_inputs, mate_ids))
     x_other = swap_cores(layer_inputs)
-    ids = lax.all_gather(own_ids, ("xl", "core"), axis=0, tiled=True)
 
     halves = [slots[:, :CHUNK].reshape(32, 2 * CHUNK), slots[:, CHUNK:].reshape(32, 2 * CHUNK)]
-    halves, x_other, g_other, ids = lax.optimization_barrier((halves, x_other, g_other, ids))
+    halves, x_other, g_other = lax.optimization_barrier((halves, x_other, g_other))
 
     first, second = direct(halves[0], "y"), direct(halves[1], "x")
 
@@ -210,6 +213,7 @@
     far_first = go_round(first[2], first[3], "x")
     odd_second = go_round(second[1], second[3], "y")
 
+    ids = jnp.where(xl == 0, jnp.stack([chip_ids, mate_ids]), jnp.stack([mate_ids, chip_ids])).reshape(-1)
     weights = doc_weights(ids, kept_counts[0])
     seq = xl * 2 + core
     w_own = lax.dynamic_slice(weights, (0, seq * 256), (DOCS, 256))

time: 110 us -> 105 us (0.955)
  starting transfers between devices: 45.2 us -> 52.5 us
  waiting for transfers between devices: 31.6 us -> 24.9 us
  blocking collectives: 5.02 us -> 0 us
  Pallas kernels: 17.4 us -> 14.2 us
  local copies, waits for them, and re-layouts: 5.33 us -> 8.18 us
    ppermute x24, starting transfers between devices: 38.2 us -> 44.8 us  [shift(): return lax.ppermute(value, AXES, pairs)]
    ppermute x24, waiting for transfers between devices: 29 us -> 23.1 us  [shift(): return lax.ppermute(value, AXES, pairs)]
    all_gather x1 -> x0, blocking collectives: 5.02 us -> none  [shards(): ids = lax.all_gather(own_ids, ('xl', 'core'), axis=0, tiled=True)]
    unnamed x22 -> x25, local copies, waits for them, and re-layouts: 2.26 us -> 6.21 us
    pallas_call x2, Pallas kernels: 17.4 us -> 14.2 us  [score(): pl.pallas_call(odd_kernel if last else even_kernel, in_specs=[pl.BlockSpe...]
    ppermute x0 -> x1, starting transfers between devices: none -> 1.21 us  [shards(): mate_ids = lax.ppermute(chip_ids, 'xl', [(0, 1), (1, 0)])]
    ppermute x3 -> x4, starting transfers between devices: 3.77 us -> 3.74 us  [swap_cores(): return lax.ppermute(value, 'core', [(0, 1), (1, 0)])]
  transfers between devices with their start and end apart: 30 -> 32, of which waited for: 14 -> 12; matrix products, arithmetic and copies ran while one was open for 4% -> 7% of each run, Pallas kernels for 7% -> 6%
where the time goes in v2:
time: 105 us
  starting transfers between devices  52.5 us (50%)
  waiting for transfers between devices  24.9 us (24%)
  Pallas kernels  14.2 us (14%)
  local copies, waits for them, and re-layouts  8.18 us (8%)
  other arithmetic  4.87 us (5%)
    ppermute x24, starting transfers between devices, shift(): return lax.ppermute(value, AXES, pairs)  44.8 us
    ppermute x24, waiting for transfers between devices, shift(): return lax.ppermute(value, AXES, pairs)  23.1 us
    pallas_call x2, Pallas kernels, score(): pl.pallas_call(odd_kernel if last else even_kernel, in_specs=[pl.BlockSpe...  14.2 us
    unnamed x25, local copies, waits for them, and re-layouts  6.21 us
    ppermute x4, starting transfers between devices, swap_cores(): return lax.ppermute(value, 'core', [(0, 1), (1, 0)])  3.74 us
    ppermute x3, starting transfers between devices, shards(): lax.ppermute(pieces[away], ('xl', 'core'), [(i, i ^ away) for i in range(...  2.66 us
  transfers between devices with their start and end apart: 32, of which 12 were waited for; matrix products, arithmetic and copies ran while one was open for 7% of the time, Pallas kernels for 6%

profile of v2, /device:TPU:1, one launch (start us, length us, event | category | flops | bytes accessed | tf_op | source)
XLA Modules:
  0.0 105.0 jit_solution(3670709942429755920)
XLA Ops:
  0.0 3.2 %collective-permute-start.1 = (s32[256]{0:T(256)}, s32[256]{0:T(256)S(1)}, u32[]{:S(2)}, u32[]{:S(2)}) collective-permute-start(s32[256]{0:T(256)} %bitcast.33), channel_id=1, source_target_pairs={{0,1},{1,0},{2,3},{3,2},{4,5},{5,4},{6,7},{7,6},{8,9},{9,8},{10,11... | collective-permute-start | bytes 3080 | tf_op jit(solution)/shard_map/ppermute | solution.py:42
  3.2 0.7 broadcast_add_fusion
  4.0 0.8 fusion
  4.8 0.7 broadcast_add_fusion.1
  5.5 0.7 fusion.3
  6.6 0.8 add_select_fusion.1
  8.1 3.8 %collective-permute-start.2 = (bf16[8,4608]{1,0:T(8,128)(2,1)S(1)}, bf16[8,4608]{1,0:T(8,128)(2,1)S(1)}, u32[]{:S(2)}, u32[]{:S(2)}) collective-permute-start(bf16[8,4608]{1,0:T(8,128)(2,1)S(1)} %select_n.58), channel_id=1, source_target_pairs={{0,8},{1,57},{2,10},{3,59},{4,12},{5,61},{6,14},{7,63},{8,16},{9,1... | collective-permute-start | bytes 221192 | tf_op jit(solution)/shard_map/ppermute | solution.py:38
  11.9 1.2 %collective-permute-start.4 = (bf16[8,4608]{1,0:T(8,128)(2,1)S(1)}, bf16[8,4608]{1,0:T(8,128)(2,1)S(1)}, u32[]{:S(2)}, u32[]{:S(2)}) collective-permute-start(bf16[8,4608]{1,0:T(8,128)(2,1)S(1)} %select_n.58), channel_id=1, source_target_pairs={{0,16},{1,49},{2,18},{3,51},{4,20},{5,53},{6,22},{7,55},{8,24},{9,... | collective-permute-start | bytes 221192 | tf_op jit(solution)/shard_map/ppermute | solution.py:38
  13.1 0.7 collective-permute-start.6
  14.4 1.2 %collective-permute-start.3 = (s32[2,256]{1,0:T(2,128)S(1)}, s32[2,256]{1,0:T(2,128)S(1)}, u32[]{:S(2)}, u32[]{:S(2)}) collective-permute-start(s32[2,256]{1,0:T(2,128)S(1)} %add_select_fusion.1), channel_id=1, source_target_pairs={{0,2},{2,0},{1,3},{3,1},{4,6},{6,4},{5,7},{7,5},{8,10},{10,8},{9,1... | collective-permute-start | bytes 6152 | tf_op jit(solution)/shard_map/ppermute | solution.py:194
  15.6 0.7 collective-permute-done.4
  16.3 3.3 %collective-permute-start.5 = (bf16[16,4608]{1,0:T(8,128)(2,1)S(1)}, bf16[16,4608]{1,0:T(8,128)(2,1)S(1)}, u32[]{:S(2)}, u32[]{:S(2)}) collective-permute-start(bf16[16,4608]{1,0:T(8,128)(2,1)S(1)} %pad_maximum_fusion), channel_id=1, source_target_pairs={{0,16},{1,49},{2,18},{3,51},{4,20},{5,53},{6,22},{7,55},{8,24},{9,... | collective-permute-start | bytes 442376 | tf_op jit(solution)/shard_map/ppermute | solution.py:38
  19.6 3.3 %collective-permute-start.7 = (bf16[8,4608]{1,0:T(8,128)(2,1)S(1)}, bf16[8,4608]{1,0:T(8,128)(2,1)S(1)}, u32[]{:S(2)}, u32[]{:S(2)}) collective-permute-start(bf16[8,4608]{1,0:T(8,128)(2,1)S(1)} %collective-permute-done.6), channel_id=1, source_target_pairs={{0,48},{1,17},{2,50},{3,19},{4,52},{5,21},{6,54},{7,23},{8,56},{9,... | collective-permute-start | bytes 221192 | tf_op jit(solution)/shard_map/ppermute | solution.py:38
  22.9 2.6 %collective-permute-done.7 = bf16[8,4608]{1,0:T(8,128)(2,1)S(1)} collective-permute-done((bf16[8,4608]{1,0:T(8,128)(2,1)S(1)}, bf16[8,4608]{1,0:T(8,128)(2,1)S(1)}, u32[]{:S(2)}, u32[]{:S(2)}) %collective-permute-start.7) | collective-permute-done | bytes 73760 | tf_op jit(solution)/shard_map/ppermute | solution.py:38
  25.6 0.8 reshape.64
  26.4 0.8 reshape.65
  27.2 1.0 constant_dynamic-update-slice_fusion.14
  28.2 3.1 %collective-permute-start.25 = (bf16[32,4608]{1,0:T(8,128)(2,1)}, bf16[32,4608]{1,0:T(8,128)(2,1)S(1)}, u32[]{:S(2)}, u32[]{:S(2)}) collective-permute-start(bf16[32,4608]{1,0:T(8,128)(2,1)} %reshape.65), channel_id=1, source_target_pairs={{0,4},{1,5},{2,6},{3,7},{4,0},{5,1},{6,2},{7,3},{8,12},{9,13},{10,... | collective-permute-start | bytes 884744 | tf_op jit(solution)/shard_map/ppermute | solution.py:38
  31.3 2.9 %collective-permute-start.13 = (bf16[32,4608]{1,0:T(8,128)(2,1)}, bf16[32,4608]{1,0:T(8,128)(2,1)S(1)}, u32[]{:S(2)}, u32[]{:S(2)}) collective-permute-start(bf16[32,4608]{1,0:T(8,128)(2,1)} %reshape.64), channel_id=1, source_target_pairs={{0,128},{1,129},{2,130},{3,131},{4,132},{5,133},{6,134},{7,135},{8... | collective-permute-start | bytes 884744 | tf_op jit(solution)/shard_map/ppermute | solution.py:38
  34.6 2.3 %collective-permute-start.11 = (bf16[32,4608]{1,0:T(8,128)(2,1)}, bf16[32,4608]{1,0:T(8,128)(2,1)S(1)}, u32[]{:S(2)}, u32[]{:S(2)}) collective-permute-start(bf16[32,4608]{1,0:T(8,128)(2,1)} %reshape.64), channel_id=1, source_target_pairs={{0,64},{1,193},{2,66},{3,195},{4,68},{5,197},{6,70},{7,199},{8,72}... | collective-permute-start | bytes 884744 | tf_op jit(solution)/shard_map/ppermute | solution.py:38
  36.9 1.2 %collective-permute-start.20 = (bf16[32,4608]{1,0:T(8,128)(2,1)}, bf16[32,4608]{1,0:T(8,128)(2,1)S(1)}, u32[]{:S(2)}, u32[]{:S(2)}) collective-permute-start(bf16[32,4608]{1,0:T(8,128)(2,1)} %reshape.65), channel_id=1, source_target_pairs={{0,2},{1,7},{2,4},{3,1},{4,6},{5,3},{6,0},{7,5},{8,10},{9,15},{10,... | collective-permute-start | bytes 884744 | tf_op jit(solution)/shard_map/ppermute | solution.py:38
  38.1 1.0 constant_dynamic-update-slice_fusion.8
  39.1 1.6 %collective-permute-start.21 = (bf16[32,4608]{1,0:T(8,128)(2,1)}, bf16[32,4608]{1,0:T(8,128)(2,1)S(1)}, u32[]{:S(2)}, u32[]{:S(2)}) collective-permute-start(bf16[32,4608]{1,0:T(8,128)(2,1)} %reshape.65), channel_id=1, source_target_pairs={{0,6},{1,3},{2,0},{3,5},{4,2},{5,7},{6,4},{7,1},{8,14},{9,11},{10,... | collective-permute-start | bytes 884744 | tf_op jit(solution)/shard_map/ppermute | solution.py:38
  41.3 2.8 %collective-permute-start.26 = (bf16[64,4608]{1,0:T(8,128)(2,1)S(1)}, bf16[64,4608]{1,0:T(8,128)(2,1)}, u32[]{:S(2)}, u32[]{:S(2)}) collective-permute-start(bf16[64,4608]{1,0:T(8,128)(2,1)S(1)} %constant_dynamic-update-slice_fusion.13.refs_8_), channel_id=1, source_target_pairs={{0,64},{1,193},{2,66},{3,195},{4,68},{5,197},{6,70},{7,199},{8,72}... | collective-permute-start | bytes 1769480 | tf_op jit(solution)/shard_map/ppermute | solution.py:38
  44.1 4.1 %collective-permute-done.14 = bf16[32,4608]{1,0:T(8,128)(2,1)S(1)} collective-permute-done((bf16[32,4608]{1,0:T(8,128)(2,1)}, bf16[32,4608]{1,0:T(8,128)(2,1)S(1)}, u32[]{:S(2)}, u32[]{:S(2)}) %collective-permute-start.14) | collective-permute-done | bytes 294944 | tf_op jit(solution)/shard_map/ppermute | solution.py:38
  48.3 1.3 %collective-permute-start.15 = (bf16[64,4608]{1,0:T(8,128)(2,1)S(1)}, bf16[64,4608]{1,0:T(8,128)(2,1)}, u32[]{:S(2)}, u32[]{:S(2)}) collective-permute-start(bf16[64,4608]{1,0:T(8,128)(2,1)S(1)} %constant_dynamic-update-slice_fusion.9.refs_5_), channel_id=1, source_target_pairs={{0,2},{1,7},{2,4},{3,1},{4,6},{5,3},{6,0},{7,5},{8,10},{9,15},{10,... | collective-permute-start | bytes 1769480 | tf_op jit(solution)/shard_map/ppermute | solution.py:38
  49.9 1.3 %collective-permute-start.12 = (bf16[64,4608]{1,0:T(8,128)(2,1)S(1)}, bf16[64,4608]{1,0:T(8,128)(2,1)}, u32[]{:S(2)}, u32[]{:S(2)}) collective-permute-start(bf16[64,4608]{1,0:T(8,128)(2,1)S(1)} %constant_dynamic-update-slice_fusion.7.refs_4_), channel_id=1, source_target_pairs={{0,2},{1,7},{2,4},{3,1},{4,6},{5,3},{6,0},{7,5},{8,10},{9,15},{10,... | collective-permute-start | bytes 1769480 | tf_op jit(solution)/shard_map/ppermute | solution.py:38
  51.2 3.9 %collective-permute-done.26.refs_9_ = bf16[64,4608]{1,0:T(8,128)(2,1)} collective-permute-done((bf16[64,4608]{1,0:T(8,128)(2,1)S(1)}, bf16[64,4608]{1,0:T(8,128)(2,1)}, u32[]{:S(2)}, u32[]{:S(2)}) %collective-permute-start.26) | collective-permute-done | bytes 589856 | tf_op jit(solution)/shard_map/ppermute | solution.py:38
  55.2 2.3 %collective-permute-start.27 = (bf16[64,4608]{1,0:T(8,128)(2,1)}, bf16[64,4608]{1,0:T(8,128)(2,1)}, u32[]{:S(2)}, u32[]{:S(2)}) collective-permute-start(bf16[64,4608]{1,0:T(8,128)(2,1)} %collective-permute-done.26.refs_9_), channel_id=1, source_target_pairs={{0,64},{1,193},{2,66},{3,195},{4,68},{5,197},{6,70},{7,199},{8,72}... | collective-permute-start | bytes 1769480 | tf_op jit(solution)/shard_map/ppermute | solution.py:38
  57.5 4.0 %collective-permute-done.22.refs_9_ = bf16[64,4608]{1,0:T(8,128)(2,1)} collective-permute-done((bf16[64,4608]{1,0:T(8,128)(2,1)S(1)}, bf16[64,4608]{1,0:T(8,128)(2,1)}, u32[]{:S(2)}, u32[]{:S(2)}) %collective-permute-start.22) | collective-permute-done | bytes 589856 | tf_op jit(solution)/shard_map/ppermute | solution.py:38
  61.5 2.3 %collective-permute-start.23 = (bf16[64,4608]{1,0:T(8,128)(2,1)}, bf16[64,4608]{1,0:T(8,128)(2,1)}, u32[]{:S(2)}, u32[]{:S(2)}) collective-permute-start(bf16[64,4608]{1,0:T(8,128)(2,1)} %collective-permute-done.22.refs_9_), channel_id=1, source_target_pairs={{0,64},{1,193},{2,66},{3,195},{4,68},{5,197},{6,70},{7,199},{8,72}... | collective-permute-start | bytes 1769480 | tf_op jit(solution)/shard_map/ppermute | solution.py:38
  63.8 1.0 collective-permute-start.18
  64.8 1.5 %collective-permute-start.16 = (bf16[64,4608]{1,0:T(8,128)(2,1)}, bf16[64,4608]{1,0:T(8,128)(2,1)}, u32[]{:S(2)}, u32[]{:S(2)}) collective-permute-start(bf16[64,4608]{1,0:T(8,128)(2,1)} %collective-permute-done.12.refs_4_), channel_id=1, source_target_pairs={{0,2},{1,7},{2,4},{3,1},{4,6},{5,3},{6,0},{7,5},{8,10},{9,15},{10,... | collective-permute-start | bytes 1769480 | tf_op jit(solution)/shard_map/ppermute | solution.py:38
  66.7 1.1 %collective-permute-done.27.refs_10_ = bf16[64,4608]{1,0:T(8,128)(2,1)} collective-permute-done((bf16[64,4608]{1,0:T(8,128)(2,1)}, bf16[64,4608]{1,0:T(8,128)(2,1)}, u32[]{:S(2)}, u32[]{:S(2)}) %collective-permute-start.27) | collective-permute-done | bytes 589856 | tf_op jit(solution)/shard_map/ppermute | solution.py:38
  67.8 2.3 %collective-permute-start.28 = (bf16[64,4608]{1,0:T(8,128)(2,1)}, bf16[64,4608]{1,0:T(8,128)(2,1)S(1)}, u32[]{:S(2)}, u32[]{:S(2)}) collective-permute-start(bf16[64,4608]{1,0:T(8,128)(2,1)} %collective-permute-done.27.refs_10_), channel_id=1, source_target_pairs={{0,64},{1,193},{2,66},{3,195},{4,68},{5,197},{6,70},{7,199},{8,72}... | collective-permute-start | bytes 1769480 | tf_op jit(solution)/shard_map/ppermute | solution.py:38
  70.2 4.0 %collective-permute-done.23.refs_10_ = bf16[64,4608]{1,0:T(8,128)(2,1)} collective-permute-done((bf16[64,4608]{1,0:T(8,128)(2,1)}, bf16[64,4608]{1,0:T(8,128)(2,1)}, u32[]{:S(2)}, u32[]{:S(2)}) %collective-permute-start.23) | collective-permute-done | bytes 589856 | tf_op jit(solution)/shard_map/ppermute | solution.py:38
  74.1 2.3 %collective-permute-start.24 = (bf16[64,4608]{1,0:T(8,128)(2,1)}, bf16[64,4608]{1,0:T(8,128)(2,1)S(1)}, u32[]{:S(2)}, u32[]{:S(2)}) collective-permute-start(bf16[64,4608]{1,0:T(8,128)(2,1)} %collective-permute-done.23.refs_10_), channel_id=1, source_target_pairs={{0,64},{1,193},{2,66},{3,195},{4,68},{5,197},{6,70},{7,199},{8,72}... | collective-permute-start | bytes 1769480 | tf_op jit(solution)/shard_map/ppermute | solution.py:38
  76.5 1.0 collective-permute-start.19
  77.4 2.1 %collective-permute-done.16.refs_6_ = bf16[64,4608]{1,0:T(8,128)(2,1)} collective-permute-done((bf16[64,4608]{1,0:T(8,128)(2,1)}, bf16[64,4608]{1,0:T(8,128)(2,1)}, u32[]{:S(2)}, u32[]{:S(2)}) %collective-permute-start.16) | collective-permute-done | bytes 589856 | tf_op jit(solution)/shard_map/ppermute | solution.py:38
  79.5 2.1 %collective-permute-start.17 = (bf16[64,4608]{1,0:T(8,128)(2,1)}, bf16[64,4608]{1,0:T(8,128)(2,1)S(1)}, u32[]{:S(2)}, u32[]{:S(2)}) collective-permute-start(bf16[64,4608]{1,0:T(8,128)(2,1)} %collective-permute-done.16.refs_6_), channel_id=1, source_target_pairs={{0,2},{1,7},{2,4},{3,1},{4,6},{5,3},{6,0},{7,5},{8,10},{9,15},{10,... | collective-permute-start | bytes 1769480 | tf_op jit(solution)/shard_map/ppermute | solution.py:38
  81.7 3.1 %copy-done = bf16[256,14336]{1,0:T(8,128)(2,1)S(1)} copy-done((bf16[256,14336]{1,0:T(8,128)(2,1)S(1)}, bf16[256,14336]{1,0:T(8,128)(2,1)}, u32[]{:S(2)}) %copy-start) | copy-done | bytes 7340056
  84.8 1.1 %copy-done.5 = bf16[64,4608]{1,0:T(8,128)(2,1)S(1)} copy-done((bf16[64,4608]{1,0:T(8,128)(2,1)S(1)}, bf16[64,4608]{1,0:T(8,128)(2,1)}, u32[]{:S(2)}) %copy-start.5) | copy-done | bytes 589848
  85.8 6.8 %shard_map.82 = (f32[512,256]{1,0:T(8,128)S(1)}, f32[512,256]{1,0:T(8,128)S(1)}) custom-call(s32[5]{0:T(128)S(1)} %stack.61.where, bf16[256,4096]{1,0:T(8,128)(2,1)S(1)} %copy-done.1, bf16[256,4096]{1,0:T(8,128)(2,1)} %collective-permute-done.9.refs_1_, bf16[256,14336]{1,0:T(8,128)(2,1)S(1)} %copy-done, bf16[256,14336]{1,0:T(8,128)(2,1)} %collective-permute-done.10.refs_3_, ...), custom_call_target="tpu_custom_call" | custom-call | flops 2415919104 | bytes 14155776 | tf_op jit(solution)/shard_map/pallas_call | solution.py:148
  92.6 7.5 %shard_map.83 = (f32[8,16]{1,0:T(8,128)S(1)}, f32[8,16]{1,0:T(8,128)S(1)}, f32[8,16]{1,0:T(8,128)S(1)}, f32[8,16]{1,0:T(8,128)S(1)}) custom-call(s32[5]{0:T(128)S(1)} %stack.61.where, bf16[256,4096]{1,0:T(8,128)(2,1)S(1)} %copy-done.1, bf16[256,4096]{1,0:T(8,128)(2,1)} %collective-permute-done.9.refs_1_, bf16[256,14336]{1,0:T(8,128)(2,1)S(1)} %copy-done, ...), custom_call_target="tpu_custom_call" | custom-call | flops 2415919104 | bytes 14155776 | tf_op jit(solution)/shard_map/pallas_call | solution.py:148
  100.1 0.9 collective-permute-start.29
  101.1 1.7 %collective-permute-start.31 = (f32[8,16]{1,0:T(8,128)S(1)}, f32[8,16]{1,0:T(8,128)S(1)}, u32[]{:S(2)}, u32[]{:S(2)}) collective-permute-start(f32[8,16]{1,0:T(8,128)S(1)} %get-tuple-element.34), channel_id=1, source_target_pairs={{0,3},{1,2},{2,1},{3,0},{4,7},{5,6},{6,5},{7,4},{8,11},{9,10},{10,... | collective-permute-start | bytes 1544 | tf_op jit(solution)/shard_map/ppermute | solution.py:234
  102.8 0.7 collective-permute-done.30
  103.6 0.8 collective-permute-done.31
  (73 shorter events, 4.1 us)
Async XLA Ops:
  0.0 81.7 %copy-start.1 = (bf16[256,4096]{1,0:T(8,128)(2,1)S(1)}, bf16[256,4096]{1,0:T(8,128)(2,1)}, u32[]{:S(2)}) copy-start(bf16[256,4096]{1,0:T(8,128)(2,1)} %refs_0_.1) | copy-start | bytes 6291460
  0.0 81.6 %copy-start.6 = (s32[1,8]{1,0:T(1,128)S(1)}, s32[1,8]{1,0:T(1,128)}, u32[]{:S(2)}) copy-start(s32[1,8]{1,0:T(1,128)} %param.15) | copy-start | bytes 100
  0.0 6.6 %collective-permute-start.1 = (s32[256]{0:T(256)}, s32[256]{0:T(256)S(1)}, u32[]{:S(2)}, u32[]{:S(2)}) collective-permute-start(s32[256]{0:T(256)} %bitcast.33), channel_id=1, source_target_pairs={{0,1},{1,0},{2,3},{3,2},{4,5},{5,4},{6,7},{7,6},{8,9},{9,8},{10,11... | collective-permute-start | bytes 3080 | tf_op jit(solution)/shard_map/ppermute | solution.py:42
  6.3 1.3 %collective-permute-start = (bf16[4,4608]{1,0:T(4,128)(2,1)S(1)}, bf16[4,4608]{1,0:T(4,128)(2,1)S(1)}, u32[]{:S(2)}, u32[]{:S(2)}) collective-permute-start(bf16[4,4608]{1,0:T(4,128)(2,1)S(1)} %get-tuple-element.38), channel_id=1, source_target_pairs={{0,1},{1,0},{2,3},{3,2},{4,5},{5,4},{6,7},{7,6},{8,9},{9,8},{10,11... | collective-permute-start | bytes 110600 | tf_op jit(solution)/shard_map/ppermute | solution.py:42
  7.8 19.4 %collective-permute-start.10 = (bf16[256,14336]{1,0:T(8,128)(2,1)}, bf16[256,14336]{1,0:T(8,128)(2,1)}, u32[]{:S(2)}, u32[]{:S(2)}) collective-permute-start(bf16[256,14336]{1,0:T(8,128)(2,1)} %refs_2_.1), channel_id=1, source_target_pairs={{0,1},{1,0},{2,3},{3,2},{4,5},{5,4},{6,7},{7,6},{8,9},{9,8},{10,11... | collective-permute-start | bytes 22020104 | tf_op jit(solution)/shard_map/ppermute | solution.py:42
  8.1 6.3 %collective-permute-start.2 = (bf16[8,4608]{1,0:T(8,128)(2,1)S(1)}, bf16[8,4608]{1,0:T(8,128)(2,1)S(1)}, u32[]{:S(2)}, u32[]{:S(2)}) collective-permute-start(bf16[8,4608]{1,0:T(8,128)(2,1)S(1)} %select_n.58), channel_id=1, source_target_pairs={{0,8},{1,57},{2,10},{3,59},{4,12},{5,61},{6,14},{7,63},{8,16},{9,1... | collective-permute-start | bytes 221192 | tf_op jit(solution)/shard_map/ppermute | solution.py:38
  11.9 4.4 %collective-permute-start.4 = (bf16[8,4608]{1,0:T(8,128)(2,1)S(1)}, bf16[8,4608]{1,0:T(8,128)(2,1)S(1)}, u32[]{:S(2)}, u32[]{:S(2)}) collective-permute-start(bf16[8,4608]{1,0:T(8,128)(2,1)S(1)} %select_n.58), channel_id=1, source_target_pairs={{0,16},{1,49},{2,18},{3,51},{4,20},{5,53},{6,22},{7,55},{8,24},{9,... | collective-permute-start | bytes 221192 | tf_op jit(solution)/shard_map/ppermute | solution.py:38
  13.1 6.5 %collective-permute-start.6 = (bf16[8,4608]{1,0:T(8,128)(2,1)S(1)}, bf16[8,4608]{1,0:T(8,128)(2,1)S(1)}, u32[]{:S(2)}, u32[]{:S(2)}) collective-permute-start(bf16[8,4608]{1,0:T(8,128)(2,1)S(1)} %select_n.58), channel_id=1, source_target_pairs={{0,56},{1,9},{2,58},{3,11},{4,60},{5,13},{6,62},{7,15},{8,0},{9,17... | collective-permute-start | bytes 221192 | tf_op jit(solution)/shard_map/ppermute | solution.py:38
  13.8 11.7 %collective-permute-start.8 = (bf16[8,4608]{1,0:T(8,128)(2,1)S(1)}, bf16[8,4608]{1,0:T(8,128)(2,1)S(1)}, u32[]{:S(2)}, u32[]{:S(2)}) collective-permute-start(bf16[8,4608]{1,0:T(8,128)(2,1)S(1)} %select_n.58), channel_id=1, source_target_pairs={{0,48},{1,17},{2,50},{3,19},{4,52},{5,21},{6,54},{7,23},{8,56},{9,... | collective-permute-start | bytes 221192 | tf_op jit(solution)/shard_map/ppermute | solution.py:38
  14.4 5.2 %collective-permute-start.3 = (s32[2,256]{1,0:T(2,128)S(1)}, s32[2,256]{1,0:T(2,128)S(1)}, u32[]{:S(2)}, u32[]{:S(2)}) collective-permute-start(s32[2,256]{1,0:T(2,128)S(1)} %add_select_fusion.1), channel_id=1, source_target_pairs={{0,2},{2,0},{1,3},{3,1},{4,6},{6,4},{5,7},{7,5},{8,10},{10,8},{9,1... | collective-permute-start | bytes 6152 | tf_op jit(solution)/shard_map/ppermute | solution.py:194
  16.3 6.6 %collective-permute-start.5 = (bf16[16,4608]{1,0:T(8,128)(2,1)S(1)}, bf16[16,4608]{1,0:T(8,128)(2,1)S(1)}, u32[]{:S(2)}, u32[]{:S(2)}) collective-permute-start(bf16[16,4608]{1,0:T(8,128)(2,1)S(1)} %pad_maximum_fusion), channel_id=1, source_target_pairs={{0,16},{1,49},{2,18},{3,51},{4,20},{5,53},{6,22},{7,55},{8,24},{9,... | collective-permute-start | bytes 442376 | tf_op jit(solution)/shard_map/ppermute | solution.py:38
  19.6 7.7 %collective-permute-start.9 = (bf16[256,4096]{1,0:T(8,128)(2,1)}, bf16[256,4096]{1,0:T(8,128)(2,1)}, u32[]{:S(2)}, u32[]{:S(2)}) collective-permute-start(bf16[256,4096]{1,0:T(8,128)(2,1)} %refs_0_.1), channel_id=1, source_target_pairs={{0,1},{1,0},{2,3},{3,2},{4,5},{5,4},{6,7},{7,6},{8,9},{9,8},{10,11... | collective-permute-start | bytes 6291464 | tf_op jit(solution)/shard_map/ppermute | solution.py:42
  19.6 5.9 %collective-permute-start.7 = (bf16[8,4608]{1,0:T(8,128)(2,1)S(1)}, bf16[8,4608]{1,0:T(8,128)(2,1)S(1)}, u32[]{:S(2)}, u32[]{:S(2)}) collective-permute-start(bf16[8,4608]{1,0:T(8,128)(2,1)S(1)} %collective-permute-done.6), channel_id=1, source_target_pairs={{0,48},{1,17},{2,50},{3,19},{4,52},{5,21},{6,54},{7,23},{8,56},{9,... | collective-permute-start | bytes 221192 | tf_op jit(solution)/shard_map/ppermute | solution.py:38
  28.2 10.9 %collective-permute-start.25 = (bf16[32,4608]{1,0:T(8,128)(2,1)}, bf16[32,4608]{1,0:T(8,128)(2,1)S(1)}, u32[]{:S(2)}, u32[]{:S(2)}) collective-permute-start(bf16[32,4608]{1,0:T(8,128)(2,1)} %reshape.65), channel_id=1, source_target_pairs={{0,4},{1,5},{2,6},{3,7},{4,0},{5,1},{6,2},{7,3},{8,12},{9,13},{10,... | collective-permute-start | bytes 884744 | tf_op jit(solution)/shard_map/ppermute | solution.py:38
  31.3 10.0 %collective-permute-start.13 = (bf16[32,4608]{1,0:T(8,128)(2,1)}, bf16[32,4608]{1,0:T(8,128)(2,1)S(1)}, u32[]{:S(2)}, u32[]{:S(2)}) collective-permute-start(bf16[32,4608]{1,0:T(8,128)(2,1)} %reshape.64), channel_id=1, source_target_pairs={{0,128},{1,129},{2,130},{3,131},{4,132},{5,133},{6,134},{7,135},{8... | collective-permute-start | bytes 884744 | tf_op jit(solution)/shard_map/ppermute | solution.py:38
  34.2 14.1 %collective-permute-start.14 = (bf16[32,4608]{1,0:T(8,128)(2,1)}, bf16[32,4608]{1,0:T(8,128)(2,1)S(1)}, u32[]{:S(2)}, u32[]{:S(2)}) collective-permute-start(bf16[32,4608]{1,0:T(8,128)(2,1)} %reshape.64), channel_id=1, source_target_pairs={{0,192},{1,65},{2,194},{3,67},{4,196},{5,69},{6,198},{7,71},{8,200... | collective-permute-start | bytes 884744 | tf_op jit(solution)/shard_map/ppermute | solution.py:38
  34.6 15.3 %collective-permute-start.11 = (bf16[32,4608]{1,0:T(8,128)(2,1)}, bf16[32,4608]{1,0:T(8,128)(2,1)S(1)}, u32[]{:S(2)}, u32[]{:S(2)}) collective-permute-start(bf16[32,4608]{1,0:T(8,128)(2,1)} %reshape.64), channel_id=1, source_target_pairs={{0,64},{1,193},{2,66},{3,195},{4,68},{5,197},{6,70},{7,199},{8,72}... | collective-permute-start | bytes 884744 | tf_op jit(solution)/shard_map/ppermute | solution.py:38
  36.9 12.7 %collective-permute-start.20 = (bf16[32,4608]{1,0:T(8,128)(2,1)}, bf16[32,4608]{1,0:T(8,128)(2,1)S(1)}, u32[]{:S(2)}, u32[]{:S(2)}) collective-permute-start(bf16[32,4608]{1,0:T(8,128)(2,1)} %reshape.65), channel_id=1, source_target_pairs={{0,2},{1,7},{2,4},{3,1},{4,6},{5,3},{6,0},{7,5},{8,10},{9,15},{10,... | collective-permute-start | bytes 884744 | tf_op jit(solution)/shard_map/ppermute | solution.py:38
  39.1 10.5 %collective-permute-start.21 = (bf16[32,4608]{1,0:T(8,128)(2,1)}, bf16[32,4608]{1,0:T(8,128)(2,1)S(1)}, u32[]{:S(2)}, u32[]{:S(2)}) collective-permute-start(bf16[32,4608]{1,0:T(8,128)(2,1)} %reshape.65), channel_id=1, source_target_pairs={{0,6},{1,3},{2,0},{3,5},{4,2},{5,7},{6,4},{7,1},{8,14},{9,11},{10,... | collective-permute-start | bytes 884744 | tf_op jit(solution)/shard_map/ppermute | solution.py:38
  41.3 13.8 %collective-permute-start.26 = (bf16[64,4608]{1,0:T(8,128)(2,1)S(1)}, bf16[64,4608]{1,0:T(8,128)(2,1)}, u32[]{:S(2)}, u32[]{:S(2)}) collective-permute-start(bf16[64,4608]{1,0:T(8,128)(2,1)S(1)} %constant_dynamic-update-slice_fusion.13.refs_8_), channel_id=1, source_target_pairs={{0,64},{1,193},{2,66},{3,195},{4,68},{5,197},{6,70},{7,199},{8,72}... | collective-permute-start | bytes 1769480 | tf_op jit(solution)/shard_map/ppermute | solution.py:38
  48.3 16.5 %copy-start.4 = (bf16[64,4608]{1,0:T(8,128)(2,1)}, bf16[64,4608]{1,0:T(8,128)(2,1)S(1)}, u32[]{:S(2)}) copy-start(bf16[64,4608]{1,0:T(8,128)(2,1)S(1)} %constant_dynamic-update-slice_fusion.9.refs_5_) | copy-start | bytes 1769476
  48.3 15.5 %collective-permute-start.15 = (bf16[64,4608]{1,0:T(8,128)(2,1)S(1)}, bf16[64,4608]{1,0:T(8,128)(2,1)}, u32[]{:S(2)}, u32[]{:S(2)}) collective-permute-start(bf16[64,4608]{1,0:T(8,128)(2,1)S(1)} %constant_dynamic-update-slice_fusion.9.refs_5_), channel_id=1, source_target_pairs={{0,2},{1,7},{2,4},{3,1},{4,6},{5,3},{6,0},{7,5},{8,10},{9,15},{10,... | collective-permute-start | bytes 1769480 | tf_op jit(solution)/shard_map/ppermute | solution.py:38
  49.7 15.1 %copy-start.2 = (bf16[64,4608]{1,0:T(8,128)(2,1)}, bf16[64,4608]{1,0:T(8,128)(2,1)S(1)}, u32[]{:S(2)}) copy-start(bf16[64,4608]{1,0:T(8,128)(2,1)S(1)} %constant_dynamic-update-slice_fusion.11.refs_8_) | copy-start | bytes 1769476
  49.7 11.8 %collective-permute-start.22 = (bf16[64,4608]{1,0:T(8,128)(2,1)S(1)}, bf16[64,4608]{1,0:T(8,128)(2,1)}, u32[]{:S(2)}, u32[]{:S(2)}) collective-permute-start(bf16[64,4608]{1,0:T(8,128)(2,1)S(1)} %constant_dynamic-update-slice_fusion.11.refs_8_), channel_id=1, source_target_pairs={{0,64},{1,193},{2,66},{3,195},{4,68},{5,197},{6,70},{7,199},{8,72}... | collective-permute-start | bytes 1769480 | tf_op jit(solution)/shard_map/ppermute | solution.py:38
  49.9 14.9 %collective-permute-start.12 = (bf16[64,4608]{1,0:T(8,128)(2,1)S(1)}, bf16[64,4608]{1,0:T(8,128)(2,1)}, u32[]{:S(2)}, u32[]{:S(2)}) collective-permute-start(bf16[64,4608]{1,0:T(8,128)(2,1)S(1)} %constant_dynamic-update-slice_fusion.7.refs_4_), channel_id=1, source_target_pairs={{0,2},{1,7},{2,4},{3,1},{4,6},{5,3},{6,0},{7,5},{8,10},{9,15},{10,... | collective-permute-start | bytes 1769480 | tf_op jit(solution)/shard_map/ppermute | solution.py:38
  55.2 12.6 %collective-permute-start.27 = (bf16[64,4608]{1,0:T(8,128)(2,1)}, bf16[64,4608]{1,0:T(8,128)(2,1)}, u32[]{:S(2)}, u32[]{:S(2)}) collective-permute-start(bf16[64,4608]{1,0:T(8,128)(2,1)} %collective-permute-done.26.refs_9_), channel_id=1, source_target_pairs={{0,64},{1,193},{2,66},{3,195},{4,68},{5,197},{6,70},{7,199},{8,72}... | collective-permute-start | bytes 1769480 | tf_op jit(solution)/shard_map/ppermute | solution.py:38
  61.5 12.6 %collective-permute-start.23 = (bf16[64,4608]{1,0:T(8,128)(2,1)}, bf16[64,4608]{1,0:T(8,128)(2,1)}, u32[]{:S(2)}, u32[]{:S(2)}) collective-permute-start(bf16[64,4608]{1,0:T(8,128)(2,1)} %collective-permute-done.22.refs_9_), channel_id=1, source_target_pairs={{0,64},{1,193},{2,66},{3,195},{4,68},{5,197},{6,70},{7,199},{8,72}... | collective-permute-start | bytes 1769480 | tf_op jit(solution)/shard_map/ppermute | solution.py:38
  63.8 12.6 %collective-permute-start.18 = (bf16[64,4608]{1,0:T(8,128)(2,1)}, bf16[64,4608]{1,0:T(8,128)(2,1)}, u32[]{:S(2)}, u32[]{:S(2)}) collective-permute-start(bf16[64,4608]{1,0:T(8,128)(2,1)} %collective-permute-done.15.refs_5_), channel_id=1, source_target_pairs={{0,2},{1,7},{2,4},{3,1},{4,6},{5,3},{6,0},{7,5},{8,10},{9,15},{10,... | collective-permute-start | bytes 1769480 | tf_op jit(solution)/shard_map/ppermute | solution.py:38
  64.8 14.7 %collective-permute-start.16 = (bf16[64,4608]{1,0:T(8,128)(2,1)}, bf16[64,4608]{1,0:T(8,128)(2,1)}, u32[]{:S(2)}, u32[]{:S(2)}) collective-permute-start(bf16[64,4608]{1,0:T(8,128)(2,1)} %collective-permute-done.12.refs_4_), channel_id=1, source_target_pairs={{0,2},{1,7},{2,4},{3,1},{4,6},{5,3},{6,0},{7,5},{8,10},{9,15},{10,... | collective-permute-start | bytes 1769480 | tf_op jit(solution)/shard_map/ppermute | solution.py:38
  67.8 13.9 %collective-permute-start.28 = (bf16[64,4608]{1,0:T(8,128)(2,1)}, bf16[64,4608]{1,0:T(8,128)(2,1)S(1)}, u32[]{:S(2)}, u32[]{:S(2)}) collective-permute-start(bf16[64,4608]{1,0:T(8,128)(2,1)} %collective-permute-done.27.refs_10_), channel_id=1, source_target_pairs={{0,64},{1,193},{2,66},{3,195},{4,68},{5,197},{6,70},{7,199},{8,72}... | collective-permute-start | bytes 1769480 | tf_op jit(solution)/shard_map/ppermute | solution.py:38
  74.1 18.5 %collective-permute-start.24 = (bf16[64,4608]{1,0:T(8,128)(2,1)}, bf16[64,4608]{1,0:T(8,128)(2,1)S(1)}, u32[]{:S(2)}, u32[]{:S(2)}) collective-permute-start(bf16[64,4608]{1,0:T(8,128)(2,1)} %collective-permute-done.23.refs_10_), channel_id=1, source_target_pairs={{0,64},{1,193},{2,66},{3,195},{4,68},{5,197},{6,70},{7,199},{8,72}... | collective-permute-start | bytes 1769480 | tf_op jit(solution)/shard_map/ppermute | solution.py:38
  76.5 16.1 %collective-permute-start.19 = (bf16[64,4608]{1,0:T(8,128)(2,1)}, bf16[64,4608]{1,0:T(8,128)(2,1)S(1)}, u32[]{:S(2)}, u32[]{:S(2)}) collective-permute-start(bf16[64,4608]{1,0:T(8,128)(2,1)} %collective-permute-done.18.refs_7_), channel_id=1, source_target_pairs={{0,2},{1,7},{2,4},{3,1},{4,6},{5,3},{6,0},{7,5},{8,10},{9,15},{10,... | collective-permute-start | bytes 1769480 | tf_op jit(solution)/shard_map/ppermute | solution.py:38
  79.5 13.1 %collective-permute-start.17 = (bf16[64,4608]{1,0:T(8,128)(2,1)}, bf16[64,4608]{1,0:T(8,128)(2,1)S(1)}, u32[]{:S(2)}, u32[]{:S(2)}) collective-permute-start(bf16[64,4608]{1,0:T(8,128)(2,1)} %collective-permute-done.16.refs_6_), channel_id=1, source_target_pairs={{0,2},{1,7},{2,4},{3,1},{4,6},{5,3},{6,0},{7,5},{8,10},{9,15},{10,... | collective-permute-start | bytes 1769480 | tf_op jit(solution)/shard_map/ppermute | solution.py:38
  81.7 3.1 %copy-start = (bf16[256,14336]{1,0:T(8,128)(2,1)S(1)}, bf16[256,14336]{1,0:T(8,128)(2,1)}, u32[]{:S(2)}) copy-start(bf16[256,14336]{1,0:T(8,128)(2,1)} %refs_2_.1) | copy-start | bytes 22020100
  84.8 1.1 %copy-start.5 = (bf16[64,4608]{1,0:T(8,128)(2,1)S(1)}, bf16[64,4608]{1,0:T(8,128)(2,1)}, u32[]{:S(2)}) copy-start(bf16[64,4608]{1,0:T(8,128)(2,1)} %copy-done.4) | copy-start | bytes 1769476
  85.8 6.8 %copy-start.3 = (bf16[64,4608]{1,0:T(8,128)(2,1)S(1)}, bf16[64,4608]{1,0:T(8,128)(2,1)}, u32[]{:S(2)}) copy-start(bf16[64,4608]{1,0:T(8,128)(2,1)} %copy-done.2) | copy-start | bytes 1769476
  100.1 2.7 %collective-permute-start.29 = (f32[8,16]{1,0:T(8,128)S(1)}, f32[8,16]{1,0:T(8,128)S(1)}, u32[]{:S(2)}, u32[]{:S(2)}) collective-permute-start(f32[8,16]{1,0:T(8,128)S(1)} %get-tuple-element.32), channel_id=1, source_target_pairs={{0,1},{1,0},{2,3},{3,2},{4,5},{5,4},{6,7},{7,6},{8,9},{9,8},{10,11... | collective-permute-start | bytes 1544 | tf_op jit(solution)/shard_map/ppermute | solution.py:234
  101.1 2.5 %collective-permute-start.30 = (f32[8,16]{1,0:T(8,128)S(1)}, f32[8,16]{1,0:T(8,128)S(1)}, u32[]{:S(2)}, u32[]{:S(2)}) collective-permute-start(f32[8,16]{1,0:T(8,128)S(1)} %get-tuple-element.33), channel_id=1, source_target_pairs={{0,2},{1,3},{2,0},{3,1},{4,6},{5,7},{6,4},{7,5},{8,10},{9,11},{10,... | collective-permute-start | bytes 1544 | tf_op jit(solution)/shard_map/ppermute | solution.py:234
  101.1 3.3 %collective-permute-start.31 = (f32[8,16]{1,0:T(8,128)S(1)}, f32[8,16]{1,0:T(8,128)S(1)}, u32[]{:S(2)}, u32[]{:S(2)}) collective-permute-start(f32[8,16]{1,0:T(8,128)S(1)} %get-tuple-element.34), channel_id=1, source_target_pairs={{0,3},{1,2},{2,1},{3,0},{4,7},{5,6},{6,5},{7,4},{8,11},{9,10},{10,... | collective-permute-start | bytes 1544 | tf_op jit(solution)/shard_map/ppermute | solution.py:234

commit v3 on v2

--- a/solution.py
+++ b/solution.py
@@ -123,21 +123,30 @@
         return even[...] + jnp.where(swapped, turned, odd)
 
     prod = total(even_in, acc_in) * total(even_out, acc_out)
-    weights = jnp.concatenate([w_own[...], w_other[...]], axis=1)
-    sums = jnp.dot(weights, prod, precision=lax.Precision.HIGHEST, preferred_element_type=jnp.float32)
-    row = lax.broadcasted_iota(jnp.int32, (16, ROWS), 1)
-    slot = lax.broadcasted_iota(jnp.int32, (16, ROWS), 0)
+    own_prod, other_prod = prod[:256], prod[256:]
+    by_doc = []
+    for doc in range(DOCS):
+        weighted = own_prod * w_own[:, doc : doc + 1] + other_prod * w_other[:, doc : doc + 1]
+        by_doc.append(jnp.sum(weighted, axis=0, keepdims=True))
+    sums = jnp.concatenate(by_doc, axis=0)
+    row = lax.broadcasted_iota(jnp.int32, (64, ROWS), 1)
+    slot = lax.broadcasted_iota(jnp.int32, (64, ROWS), 0)
     sign = 2 * core - 1
     row_z = (z + sign * ((row >> 2) & 7)) & 7
     row_y = (y + sign * ((row >> 5) & 3)) & 3
     row_xh = xh ^ (row >> 7)
     row_query = (row_y * 8 + row_z) * 2 + row_xh
     seq = xl * 2 + core
+    pick = (row_query == (seq ^ (slot >> 4)) * 16 + (slot & 15)).astype(jnp.float32).astype(jnp.bfloat16)
+    top = sums.astype(jnp.bfloat16)
+    rest = sums - top.astype(jnp.float32)
+    middle = rest.astype(jnp.bfloat16)
+    low = (rest - middle.astype(jnp.float32)).astype(jnp.bfloat16)
+    picked = sum(
+        lax.dot_general(part, pick, NT, preferred_element_type=jnp.float32) for part in (low, middle, top)
+    )
     for away in range(4):
-        pick = (row_query == (seq ^ away) * 16 + slot).astype(jnp.float32)
-        outs[away][...] = lax.dot_general(
-            sums, pick, NT, precision=lax.Precision.HIGHEST, preferred_element_type=jnp.float32
-        )
+        outs[away][...] = picked[:, 16 * away : 16 * away + 16]
 
 
 def score(where, tokens, first, second, extra=()):
@@ -177,11 +186,13 @@
     kept_counts,
 ):
     y, z, xh, xl, core = (lax.axis_index(a) for a in AXES)
-    pre_in = (query_inputs[0].astype(jnp.float32) / (input_eigen + damping)[None, :]).astype(jnp.bfloat16)
-    pre_out = (query_grads[0].astype(jnp.float32) / (output_eigen + damping)[None, :]).astype(jnp.bfloat16)
-    pre = jnp.concatenate(
-        [pre_in[:, :HALF_IN], pre_out[:, :HALF_OUT], pre_in[:, HALF_IN:], pre_out[:, HALF_OUT:]], axis=1
-    )
+    def mixed(of_in, of_out):
+        return jnp.concatenate(
+            [of_in[..., :HALF_IN], of_out[..., :HALF_OUT], of_in[..., HALF_IN:], of_out[..., HALF_OUT:]], axis=-1
+        )
+
+    factors, eigen = mixed(query_inputs[0], query_grads[0]), mixed(input_eigen, output_eigen)
+    pre = (factors.astype(jnp.float32) / (eigen + damping)[None, :]).astype(jnp.bfloat16)
     low, high = pre[:4], pre[4:]
     kept = jnp.where(core == 0, low, high)
     came = swap_cores(jnp.where(core == 0, high, low))
@@ -214,10 +225,10 @@
     odd_second = go_round(second[1], second[3], "y")
 
     ids = jnp.where(xl == 0, jnp.stack([chip_ids, mate_ids]), jnp.stack([mate_ids, chip_ids])).reshape(-1)
-    weights = doc_weights(ids, kept_counts[0])
+    weights = doc_weights(ids, kept_counts[0]).T
     seq = xl * 2 + core
-    w_own = lax.dynamic_slice(weights, (0, seq * 256), (DOCS, 256))
-    w_other = lax.dynamic_slice(weights, (0, (seq ^ 1) * 256), (DOCS, 256))
+    w_own = lax.dynamic_slice(weights, (seq * 256, 0), (256, DOCS))
+    w_other = lax.dynamic_slice(weights, ((seq ^ 1) * 256, 0), (256, DOCS))
 
     where = jnp.stack([y, z, xh, xl, core]).astype(jnp.int32)
     tokens = (layer_inputs, x_other, output_grads, g_other)

time: 105 us -> 105 us (level)
  local copies, waits for them, and re-layouts: 8.18 us -> 11.2 us
  other arithmetic: 4.87 us -> 2.14 us
    slice x2 -> x4, local copies, waits for them, and re-layouts: 0.01 us -> 3.03 us  [the longest x2 1.55 us: mixed(): of_out[..., :HALF_OUT]]
    convert_element_type x2 -> x1, other arithmetic: 1.57 us -> 0.03 us  [shards(): (factors.astype(jnp.float32) / (eigen + damping)[None, :]).astype(jnp.bfl...]
    add x2 -> x1, other arithmetic: 1.41 us -> 0.01 us  [shards(): eigen + damping]
where the time goes in v3:
time: 105 us
  starting transfers between devices  52.3 us (50%)
  waiting for transfers between devices  24.9 us (24%)
  Pallas kernels  13.9 us (13%)
  local copies, waits for them, and re-layouts  11.2 us (11%)
  other arithmetic  2.14 us (2%)
    ppermute x24, starting transfers between devices, shift(): return lax.ppermute(value, AXES, pairs)  44.9 us
    ppermute x24, waiting for transfers between devices, shift(): return lax.ppermute(value, AXES, pairs)  22.9 us
    pallas_call x2, Pallas kernels, score(): pl.pallas_call(odd_kernel if last else even_kernel, in_specs=[pl.BlockSpe...  13.9 us
    unnamed x25, local copies, waits for them, and re-layouts  6.21 us
    ppermute x4, starting transfers between devices, swap_cores(): return lax.ppermute(value, 'core', [(0, 1), (1, 0)])  3.68 us
    ppermute x3, starting transfers between devices, shards(): lax.ppermute(pieces[away], ('xl', 'core'), [(i, i ^ away) for i in range(...  2.5 us
  transfers between devices with their start and end apart: 32, of which 12 were waited for; matrix products, arithmetic and copies ran while one was open for 7% of the time, Pallas kernels for 6%

profile of v3, /device:TPU:1, one launch (start us, length us, event | category | flops | bytes accessed | tf_op | source)
XLA Modules:
  0.0 104.7 jit_solution(15187522756313666963)
XLA Ops:
  0.0 3.2 %collective-permute-start.1 = (s32[256]{0:T(256)}, s32[256]{0:T(256)S(1)}, u32[]{:S(2)}, u32[]{:S(2)}) collective-permute-start(s32[256]{0:T(256)} %bitcast.35), channel_id=1, source_target_pairs={{0,1},{1,0},{2,3},{3,2},{4,5},{5,4},{6,7},{7,6},{8,9},{9,8},{10,11... | collective-permute-start | bytes 3080 | tf_op jit(solution)/shard_map/ppermute | solution.py:42
  3.2 0.8 fusion.5
  4.0 0.8 fusion.7
  4.8 0.8 fusion.4
  5.6 0.7 fusion.6
  6.6 0.8 add_select_fusion.1
  8.1 3.8 %collective-permute-start.2 = (bf16[8,4608]{1,0:T(8,128)(2,1)S(1)}, bf16[8,4608]{1,0:T(8,128)(2,1)S(1)}, u32[]{:S(2)}, u32[]{:S(2)}) collective-permute-start(bf16[8,4608]{1,0:T(8,128)(2,1)S(1)} %select_n.58), channel_id=1, source_target_pairs={{0,8},{1,57},{2,10},{3,59},{4,12},{5,61},{6,14},{7,63},{8,16},{9,1... | collective-permute-start | bytes 221192 | tf_op jit(solution)/shard_map/ppermute | solution.py:38
  11.9 1.2 %collective-permute-start.4 = (bf16[8,4608]{1,0:T(8,128)(2,1)S(1)}, bf16[8,4608]{1,0:T(8,128)(2,1)S(1)}, u32[]{:S(2)}, u32[]{:S(2)}) collective-permute-start(bf16[8,4608]{1,0:T(8,128)(2,1)S(1)} %select_n.58), channel_id=1, source_target_pairs={{0,16},{1,49},{2,18},{3,51},{4,20},{5,53},{6,22},{7,55},{8,24},{9,... | collective-permute-start | bytes 221192 | tf_op jit(solution)/shard_map/ppermute | solution.py:38
  13.1 0.7 collective-permute-start.6
  14.4 1.2 %collective-permute-start.3 = (s32[2,256]{1,0:T(2,128)S(1)}, s32[2,256]{1,0:T(2,128)S(1)}, u32[]{:S(2)}, u32[]{:S(2)}) collective-permute-start(s32[2,256]{1,0:T(2,128)S(1)} %add_select_fusion.1), channel_id=1, source_target_pairs={{0,2},{2,0},{1,3},{3,1},{4,6},{6,4},{5,7},{7,5},{8,10},{10,8},{9,1... | collective-permute-start | bytes 6152 | tf_op jit(solution)/shard_map/ppermute | solution.py:205
  15.6 0.7 collective-permute-done.4
  16.4 3.3 %collective-permute-start.5 = (bf16[16,4608]{1,0:T(8,128)(2,1)S(1)}, bf16[16,4608]{1,0:T(8,128)(2,1)S(1)}, u32[]{:S(2)}, u32[]{:S(2)}) collective-permute-start(bf16[16,4608]{1,0:T(8,128)(2,1)S(1)} %pad_maximum_fusion), channel_id=1, source_target_pairs={{0,16},{1,49},{2,18},{3,51},{4,20},{5,53},{6,22},{7,55},{8,24},{9,... | collective-permute-start | bytes 442376 | tf_op jit(solution)/shard_map/ppermute | solution.py:38
  19.7 3.3 %collective-permute-start.7 = (bf16[8,4608]{1,0:T(8,128)(2,1)S(1)}, bf16[8,4608]{1,0:T(8,128)(2,1)S(1)}, u32[]{:S(2)}, u32[]{:S(2)}) collective-permute-start(bf16[8,4608]{1,0:T(8,128)(2,1)S(1)} %collective-permute-done.6), channel_id=1, source_target_pairs={{0,48},{1,17},{2,50},{3,19},{4,52},{5,21},{6,54},{7,23},{8,56},{9,... | collective-permute-start | bytes 221192 | tf_op jit(solution)/shard_map/ppermute | solution.py:38
  23.0 2.6 %collective-permute-done.7 = bf16[8,4608]{1,0:T(8,128)(2,1)S(1)} collective-permute-done((bf16[8,4608]{1,0:T(8,128)(2,1)S(1)}, bf16[8,4608]{1,0:T(8,128)(2,1)S(1)}, u32[]{:S(2)}, u32[]{:S(2)}) %collective-permute-start.7) | collective-permute-done | bytes 73760 | tf_op jit(solution)/shard_map/ppermute | solution.py:38
  25.6 0.8 reshape.87
  26.4 0.8 reshape.88
  27.3 1.0 constant_dynamic-update-slice_fusion.14
  28.3 3.1 %collective-permute-start.25 = (bf16[32,4608]{1,0:T(8,128)(2,1)}, bf16[32,4608]{1,0:T(8,128)(2,1)S(1)}, u32[]{:S(2)}, u32[]{:S(2)}) collective-permute-start(bf16[32,4608]{1,0:T(8,128)(2,1)} %reshape.88), channel_id=1, source_target_pairs={{0,4},{1,5},{2,6},{3,7},{4,0},{5,1},{6,2},{7,3},{8,12},{9,13},{10,... | collective-permute-start | bytes 884744 | tf_op jit(solution)/shard_map/ppermute | solution.py:38
  31.4 2.9 %collective-permute-start.13 = (bf16[32,4608]{1,0:T(8,128)(2,1)}, bf16[32,4608]{1,0:T(8,128)(2,1)S(1)}, u32[]{:S(2)}, u32[]{:S(2)}) collective-permute-start(bf16[32,4608]{1,0:T(8,128)(2,1)} %reshape.87), channel_id=1, source_target_pairs={{0,128},{1,129},{2,130},{3,131},{4,132},{5,133},{6,134},{7,135},{8... | collective-permute-start | bytes 884744 | tf_op jit(solution)/shard_map/ppermute | solution.py:38
  34.7 2.3 %collective-permute-start.11 = (bf16[32,4608]{1,0:T(8,128)(2,1)}, bf16[32,4608]{1,0:T(8,128)(2,1)S(1)}, u32[]{:S(2)}, u32[]{:S(2)}) collective-permute-start(bf16[32,4608]{1,0:T(8,128)(2,1)} %reshape.87), channel_id=1, source_target_pairs={{0,64},{1,193},{2,66},{3,195},{4,68},{5,197},{6,70},{7,199},{8,72}... | collective-permute-start | bytes 884744 | tf_op jit(solution)/shard_map/ppermute | solution.py:38
  36.9 1.2 %collective-permute-start.20 = (bf16[32,4608]{1,0:T(8,128)(2,1)}, bf16[32,4608]{1,0:T(8,128)(2,1)S(1)}, u32[]{:S(2)}, u32[]{:S(2)}) collective-permute-start(bf16[32,4608]{1,0:T(8,128)(2,1)} %reshape.88), channel_id=1, source_target_pairs={{0,2},{1,7},{2,4},{3,1},{4,6},{5,3},{6,0},{7,5},{8,10},{9,15},{10,... | collective-permute-start | bytes 884744 | tf_op jit(solution)/shard_map/ppermute | solution.py:38
  38.2 1.0 constant_dynamic-update-slice_fusion.8
  39.2 1.7 %collective-permute-start.21 = (bf16[32,4608]{1,0:T(8,128)(2,1)}, bf16[32,4608]{1,0:T(8,128)(2,1)S(1)}, u32[]{:S(2)}, u32[]{:S(2)}) collective-permute-start(bf16[32,4608]{1,0:T(8,128)(2,1)} %reshape.88), channel_id=1, source_target_pairs={{0,6},{1,3},{2,0},{3,5},{4,2},{5,7},{6,4},{7,1},{8,14},{9,11},{10,... | collective-permute-start | bytes 884744 | tf_op jit(solution)/shard_map/ppermute | solution.py:38
  41.4 2.8 %collective-permute-start.26 = (bf16[64,4608]{1,0:T(8,128)(2,1)S(1)}, bf16[64,4608]{1,0:T(8,128)(2,1)}, u32[]{:S(2)}, u32[]{:S(2)}) collective-permute-start(bf16[64,4608]{1,0:T(8,128)(2,1)S(1)} %constant_dynamic-update-slice_fusion.13.refs_8_), channel_id=1, source_target_pairs={{0,64},{1,193},{2,66},{3,195},{4,68},{5,197},{6,70},{7,199},{8,72}... | collective-permute-start | bytes 1769480 | tf_op jit(solution)/shard_map/ppermute | solution.py:38
  44.2 4.1 %collective-permute-done.14 = bf16[32,4608]{1,0:T(8,128)(2,1)S(1)} collective-permute-done((bf16[32,4608]{1,0:T(8,128)(2,1)}, bf16[32,4608]{1,0:T(8,128)(2,1)S(1)}, u32[]{:S(2)}, u32[]{:S(2)}) %collective-permute-start.14) | collective-permute-done | bytes 294944 | tf_op jit(solution)/shard_map/ppermute | solution.py:38
  48.4 1.3 %collective-permute-start.15 = (bf16[64,4608]{1,0:T(8,128)(2,1)S(1)}, bf16[64,4608]{1,0:T(8,128)(2,1)}, u32[]{:S(2)}, u32[]{:S(2)}) collective-permute-start(bf16[64,4608]{1,0:T(8,128)(2,1)S(1)} %constant_dynamic-update-slice_fusion.9.refs_5_), channel_id=1, source_target_pairs={{0,2},{1,7},{2,4},{3,1},{4,6},{5,3},{6,0},{7,5},{8,10},{9,15},{10,... | collective-permute-start | bytes 1769480 | tf_op jit(solution)/shard_map/ppermute | solution.py:38
  50.0 1.3 %collective-permute-start.12 = (bf16[64,4608]{1,0:T(8,128)(2,1)S(1)}, bf16[64,4608]{1,0:T(8,128)(2,1)}, u32[]{:S(2)}, u32[]{:S(2)}) collective-permute-start(bf16[64,4608]{1,0:T(8,128)(2,1)S(1)} %constant_dynamic-update-slice_fusion.7.refs_4_), channel_id=1, source_target_pairs={{0,2},{1,7},{2,4},{3,1},{4,6},{5,3},{6,0},{7,5},{8,10},{9,15},{10,... | collective-permute-start | bytes 1769480 | tf_op jit(solution)/shard_map/ppermute | solution.py:38
  51.3 3.9 %collective-permute-done.26.refs_9_ = bf16[64,4608]{1,0:T(8,128)(2,1)} collective-permute-done((bf16[64,4608]{1,0:T(8,128)(2,1)S(1)}, bf16[64,4608]{1,0:T(8,128)(2,1)}, u32[]{:S(2)}, u32[]{:S(2)}) %collective-permute-start.26) | collective-permute-done | bytes 589856 | tf_op jit(solution)/shard_map/ppermute | solution.py:38
  55.2 2.3 %collective-permute-start.27 = (bf16[64,4608]{1,0:T(8,128)(2,1)}, bf16[64,4608]{1,0:T(8,128)(2,1)}, u32[]{:S(2)}, u32[]{:S(2)}) collective-permute-start(bf16[64,4608]{1,0:T(8,128)(2,1)} %collective-permute-done.26.refs_9_), channel_id=1, source_target_pairs={{0,64},{1,193},{2,66},{3,195},{4,68},{5,197},{6,70},{7,199},{8,72}... | collective-permute-start | bytes 1769480 | tf_op jit(solution)/shard_map/ppermute | solution.py:38
  57.6 4.0 %collective-permute-done.22.refs_9_ = bf16[64,4608]{1,0:T(8,128)(2,1)} collective-permute-done((bf16[64,4608]{1,0:T(8,128)(2,1)S(1)}, bf16[64,4608]{1,0:T(8,128)(2,1)}, u32[]{:S(2)}, u32[]{:S(2)}) %collective-permute-start.22) | collective-permute-done | bytes 589856 | tf_op jit(solution)/shard_map/ppermute | solution.py:38
  61.5 2.3 %collective-permute-start.23 = (bf16[64,4608]{1,0:T(8,128)(2,1)}, bf16[64,4608]{1,0:T(8,128)(2,1)}, u32[]{:S(2)}, u32[]{:S(2)}) collective-permute-start(bf16[64,4608]{1,0:T(8,128)(2,1)} %collective-permute-done.22.refs_9_), channel_id=1, source_target_pairs={{0,64},{1,193},{2,66},{3,195},{4,68},{5,197},{6,70},{7,199},{8,72}... | collective-permute-start | bytes 1769480 | tf_op jit(solution)/shard_map/ppermute | solution.py:38
  63.9 1.0 collective-permute-start.18
  64.9 1.5 %collective-permute-start.16 = (bf16[64,4608]{1,0:T(8,128)(2,1)}, bf16[64,4608]{1,0:T(8,128)(2,1)}, u32[]{:S(2)}, u32[]{:S(2)}) collective-permute-start(bf16[64,4608]{1,0:T(8,128)(2,1)} %collective-permute-done.12.refs_4_), channel_id=1, source_target_pairs={{0,2},{1,7},{2,4},{3,1},{4,6},{5,3},{6,0},{7,5},{8,10},{9,15},{10,... | collective-permute-start | bytes 1769480 | tf_op jit(solution)/shard_map/ppermute | solution.py:38
  66.9 1.0 collective-permute-done.27.refs_10_
  67.9 2.3 %collective-permute-start.28 = (bf16[64,4608]{1,0:T(8,128)(2,1)}, bf16[64,4608]{1,0:T(8,128)(2,1)S(1)}, u32[]{:S(2)}, u32[]{:S(2)}) collective-permute-start(bf16[64,4608]{1,0:T(8,128)(2,1)} %collective-permute-done.27.refs_10_), channel_id=1, source_target_pairs={{0,64},{1,193},{2,66},{3,195},{4,68},{5,197},{6,70},{7,199},{8,72}... | collective-permute-start | bytes 1769480 | tf_op jit(solution)/shard_map/ppermute | solution.py:38
  70.2 4.0 %collective-permute-done.23.refs_10_ = bf16[64,4608]{1,0:T(8,128)(2,1)} collective-permute-done((bf16[64,4608]{1,0:T(8,128)(2,1)}, bf16[64,4608]{1,0:T(8,128)(2,1)}, u32[]{:S(2)}, u32[]{:S(2)}) %collective-permute-start.23) | collective-permute-done | bytes 589856 | tf_op jit(solution)/shard_map/ppermute | solution.py:38
  74.2 2.3 %collective-permute-start.24 = (bf16[64,4608]{1,0:T(8,128)(2,1)}, bf16[64,4608]{1,0:T(8,128)(2,1)S(1)}, u32[]{:S(2)}, u32[]{:S(2)}) collective-permute-start(bf16[64,4608]{1,0:T(8,128)(2,1)} %collective-permute-done.23.refs_10_), channel_id=1, source_target_pairs={{0,64},{1,193},{2,66},{3,195},{4,68},{5,197},{6,70},{7,199},{8,72}... | collective-permute-start | bytes 1769480 | tf_op jit(solution)/shard_map/ppermute | solution.py:38
  76.5 1.0 collective-permute-start.19
  77.5 2.1 %collective-permute-done.16.refs_6_ = bf16[64,4608]{1,0:T(8,128)(2,1)} collective-permute-done((bf16[64,4608]{1,0:T(8,128)(2,1)}, bf16[64,4608]{1,0:T(8,128)(2,1)}, u32[]{:S(2)}, u32[]{:S(2)}) %collective-permute-start.16) | collective-permute-done | bytes 589856 | tf_op jit(solution)/shard_map/ppermute | solution.py:38
  79.6 2.1 %collective-permute-start.17 = (bf16[64,4608]{1,0:T(8,128)(2,1)}, bf16[64,4608]{1,0:T(8,128)(2,1)S(1)}, u32[]{:S(2)}, u32[]{:S(2)}) collective-permute-start(bf16[64,4608]{1,0:T(8,128)(2,1)} %collective-permute-done.16.refs_6_), channel_id=1, source_target_pairs={{0,2},{1,7},{2,4},{3,1},{4,6},{5,3},{6,0},{7,5},{8,10},{9,15},{10,... | collective-permute-start | bytes 1769480 | tf_op jit(solution)/shard_map/ppermute | solution.py:38
  81.9 3.1 %copy-done = bf16[256,14336]{1,0:T(8,128)(2,1)S(1)} copy-done((bf16[256,14336]{1,0:T(8,128)(2,1)S(1)}, bf16[256,14336]{1,0:T(8,128)(2,1)}, u32[]{:S(2)}) %copy-start) | copy-done | bytes 7340056
  85.0 1.1 %copy-done.5 = bf16[64,4608]{1,0:T(8,128)(2,1)S(1)} copy-done((bf16[64,4608]{1,0:T(8,128)(2,1)S(1)}, bf16[64,4608]{1,0:T(8,128)(2,1)}, u32[]{:S(2)}) %copy-start.5) | copy-done | bytes 589848
  86.1 6.8 %shard_map.82 = (f32[512,256]{1,0:T(8,128)S(1)}, f32[512,256]{1,0:T(8,128)S(1)}) custom-call(s32[5]{0:T(128)S(1)} %stack.61.where, bf16[256,4096]{1,0:T(8,128)(2,1)S(1)} %copy-done.1, bf16[256,4096]{1,0:T(8,128)(2,1)} %collective-permute-done.9.refs_1_, bf16[256,14336]{1,0:T(8,128)(2,1)S(1)} %copy-done, bf16[256,14336]{1,0:T(8,128)(2,1)} %collective-permute-done.10.refs_3_, ...), custom_call_target="tpu_custom_call" | custom-call | flops 2415919104 | bytes 14155776 | tf_op jit(solution)/shard_map/pallas_call | solution.py:157
  92.9 7.1 %shard_map.83 = (f32[8,16]{1,0:T(8,128)S(1)}, f32[8,16]{1,0:T(8,128)S(1)}, f32[8,16]{1,0:T(8,128)S(1)}, f32[8,16]{1,0:T(8,128)S(1)}) custom-call(s32[5]{0:T(128)S(1)} %stack.61.where, bf16[256,4096]{1,0:T(8,128)(2,1)S(1)} %copy-done.1, bf16[256,4096]{1,0:T(8,128)(2,1)} %collective-permute-done.9.refs_1_, bf16[256,14336]{1,0:T(8,128)(2,1)S(1)} %copy-done, ...), custom_call_target="tpu_custom_call" | custom-call | flops 2415919104 | bytes 14155776 | tf_op jit(solution)/shard_map/pallas_call | solution.py:157
  100.0 0.8 collective-permute-start.29
  100.8 1.7 %collective-permute-start.31 = (f32[8,16]{1,0:T(8,128)S(1)}, f32[8,16]{1,0:T(8,128)S(1)}, u32[]{:S(2)}, u32[]{:S(2)}) collective-permute-start(f32[8,16]{1,0:T(8,128)S(1)} %get-tuple-element.34), channel_id=1, source_target_pairs={{0,3},{1,2},{2,1},{3,0},{4,7},{5,6},{6,5},{7,4},{8,11},{9,10},{10,... | collective-permute-start | bytes 1544 | tf_op jit(solution)/shard_map/ppermute | solution.py:245
  102.5 0.7 collective-permute-done.30
  103.2 0.8 collective-permute-done.31
  (72 shorter events, 4.3 us)
Async XLA Ops:
  0.0 81.9 %copy-start.1 = (bf16[256,4096]{1,0:T(8,128)(2,1)S(1)}, bf16[256,4096]{1,0:T(8,128)(2,1)}, u32[]{:S(2)}) copy-start(bf16[256,4096]{1,0:T(8,128)(2,1)} %refs_0_.1) | copy-start | bytes 6291460
  0.0 81.6 %copy-start.6 = (s32[1,8]{1,0:T(1,128)S(1)}, s32[1,8]{1,0:T(1,128)}, u32[]{:S(2)}) copy-start(s32[1,8]{1,0:T(1,128)} %param.15) | copy-start | bytes 100
  0.0 6.6 %collective-permute-start.1 = (s32[256]{0:T(256)}, s32[256]{0:T(256)S(1)}, u32[]{:S(2)}, u32[]{:S(2)}) collective-permute-start(s32[256]{0:T(256)} %bitcast.35), channel_id=1, source_target_pairs={{0,1},{1,0},{2,3},{3,2},{4,5},{5,4},{6,7},{7,6},{8,9},{9,8},{10,11... | collective-permute-start | bytes 3080 | tf_op jit(solution)/shard_map/ppermute | solution.py:42
  6.4 1.3 %collective-permute-start = (bf16[4,4608]{1,0:T(4,128)(2,1)S(1)}, bf16[4,4608]{1,0:T(4,128)(2,1)S(1)}, u32[]{:S(2)}, u32[]{:S(2)}) collective-permute-start(bf16[4,4608]{1,0:T(4,128)(2,1)S(1)} %get-tuple-element.40), channel_id=1, source_target_pairs={{0,1},{1,0},{2,3},{3,2},{4,5},{5,4},{6,7},{7,6},{8,9},{9,8},{10,11... | collective-permute-start | bytes 110600 | tf_op jit(solution)/shard_map/ppermute | solution.py:42
  7.9 19.4 %collective-permute-start.10 = (bf16[256,14336]{1,0:T(8,128)(2,1)}, bf16[256,14336]{1,0:T(8,128)(2,1)}, u32[]{:S(2)}, u32[]{:S(2)}) collective-permute-start(bf16[256,14336]{1,0:T(8,128)(2,1)} %refs_2_.1), channel_id=1, source_target_pairs={{0,1},{1,0},{2,3},{3,2},{4,5},{5,4},{6,7},{7,6},{8,9},{9,8},{10,11... | collective-permute-start | bytes 22020104 | tf_op jit(solution)/shard_map/ppermute | solution.py:42
  8.1 6.3 %collective-permute-start.2 = (bf16[8,4608]{1,0:T(8,128)(2,1)S(1)}, bf16[8,4608]{1,0:T(8,128)(2,1)S(1)}, u32[]{:S(2)}, u32[]{:S(2)}) collective-permute-start(bf16[8,4608]{1,0:T(8,128)(2,1)S(1)} %select_n.58), channel_id=1, source_target_pairs={{0,8},{1,57},{2,10},{3,59},{4,12},{5,61},{6,14},{7,63},{8,16},{9,1... | collective-permute-start | bytes 221192 | tf_op jit(solution)/shard_map/ppermute | solution.py:38
  11.9 4.4 %collective-permute-start.4 = (bf16[8,4608]{1,0:T(8,128)(2,1)S(1)}, bf16[8,4608]{1,0:T(8,128)(2,1)S(1)}, u32[]{:S(2)}, u32[]{:S(2)}) collective-permute-start(bf16[8,4608]{1,0:T(8,128)(2,1)S(1)} %select_n.58), channel_id=1, source_target_pairs={{0,16},{1,49},{2,18},{3,51},{4,20},{5,53},{6,22},{7,55},{8,24},{9,... | collective-permute-start | bytes 221192 | tf_op jit(solution)/shard_map/ppermute | solution.py:38
  13.1 6.5 %collective-permute-start.6 = (bf16[8,4608]{1,0:T(8,128)(2,1)S(1)}, bf16[8,4608]{1,0:T(8,128)(2,1)S(1)}, u32[]{:S(2)}, u32[]{:S(2)}) collective-permute-start(bf16[8,4608]{1,0:T(8,128)(2,1)S(1)} %select_n.58), channel_id=1, source_target_pairs={{0,56},{1,9},{2,58},{3,11},{4,60},{5,13},{6,62},{7,15},{8,0},{9,17... | collective-permute-start | bytes 221192 | tf_op jit(solution)/shard_map/ppermute | solution.py:38
  13.9 11.7 %collective-permute-start.8 = (bf16[8,4608]{1,0:T(8,128)(2,1)S(1)}, bf16[8,4608]{1,0:T(8,128)(2,1)S(1)}, u32[]{:S(2)}, u32[]{:S(2)}) collective-permute-start(bf16[8,4608]{1,0:T(8,128)(2,1)S(1)} %select_n.58), channel_id=1, source_target_pairs={{0,48},{1,17},{2,50},{3,19},{4,52},{5,21},{6,54},{7,23},{8,56},{9,... | collective-permute-start | bytes 221192 | tf_op jit(solution)/shard_map/ppermute | solution.py:38
  14.4 5.2 %collective-permute-start.3 = (s32[2,256]{1,0:T(2,128)S(1)}, s32[2,256]{1,0:T(2,128)S(1)}, u32[]{:S(2)}, u32[]{:S(2)}) collective-permute-start(s32[2,256]{1,0:T(2,128)S(1)} %add_select_fusion.1), channel_id=1, source_target_pairs={{0,2},{2,0},{1,3},{3,1},{4,6},{6,4},{5,7},{7,5},{8,10},{10,8},{9,1... | collective-permute-start | bytes 6152 | tf_op jit(solution)/shard_map/ppermute | solution.py:205
  16.4 6.6 %collective-permute-start.5 = (bf16[16,4608]{1,0:T(8,128)(2,1)S(1)}, bf16[16,4608]{1,0:T(8,128)(2,1)S(1)}, u32[]{:S(2)}, u32[]{:S(2)}) collective-permute-start(bf16[16,4608]{1,0:T(8,128)(2,1)S(1)} %pad_maximum_fusion), channel_id=1, source_target_pairs={{0,16},{1,49},{2,18},{3,51},{4,20},{5,53},{6,22},{7,55},{8,24},{9,... | collective-permute-start | bytes 442376 | tf_op jit(solution)/shard_map/ppermute | solution.py:38
  19.6 7.7 %collective-permute-start.9 = (bf16[256,4096]{1,0:T(8,128)(2,1)}, bf16[256,4096]{1,0:T(8,128)(2,1)}, u32[]{:S(2)}, u32[]{:S(2)}) collective-permute-start(bf16[256,4096]{1,0:T(8,128)(2,1)} %refs_0_.1), channel_id=1, source_target_pairs={{0,1},{1,0},{2,3},{3,2},{4,5},{5,4},{6,7},{7,6},{8,9},{9,8},{10,11... | collective-permute-start | bytes 6291464 | tf_op jit(solution)/shard_map/ppermute | solution.py:42
  19.7 5.9 %collective-permute-start.7 = (bf16[8,4608]{1,0:T(8,128)(2,1)S(1)}, bf16[8,4608]{1,0:T(8,128)(2,1)S(1)}, u32[]{:S(2)}, u32[]{:S(2)}) collective-permute-start(bf16[8,4608]{1,0:T(8,128)(2,1)S(1)} %collective-permute-done.6), channel_id=1, source_target_pairs={{0,48},{1,17},{2,50},{3,19},{4,52},{5,21},{6,54},{7,23},{8,56},{9,... | collective-permute-start | bytes 221192 | tf_op jit(solution)/shard_map/ppermute | solution.py:38
  28.3 10.9 %collective-permute-start.25 = (bf16[32,4608]{1,0:T(8,128)(2,1)}, bf16[32,4608]{1,0:T(8,128)(2,1)S(1)}, u32[]{:S(2)}, u32[]{:S(2)}) collective-permute-start(bf16[32,4608]{1,0:T(8,128)(2,1)} %reshape.88), channel_id=1, source_target_pairs={{0,4},{1,5},{2,6},{3,7},{4,0},{5,1},{6,2},{7,3},{8,12},{9,13},{10,... | collective-permute-start | bytes 884744 | tf_op jit(solution)/shard_map/ppermute | solution.py:38
  31.4 10.0 %collective-permute-start.13 = (bf16[32,4608]{1,0:T(8,128)(2,1)}, bf16[32,4608]{1,0:T(8,128)(2,1)S(1)}, u32[]{:S(2)}, u32[]{:S(2)}) collective-permute-start(bf16[32,4608]{1,0:T(8,128)(2,1)} %reshape.87), channel_id=1, source_target_pairs={{0,128},{1,129},{2,130},{3,131},{4,132},{5,133},{6,134},{7,135},{8... | collective-permute-start | bytes 884744 | tf_op jit(solution)/shard_map/ppermute | solution.py:38
  34.3 14.1 %collective-permute-start.14 = (bf16[32,4608]{1,0:T(8,128)(2,1)}, bf16[32,4608]{1,0:T(8,128)(2,1)S(1)}, u32[]{:S(2)}, u32[]{:S(2)}) collective-permute-start(bf16[32,4608]{1,0:T(8,128)(2,1)} %reshape.87), channel_id=1, source_target_pairs={{0,192},{1,65},{2,194},{3,67},{4,196},{5,69},{6,198},{7,71},{8,200... | collective-permute-start | bytes 884744 | tf_op jit(solution)/shard_map/ppermute | solution.py:38
  34.7 15.3 %collective-permute-start.11 = (bf16[32,4608]{1,0:T(8,128)(2,1)}, bf16[32,4608]{1,0:T(8,128)(2,1)S(1)}, u32[]{:S(2)}, u32[]{:S(2)}) collective-permute-start(bf16[32,4608]{1,0:T(8,128)(2,1)} %reshape.87), channel_id=1, source_target_pairs={{0,64},{1,193},{2,66},{3,195},{4,68},{5,197},{6,70},{7,199},{8,72}... | collective-permute-start | bytes 884744 | tf_op jit(solution)/shard_map/ppermute | solution.py:38
  36.9 12.7 %collective-permute-start.20 = (bf16[32,4608]{1,0:T(8,128)(2,1)}, bf16[32,4608]{1,0:T(8,128)(2,1)S(1)}, u32[]{:S(2)}, u32[]{:S(2)}) collective-permute-start(bf16[32,4608]{1,0:T(8,128)(2,1)} %reshape.88), channel_id=1, source_target_pairs={{0,2},{1,7},{2,4},{3,1},{4,6},{5,3},{6,0},{7,5},{8,10},{9,15},{10,... | collective-permute-start | bytes 884744 | tf_op jit(solution)/shard_map/ppermute | solution.py:38
  39.2 10.5 %collective-permute-start.21 = (bf16[32,4608]{1,0:T(8,128)(2,1)}, bf16[32,4608]{1,0:T(8,128)(2,1)S(1)}, u32[]{:S(2)}, u32[]{:S(2)}) collective-permute-start(bf16[32,4608]{1,0:T(8,128)(2,1)} %reshape.88), channel_id=1, source_target_pairs={{0,6},{1,3},{2,0},{3,5},{4,2},{5,7},{6,4},{7,1},{8,14},{9,11},{10,... | collective-permute-start | bytes 884744 | tf_op jit(solution)/shard_map/ppermute | solution.py:38
  41.4 13.8 %collective-permute-start.26 = (bf16[64,4608]{1,0:T(8,128)(2,1)S(1)}, bf16[64,4608]{1,0:T(8,128)(2,1)}, u32[]{:S(2)}, u32[]{:S(2)}) collective-permute-start(bf16[64,4608]{1,0:T(8,128)(2,1)S(1)} %constant_dynamic-update-slice_fusion.13.refs_8_), channel_id=1, source_target_pairs={{0,64},{1,193},{2,66},{3,195},{4,68},{5,197},{6,70},{7,199},{8,72}... | collective-permute-start | bytes 1769480 | tf_op jit(solution)/shard_map/ppermute | solution.py:38
  48.3 16.5 %copy-start.4 = (bf16[64,4608]{1,0:T(8,128)(2,1)}, bf16[64,4608]{1,0:T(8,128)(2,1)S(1)}, u32[]{:S(2)}) copy-start(bf16[64,4608]{1,0:T(8,128)(2,1)S(1)} %constant_dynamic-update-slice_fusion.9.refs_5_) | copy-start | bytes 1769476
  48.4 15.5 %collective-permute-start.15 = (bf16[64,4608]{1,0:T(8,128)(2,1)S(1)}, bf16[64,4608]{1,0:T(8,128)(2,1)}, u32[]{:S(2)}, u32[]{:S(2)}) collective-permute-start(bf16[64,4608]{1,0:T(8,128)(2,1)S(1)} %constant_dynamic-update-slice_fusion.9.refs_5_), channel_id=1, source_target_pairs={{0,2},{1,7},{2,4},{3,1},{4,6},{5,3},{6,0},{7,5},{8,10},{9,15},{10,... | collective-permute-start | bytes 1769480 | tf_op jit(solution)/shard_map/ppermute | solution.py:38
  49.8 15.1 %copy-start.2 = (bf16[64,4608]{1,0:T(8,128)(2,1)}, bf16[64,4608]{1,0:T(8,128)(2,1)S(1)}, u32[]{:S(2)}) copy-start(bf16[64,4608]{1,0:T(8,128)(2,1)S(1)} %constant_dynamic-update-slice_fusion.11.refs_8_) | copy-start | bytes 1769476
  49.8 11.8 %collective-permute-start.22 = (bf16[64,4608]{1,0:T(8,128)(2,1)S(1)}, bf16[64,4608]{1,0:T(8,128)(2,1)}, u32[]{:S(2)}, u32[]{:S(2)}) collective-permute-start(bf16[64,4608]{1,0:T(8,128)(2,1)S(1)} %constant_dynamic-update-slice_fusion.11.refs_8_), channel_id=1, source_target_pairs={{0,64},{1,193},{2,66},{3,195},{4,68},{5,197},{6,70},{7,199},{8,72}... | collective-permute-start | bytes 1769480 | tf_op jit(solution)/shard_map/ppermute | solution.py:38
  50.0 14.9 %collective-permute-start.12 = (bf16[64,4608]{1,0:T(8,128)(2,1)S(1)}, bf16[64,4608]{1,0:T(8,128)(2,1)}, u32[]{:S(2)}, u32[]{:S(2)}) collective-permute-start(bf16[64,4608]{1,0:T(8,128)(2,1)S(1)} %constant_dynamic-update-slice_fusion.7.refs_4_), channel_id=1, source_target_pairs={{0,2},{1,7},{2,4},{3,1},{4,6},{5,3},{6,0},{7,5},{8,10},{9,15},{10,... | collective-permute-start | bytes 1769480 | tf_op jit(solution)/shard_map/ppermute | solution.py:38
  55.2 12.6 %collective-permute-start.27 = (bf16[64,4608]{1,0:T(8,128)(2,1)}, bf16[64,4608]{1,0:T(8,128)(2,1)}, u32[]{:S(2)}, u32[]{:S(2)}) collective-permute-start(bf16[64,4608]{1,0:T(8,128)(2,1)} %collective-permute-done.26.refs_9_), channel_id=1, source_target_pairs={{0,64},{1,193},{2,66},{3,195},{4,68},{5,197},{6,70},{7,199},{8,72}... | collective-permute-start | bytes 1769480 | tf_op jit(solution)/shard_map/ppermute | solution.py:38
  61.5 12.6 %collective-permute-start.23 = (bf16[64,4608]{1,0:T(8,128)(2,1)}, bf16[64,4608]{1,0:T(8,128)(2,1)}, u32[]{:S(2)}, u32[]{:S(2)}) collective-permute-start(bf16[64,4608]{1,0:T(8,128)(2,1)} %collective-permute-done.22.refs_9_), channel_id=1, source_target_pairs={{0,64},{1,193},{2,66},{3,195},{4,68},{5,197},{6,70},{7,199},{8,72}... | collective-permute-start | bytes 1769480 | tf_op jit(solution)/shard_map/ppermute | solution.py:38
  63.9 12.6 %collective-permute-start.18 = (bf16[64,4608]{1,0:T(8,128)(2,1)}, bf16[64,4608]{1,0:T(8,128)(2,1)}, u32[]{:S(2)}, u32[]{:S(2)}) collective-permute-start(bf16[64,4608]{1,0:T(8,128)(2,1)} %collective-permute-done.15.refs_5_), channel_id=1, source_target_pairs={{0,2},{1,7},{2,4},{3,1},{4,6},{5,3},{6,0},{7,5},{8,10},{9,15},{10,... | collective-permute-start | bytes 1769480 | tf_op jit(solution)/shard_map/ppermute | solution.py:38
  64.9 14.7 %collective-permute-start.16 = (bf16[64,4608]{1,0:T(8,128)(2,1)}, bf16[64,4608]{1,0:T(8,128)(2,1)}, u32[]{:S(2)}, u32[]{:S(2)}) collective-permute-start(bf16[64,4608]{1,0:T(8,128)(2,1)} %collective-permute-done.12.refs_4_), channel_id=1, source_target_pairs={{0,2},{1,7},{2,4},{3,1},{4,6},{5,3},{6,0},{7,5},{8,10},{9,15},{10,... | collective-permute-start | bytes 1769480 | tf_op jit(solution)/shard_map/ppermute | solution.py:38
  67.9 14.0 %collective-permute-start.28 = (bf16[64,4608]{1,0:T(8,128)(2,1)}, bf16[64,4608]{1,0:T(8,128)(2,1)S(1)}, u32[]{:S(2)}, u32[]{:S(2)}) collective-permute-start(bf16[64,4608]{1,0:T(8,128)(2,1)} %collective-permute-done.27.refs_10_), channel_id=1, source_target_pairs={{0,64},{1,193},{2,66},{3,195},{4,68},{5,197},{6,70},{7,199},{8,72}... | collective-permute-start | bytes 1769480 | tf_op jit(solution)/shard_map/ppermute | solution.py:38
  74.2 18.6 %collective-permute-start.24 = (bf16[64,4608]{1,0:T(8,128)(2,1)}, bf16[64,4608]{1,0:T(8,128)(2,1)S(1)}, u32[]{:S(2)}, u32[]{:S(2)}) collective-permute-start(bf16[64,4608]{1,0:T(8,128)(2,1)} %collective-permute-done.23.refs_10_), channel_id=1, source_target_pairs={{0,64},{1,193},{2,66},{3,195},{4,68},{5,197},{6,70},{7,199},{8,72}... | collective-permute-start | bytes 1769480 | tf_op jit(solution)/shard_map/ppermute | solution.py:38
  76.5 16.3 %collective-permute-start.19 = (bf16[64,4608]{1,0:T(8,128)(2,1)}, bf16[64,4608]{1,0:T(8,128)(2,1)S(1)}, u32[]{:S(2)}, u32[]{:S(2)}) collective-permute-start(bf16[64,4608]{1,0:T(8,128)(2,1)} %collective-permute-done.18.refs_7_), channel_id=1, source_target_pairs={{0,2},{1,7},{2,4},{3,1},{4,6},{5,3},{6,0},{7,5},{8,10},{9,15},{10,... | collective-permute-start | bytes 1769480 | tf_op jit(solution)/shard_map/ppermute | solution.py:38
  79.6 13.3 %collective-permute-start.17 = (bf16[64,4608]{1,0:T(8,128)(2,1)}, bf16[64,4608]{1,0:T(8,128)(2,1)S(1)}, u32[]{:S(2)}, u32[]{:S(2)}) collective-permute-start(bf16[64,4608]{1,0:T(8,128)(2,1)} %collective-permute-done.16.refs_6_), channel_id=1, source_target_pairs={{0,2},{1,7},{2,4},{3,1},{4,6},{5,3},{6,0},{7,5},{8,10},{9,15},{10,... | collective-permute-start | bytes 1769480 | tf_op jit(solution)/shard_map/ppermute | solution.py:38
  81.9 3.1 %copy-start = (bf16[256,14336]{1,0:T(8,128)(2,1)S(1)}, bf16[256,14336]{1,0:T(8,128)(2,1)}, u32[]{:S(2)}) copy-start(bf16[256,14336]{1,0:T(8,128)(2,1)} %refs_2_.1) | copy-start | bytes 22020100
  85.0 1.1 %copy-start.5 = (bf16[64,4608]{1,0:T(8,128)(2,1)S(1)}, bf16[64,4608]{1,0:T(8,128)(2,1)}, u32[]{:S(2)}) copy-start(bf16[64,4608]{1,0:T(8,128)(2,1)} %copy-done.4) | copy-start | bytes 1769476
  86.1 6.8 %copy-start.3 = (bf16[64,4608]{1,0:T(8,128)(2,1)S(1)}, bf16[64,4608]{1,0:T(8,128)(2,1)}, u32[]{:S(2)}) copy-start(bf16[64,4608]{1,0:T(8,128)(2,1)} %copy-done.2) | copy-start | bytes 1769476
  100.0 2.5 %collective-permute-start.29 = (f32[8,16]{1,0:T(8,128)S(1)}, f32[8,16]{1,0:T(8,128)S(1)}, u32[]{:S(2)}, u32[]{:S(2)}) collective-permute-start(f32[8,16]{1,0:T(8,128)S(1)} %get-tuple-element.32), channel_id=1, source_target_pairs={{0,1},{1,0},{2,3},{3,2},{4,5},{5,4},{6,7},{7,6},{8,9},{9,8},{10,11... | collective-permute-start | bytes 1544 | tf_op jit(solution)/shard_map/ppermute | solution.py:245
  100.8 2.5 %collective-permute-start.30 = (f32[8,16]{1,0:T(8,128)S(1)}, f32[8,16]{1,0:T(8,128)S(1)}, u32[]{:S(2)}, u32[]{:S(2)}) collective-permute-start(f32[8,16]{1,0:T(8,128)S(1)} %get-tuple-element.33), channel_id=1, source_target_pairs={{0,2},{1,3},{2,0},{3,1},{4,6},{5,7},{6,4},{7,5},{8,10},{9,11},{10,... | collective-permute-start | bytes 1544 | tf_op jit(solution)/shard_map/ppermute | solution.py:245
  100.8 3.3 %collective-permute-start.31 = (f32[8,16]{1,0:T(8,128)S(1)}, f32[8,16]{1,0:T(8,128)S(1)}, u32[]{:S(2)}, u32[]{:S(2)}) collective-permute-start(f32[8,16]{1,0:T(8,128)S(1)} %get-tuple-element.34), channel_id=1, source_target_pairs={{0,3},{1,2},{2,1},{3,0},{4,7},{5,6},{6,5},{7,4},{8,11},{9,10},{10,... | collective-permute-start | bytes 1544 | tf_op jit(solution)/shard_map/ppermute | solution.py:245

commit v4 on v3

--- a/solution.py
+++ b/solution.py
@@ -16,8 +16,10 @@
 damping = 0.1
 
 ROWS = 256
-HALF_IN, HALF_OUT = 512, 1792
-CHUNK = HALF_IN + HALF_OUT
+HALF_IN, OUT = 512, 3584
+WIDTHS = 1664, 1920
+STARTS = 0, WIDTHS[0]
+CHUNKS = HALF_IN + WIDTHS[0], HALF_IN + WIDTHS[1]
 NT = (((1,), (1,)), ((), ()))
 LIMIT = 32 * 1024 * 1024
 
@@ -69,22 +71,24 @@
 def project(odd, where, tokens, first, second, acc_in, acc_out, xs, gs, ws, sems):
     def copies(piece):
         half, quarter = divmod(piece, 2)
-        at = (where[3] ^ odd) * 4 + quarter * 2 + half
-        of_x = pl.ds(pl.multiple_of(at * HALF_IN, 128), HALF_IN)
-        of_g = pl.ds(pl.multiple_of(at * HALF_OUT, 128), HALF_OUT)
-        of_w = pl.ds(quarter * CHUNK, CHUNK)
+        at = (where[3] ^ odd) * 2 + quarter
+        width, chunk = WIDTHS[half], CHUNKS[half]
+        of_x = pl.ds(pl.multiple_of(at * 2 * HALF_IN + half * HALF_IN, 128), HALF_IN)
+        of_g = pl.ds(pl.multiple_of(at * OUT + STARTS[half], 128), width)
+        of_w = pl.ds(quarter * chunk, chunk)
+        to_g, to_w = pl.ds(0, width), pl.ds(0, chunk)
         x_own, x_other, g_own, g_other = tokens
         moves = [
             (x_own.at[:, of_x], xs.at[piece, pl.ds(0, 256)]),
             (x_other.at[:, of_x], xs.at[piece, pl.ds(256, 256)]),
-            (g_own.at[:, of_g], gs.at[piece, pl.ds(0, 256)]),
-            (g_other.at[:, of_g], gs.at[piece, pl.ds(256, 256)]),
+            (g_own.at[:, of_g], gs.at[piece, pl.ds(0, 256), to_g]),
+            (g_other.at[:, of_g], gs.at[piece, pl.ds(256, 256), to_g]),
         ]
         if half == 0:
-            moves += [(v.at[:, of_w], ws.at[piece, pl.ds(64 * i, 64)]) for i, v in enumerate(first)]
+            moves += [(v.at[:, of_w], ws.at[piece, pl.ds(64 * i, 64), to_w]) for i, v in enumerate(first)]
         else:
             moves += [
-                (second[y].at[pl.ds(32 * k, 32), of_w], ws.at[piece, pl.ds(128 * k + 32 * y, 32)])
+                (second[y].at[pl.ds(32 * k, 32), of_w], ws.at[piece, pl.ds(128 * k + 32 * y, 32), to_w])
                 for k in range(2)
                 for y in range(4)
             ]
@@ -97,7 +101,10 @@
         for copy in copies(piece):
             copy.wait()
         p = lax.dot_general(xs[piece], ws[piece, :, :HALF_IN], NT, preferred_element_type=jnp.float32)
-        q = lax.dot_general(gs[piece], ws[piece, :, HALF_IN:], NT, preferred_element_type=jnp.float32)
+        width, chunk = WIDTHS[piece // 2], CHUNKS[piece // 2]
+        q = lax.dot_general(
+            gs[piece, :, :width], ws[piece, :, HALF_IN:chunk], NT, preferred_element_type=jnp.float32
+        )
         if piece == 0:
             acc_in[...] = p
             acc_out[...] = q
@@ -164,13 +171,13 @@
         scratch_shapes=([pltpu.VMEM(proj, jnp.float32)] * 2 if last else [])
         + [
             pltpu.VMEM((4, 512, HALF_IN), jnp.bfloat16),
-            pltpu.VMEM((4, 512, HALF_OUT), jnp.bfloat16),
-            pltpu.VMEM((4, ROWS, CHUNK), jnp.bfloat16),
+            pltpu.VMEM((4, 512, max(WIDTHS)), jnp.bfloat16),
+            pltpu.VMEM((4, ROWS, max(CHUNKS)), jnp.bfloat16),
             pltpu.SemaphoreType.DMA((4, 12)),
         ],
         compiler_params=pltpu.CompilerParams(vmem_limit_bytes=LIMIT),
         cost_estimate=pl.CostEstimate(
-            flops=2 * 512 * ROWS * 4 * CHUNK, bytes_accessed=2 * 768 * 4 * CHUNK, transcendentals=0
+            flops=2 * 512 * ROWS * 2 * sum(CHUNKS), bytes_accessed=2 * 768 * 2 * sum(CHUNKS), transcendentals=0
         ),
     )(where, *tokens, *first, *second, *extra)
 
@@ -188,7 +195,7 @@
     y, z, xh, xl, core = (lax.axis_index(a) for a in AXES)
     def mixed(of_in, of_out):
         return jnp.concatenate(
-            [of_in[..., :HALF_IN], of_out[..., :HALF_OUT], of_in[..., HALF_IN:], of_out[..., HALF_OUT:]], axis=-1
+            [of_in[..., :HALF_IN], of_out[..., : WIDTHS[0]], of_in[..., HALF_IN:], of_out[..., WIDTHS[0] :]], axis=-1
         )
 
     factors, eigen = mixed(query_inputs[0], query_grads[0]), mixed(input_eigen, output_eigen)
@@ -198,7 +205,7 @@
     came = swap_cores(jnp.where(core == 0, high, low))
     ids_came = swap_cores(doc_index[0])
     both = jnp.where(core == 0, jnp.stack([kept, came], axis=1), jnp.stack([came, kept], axis=1))
-    own = both.reshape(8, 2 * CHUNK)
+    own = both.reshape(8, sum(CHUNKS))
 
     chip_ids = jnp.where(core == 0, jnp.stack([doc_index[0], ids_came]), jnp.stack([ids_came, doc_index[0]]))
     own, output_grads, chip_ids = lax.optimization_barrier((own, output_grads, chip_ids))
@@ -208,7 +215,7 @@
     first_came, layer_inputs, mate_ids = lax.optimization_barrier((first_came, layer_inputs, mate_ids))
     x_other = swap_cores(layer_inputs)
 
-    halves = [slots[:, :CHUNK].reshape(32, 2 * CHUNK), slots[:, CHUNK:].reshape(32, 2 * CHUNK)]
+    halves = [slots[:, : CHUNKS[0]].reshape(32, 2 * CHUNKS[0]), slots[:, CHUNKS[0] :].reshape(32, 2 * CHUNKS[1])]
     halves, x_other, g_other = lax.optimization_barrier((halves, x_other, g_other))
 
     first, second = direct(halves[0], "y"), direct(halves[1], "x")

time: 105 us -> 113 us (1.076)
  waiting for transfers between devices: 24.9 us -> 34.7 us
  starting transfers between devices: 52.3 us -> 45.6 us
  local copies, waits for them, and re-layouts: 11.2 us -> 14.4 us
    ppermute x24, waiting for transfers between devices: 22.9 us -> 32.9 us  [shift(): return lax.ppermute(value, AXES, pairs)]
    ppermute x24, starting transfers between devices: 44.9 us -> 35.9 us  [shift(): return lax.ppermute(value, AXES, pairs)]
    ppermute x3, starting transfers between devices: 2.5 us -> 4.77 us  [shards(): lax.ppermute(pieces[away], ('xl', 'core'), [(i, i ^ away) for i in range(...]
    concatenate x4, local copies, waits for them, and re-layouts: 0.08 us -> 1.49 us  [go_round(): pair = [jnp.concatenate([one, two], axis=0)]]
    slice x3 -> x6, local copies, waits for them, and re-layouts: 1.59 us -> 2.95 us  [the longest x2 1.46 us: mixed(): of_out[..., WIDTHS[0]:]]
    unnamed x25 -> x17, local copies, waits for them, and re-layouts: 6.21 us -> 6.59 us
  transfers between devices with their start and end apart: 32 -> 32, of which waited for: 12 -> 13; matrix products, arithmetic and copies ran while one was open for 7% -> 10% of each run, Pallas kernels for 6% -> 6%
where the time goes in v4:
time: 113 us; the launch traced here: 112 us
  starting transfers between devices  45.6 us (40%)
  waiting for transfers between devices  34.7 us (31%)
  Pallas kernels  15 us (13%)
  local copies, waits for them, and re-layouts  14.4 us (13%)
  other arithmetic  2.13 us (2%)
    ppermute x24, starting transfers between devices, shift(): return lax.ppermute(value, AXES, pairs)  35.9 us
    ppermute x24, waiting for transfers between devices, shift(): return lax.ppermute(value, AXES, pairs)  32.9 us
    pallas_call x2, Pallas kernels, score(): pl.pallas_call(odd_kernel if last else even_kernel, in_specs=[pl.BlockSpe...  15 us
    unnamed x17, local copies, waits for them, and re-layouts  6.59 us
    ppermute x3, starting transfers between devices, shards(): lax.ppermute(pieces[away], ('xl', 'core'), [(i, i ^ away) for i in range(...  4.77 us
    ppermute x4, starting transfers between devices, swap_cores(): return lax.ppermute(value, 'core', [(0, 1), (1, 0)])  3.74 us
  transfers between devices with their start and end apart: 32, of which 13 were waited for; matrix products, arithmetic and copies ran while one was open for 10% of the time, Pallas kernels for 6%

profile of v4, /device:TPU:1, one launch (start us, length us, event | category | flops | bytes accessed | tf_op | source)
XLA Modules:
  0.0 112.1 jit_solution(15382347981428312153)
XLA Ops:
  0.0 3.2 %collective-permute-start.1 = (s32[256]{0:T(256)}, s32[256]{0:T(256)S(1)}, u32[]{:S(2)}, u32[]{:S(2)}) collective-permute-start(s32[256]{0:T(256)} %bitcast.36), channel_id=1, source_target_pairs={{0,1},{1,0},{2,3},{3,2},{4,5},{5,4},{6,7},{7,6},{8,9},{9,8},{10,11... | collective-permute-start | bytes 3080 | tf_op jit(solution)/shard_map/ppermute | solution.py:44
  4.7 0.8 slice.51
  5.4 0.7 slice.49
  6.2 0.8 fusion.4
  6.9 0.7 fusion.3
  8.0 0.8 add_select_fusion.1
  9.5 3.8 %collective-permute-start.2 = (bf16[8,4608]{1,0:T(8,128)(2,1)S(1)}, bf16[8,4608]{1,0:T(8,128)(2,1)S(1)}, u32[]{:S(2)}, u32[]{:S(2)}) collective-permute-start(bf16[8,4608]{1,0:T(8,128)(2,1)S(1)} %select_n.58), channel_id=1, source_target_pairs={{0,8},{1,57},{2,10},{3,59},{4,12},{5,61},{6,14},{7,63},{8,16},{9,1... | collective-permute-start | bytes 221192 | tf_op jit(solution)/shard_map/ppermute | solution.py:40
  13.3 1.2 %collective-permute-start.4 = (bf16[8,4608]{1,0:T(8,128)(2,1)S(1)}, bf16[8,4608]{1,0:T(8,128)(2,1)S(1)}, u32[]{:S(2)}, u32[]{:S(2)}) collective-permute-start(bf16[8,4608]{1,0:T(8,128)(2,1)S(1)} %select_n.58), channel_id=1, source_target_pairs={{0,16},{1,49},{2,18},{3,51},{4,20},{5,53},{6,22},{7,55},{8,24},{9,... | collective-permute-start | bytes 221192 | tf_op jit(solution)/shard_map/ppermute | solution.py:40
  14.5 0.7 collective-permute-start.6
  15.8 1.2 %collective-permute-start.3 = (s32[2,256]{1,0:T(2,128)S(1)}, s32[2,256]{1,0:T(2,128)S(1)}, u32[]{:S(2)}, u32[]{:S(2)}) collective-permute-start(s32[2,256]{1,0:T(2,128)S(1)} %add_select_fusion.1), channel_id=1, source_target_pairs={{0,2},{2,0},{1,3},{3,1},{4,6},{6,4},{5,7},{7,5},{8,10},{10,8},{9,1... | collective-permute-start | bytes 6152 | tf_op jit(solution)/shard_map/ppermute | solution.py:212
  17.0 0.7 collective-permute-done.4
  17.7 3.3 %collective-permute-start.5 = (bf16[16,4608]{1,0:T(8,128)(2,1)S(1)}, bf16[16,4608]{1,0:T(8,128)(2,1)S(1)}, u32[]{:S(2)}, u32[]{:S(2)}) collective-permute-start(bf16[16,4608]{1,0:T(8,128)(2,1)S(1)} %pad_maximum_fusion), channel_id=1, source_target_pairs={{0,16},{1,49},{2,18},{3,51},{4,20},{5,53},{6,22},{7,55},{8,24},{9,... | collective-permute-start | bytes 442376 | tf_op jit(solution)/shard_map/ppermute | solution.py:40
  21.0 3.3 %collective-permute-start.7 = (bf16[8,4608]{1,0:T(8,128)(2,1)S(1)}, bf16[8,4608]{1,0:T(8,128)(2,1)S(1)}, u32[]{:S(2)}, u32[]{:S(2)}) collective-permute-start(bf16[8,4608]{1,0:T(8,128)(2,1)S(1)} %collective-permute-done.6), channel_id=1, source_target_pairs={{0,48},{1,17},{2,50},{3,19},{4,52},{5,21},{6,54},{7,23},{8,56},{9,... | collective-permute-start | bytes 221192 | tf_op jit(solution)/shard_map/ppermute | solution.py:40
  24.3 2.6 %collective-permute-done.7 = bf16[8,4608]{1,0:T(8,128)(2,1)S(1)} collective-permute-done((bf16[8,4608]{1,0:T(8,128)(2,1)S(1)}, bf16[8,4608]{1,0:T(8,128)(2,1)S(1)}, u32[]{:S(2)}, u32[]{:S(2)}) %collective-permute-start.7) | collective-permute-done | bytes 73760 | tf_op jit(solution)/shard_map/ppermute | solution.py:40
  27.0 0.9 reshape.88
  27.9 0.8 reshape.87
  28.7 1.0 constant_dynamic-update-slice_fusion.14
  29.7 3.1 %collective-permute-start.25 = (bf16[32,4864]{1,0:T(8,128)(2,1)}, bf16[32,4864]{1,0:T(8,128)(2,1)S(1)}, u32[]{:S(2)}, u32[]{:S(2)}) collective-permute-start(bf16[32,4864]{1,0:T(8,128)(2,1)} %reshape.88), channel_id=1, source_target_pairs={{0,4},{1,5},{2,6},{3,7},{4,0},{5,1},{6,2},{7,3},{8,12},{9,13},{10,... | collective-permute-start | bytes 933896 | tf_op jit(solution)/shard_map/ppermute | solution.py:40
  32.7 2.9 %collective-permute-start.13 = (bf16[32,4352]{1,0:T(8,128)(2,1)}, bf16[32,4352]{1,0:T(8,128)(2,1)S(1)}, u32[]{:S(2)}, u32[]{:S(2)}) collective-permute-start(bf16[32,4352]{1,0:T(8,128)(2,1)} %reshape.87), channel_id=1, source_target_pairs={{0,128},{1,129},{2,130},{3,131},{4,132},{5,133},{6,134},{7,135},{8... | collective-permute-start | bytes 835592 | tf_op jit(solution)/shard_map/ppermute | solution.py:40
  36.1 1.7 %constant_dynamic-update-slice_fusion.8 = bf16[64,4352]{1,0:T(8,128)(2,1)} fusion(bf16[32,4352]{1,0:T(8,128)(2,1)} %reshape.87), kind=kLoop, calls=%fused_computation.21 | loop fusion | bytes 557056
  37.8 2.3 %collective-permute-start.11 = (bf16[32,4352]{1,0:T(8,128)(2,1)}, bf16[32,4352]{1,0:T(8,128)(2,1)S(1)}, u32[]{:S(2)}, u32[]{:S(2)}) collective-permute-start(bf16[32,4352]{1,0:T(8,128)(2,1)} %reshape.87), channel_id=1, source_target_pairs={{0,64},{1,193},{2,66},{3,195},{4,68},{5,197},{6,70},{7,199},{8,72}... | collective-permute-start | bytes 835592 | tf_op jit(solution)/shard_map/ppermute | solution.py:40
  40.0 1.2 %collective-permute-start.20 = (bf16[32,4864]{1,0:T(8,128)(2,1)}, bf16[32,4864]{1,0:T(8,128)(2,1)S(1)}, u32[]{:S(2)}, u32[]{:S(2)}) collective-permute-start(bf16[32,4864]{1,0:T(8,128)(2,1)} %reshape.88), channel_id=1, source_target_pairs={{0,2},{1,7},{2,4},{3,1},{4,6},{5,3},{6,0},{7,5},{8,10},{9,15},{10,... | collective-permute-start | bytes 933896 | tf_op jit(solution)/shard_map/ppermute | solution.py:40
  41.3 1.1 %collective-permute-done.13 = bf16[32,4352]{1,0:T(8,128)(2,1)S(1)} collective-permute-done((bf16[32,4352]{1,0:T(8,128)(2,1)}, bf16[32,4352]{1,0:T(8,128)(2,1)S(1)}, u32[]{:S(2)}, u32[]{:S(2)}) %collective-permute-start.13) | collective-permute-done | bytes 278560 | tf_op jit(solution)/shard_map/ppermute | solution.py:40
  42.4 1.1 %collective-permute-start.21 = (bf16[32,4864]{1,0:T(8,128)(2,1)}, bf16[32,4864]{1,0:T(8,128)(2,1)S(1)}, u32[]{:S(2)}, u32[]{:S(2)}) collective-permute-start(bf16[32,4864]{1,0:T(8,128)(2,1)} %reshape.88), channel_id=1, source_target_pairs={{0,6},{1,3},{2,0},{3,5},{4,2},{5,7},{6,4},{7,1},{8,14},{9,11},{10,... | collective-permute-start | bytes 933896 | tf_op jit(solution)/shard_map/ppermute | solution.py:40
  43.6 0.7 constant_dynamic-update-slice_fusion.10
  44.3 4.1 %collective-permute-done.14 = bf16[32,4352]{1,0:T(8,128)(2,1)S(1)} collective-permute-done((bf16[32,4352]{1,0:T(8,128)(2,1)}, bf16[32,4352]{1,0:T(8,128)(2,1)S(1)}, u32[]{:S(2)}, u32[]{:S(2)}) %collective-permute-start.14) | collective-permute-done | bytes 278560 | tf_op jit(solution)/shard_map/ppermute | solution.py:40
  48.4 0.7 constant_dynamic-update-slice_fusion.9.refs_5_
  49.2 1.7 %collective-permute-start.15 = (bf16[64,4352]{1,0:T(8,128)(2,1)}, bf16[64,4352]{1,0:T(8,128)(2,1)}, u32[]{:S(2)}, u32[]{:S(2)}) collective-permute-start(bf16[64,4352]{1,0:T(8,128)(2,1)} %constant_dynamic-update-slice_fusion.9.refs_5_), channel_id=1, source_target_pairs={{0,2},{1,7},{2,4},{3,1},{4,6},{5,3},{6,0},{7,5},{8,10},{9,15},{10,... | collective-permute-start | bytes 1671176 | tf_op jit(solution)/shard_map/ppermute | solution.py:40
  51.3 1.8 %collective-permute-start.22 = (bf16[64,4864]{1,0:T(8,128)(2,1)S(1)}, bf16[64,4864]{1,0:T(8,128)(2,1)}, u32[]{:S(2)}, u32[]{:S(2)}) collective-permute-start(bf16[64,4864]{1,0:T(8,128)(2,1)S(1)} %constant_dynamic-update-slice_fusion.11.refs_8_), channel_id=1, source_target_pairs={{0,64},{1,193},{2,66},{3,195},{4,68},{5,197},{6,70},{7,199},{8,72}... | collective-permute-start | bytes 1867784 | tf_op jit(solution)/shard_map/ppermute | solution.py:40
  54.0 6.5 %collective-permute-done.26.refs_9_ = bf16[64,4864]{1,0:T(8,128)(2,1)} collective-permute-done((bf16[64,4864]{1,0:T(8,128)(2,1)S(1)}, bf16[64,4864]{1,0:T(8,128)(2,1)}, u32[]{:S(2)}, u32[]{:S(2)}) %collective-permute-start.26) | collective-permute-done | bytes 622624 | tf_op jit(solution)/shard_map/ppermute | solution.py:40
  60.5 1.4 %collective-permute-start.27 = (bf16[64,4864]{1,0:T(8,128)(2,1)}, bf16[64,4864]{1,0:T(8,128)(2,1)}, u32[]{:S(2)}, u32[]{:S(2)}) collective-permute-start(bf16[64,4864]{1,0:T(8,128)(2,1)} %collective-permute-done.26.refs_9_), channel_id=1, source_target_pairs={{0,64},{1,193},{2,66},{3,195},{4,68},{5,197},{6,70},{7,199},{8,72}... | collective-permute-start | bytes 1867784 | tf_op jit(solution)/shard_map/ppermute | solution.py:40
  61.9 5.2 %collective-permute-done.22.refs_9_ = bf16[64,4864]{1,0:T(8,128)(2,1)} collective-permute-done((bf16[64,4864]{1,0:T(8,128)(2,1)S(1)}, bf16[64,4864]{1,0:T(8,128)(2,1)}, u32[]{:S(2)}, u32[]{:S(2)}) %collective-permute-start.22) | collective-permute-done | bytes 622624 | tf_op jit(solution)/shard_map/ppermute | solution.py:40
  67.1 1.4 %collective-permute-start.23 = (bf16[64,4864]{1,0:T(8,128)(2,1)}, bf16[64,4864]{1,0:T(8,128)(2,1)}, u32[]{:S(2)}, u32[]{:S(2)}) collective-permute-start(bf16[64,4864]{1,0:T(8,128)(2,1)} %collective-permute-done.22.refs_9_), channel_id=1, source_target_pairs={{0,64},{1,193},{2,66},{3,195},{4,68},{5,197},{6,70},{7,199},{8,72}... | collective-permute-start | bytes 1867784 | tf_op jit(solution)/shard_map/ppermute | solution.py:40
  68.8 1.2 %collective-permute-start.16 = (bf16[64,4352]{1,0:T(8,128)(2,1)}, bf16[64,4352]{1,0:T(8,128)(2,1)}, u32[]{:S(2)}, u32[]{:S(2)}) collective-permute-start(bf16[64,4352]{1,0:T(8,128)(2,1)} %collective-permute-done.12.refs_4_), channel_id=1, source_target_pairs={{0,2},{1,7},{2,4},{3,1},{4,6},{5,3},{6,0},{7,5},{8,10},{9,15},{10,... | collective-permute-start | bytes 1671176 | tf_op jit(solution)/shard_map/ppermute | solution.py:40
  70.4 3.4 %collective-permute-done.27.refs_10_ = bf16[64,4864]{1,0:T(8,128)(2,1)} collective-permute-done((bf16[64,4864]{1,0:T(8,128)(2,1)}, bf16[64,4864]{1,0:T(8,128)(2,1)}, u32[]{:S(2)}, u32[]{:S(2)}) %collective-permute-start.27) | collective-permute-done | bytes 622624 | tf_op jit(solution)/shard_map/ppermute | solution.py:40
  73.8 1.2 %collective-permute-start.28 = (bf16[64,4864]{1,0:T(8,128)(2,1)}, bf16[64,4864]{1,0:T(8,128)(2,1)S(1)}, u32[]{:S(2)}, u32[]{:S(2)}) collective-permute-start(bf16[64,4864]{1,0:T(8,128)(2,1)} %collective-permute-done.27.refs_10_), channel_id=1, source_target_pairs={{0,64},{1,193},{2,66},{3,195},{4,68},{5,197},{6,70},{7,199},{8,72}... | collective-permute-start | bytes 1867784 | tf_op jit(solution)/shard_map/ppermute | solution.py:40
  75.0 5.5 %collective-permute-done.23.refs_10_ = bf16[64,4864]{1,0:T(8,128)(2,1)} collective-permute-done((bf16[64,4864]{1,0:T(8,128)(2,1)}, bf16[64,4864]{1,0:T(8,128)(2,1)}, u32[]{:S(2)}, u32[]{:S(2)}) %collective-permute-start.23) | collective-permute-done | bytes 622624 | tf_op jit(solution)/shard_map/ppermute | solution.py:40
  80.5 1.4 %collective-permute-start.24 = (bf16[64,4864]{1,0:T(8,128)(2,1)}, bf16[64,4864]{1,0:T(8,128)(2,1)S(1)}, u32[]{:S(2)}, u32[]{:S(2)}) collective-permute-start(bf16[64,4864]{1,0:T(8,128)(2,1)} %collective-permute-done.23.refs_10_), channel_id=1, source_target_pairs={{0,64},{1,193},{2,66},{3,195},{4,68},{5,197},{6,70},{7,199},{8,72}... | collective-permute-start | bytes 1867784 | tf_op jit(solution)/shard_map/ppermute | solution.py:40
  82.0 1.7 %collective-permute-done.16.refs_6_ = bf16[64,4352]{1,0:T(8,128)(2,1)} collective-permute-done((bf16[64,4352]{1,0:T(8,128)(2,1)}, bf16[64,4352]{1,0:T(8,128)(2,1)}, u32[]{:S(2)}, u32[]{:S(2)}) %collective-permute-start.16) | collective-permute-done | bytes 557088 | tf_op jit(solution)/shard_map/ppermute | solution.py:40
  83.7 1.1 %collective-permute-start.17 = (bf16[64,4352]{1,0:T(8,128)(2,1)}, bf16[64,4352]{1,0:T(8,128)(2,1)S(1)}, u32[]{:S(2)}, u32[]{:S(2)}) collective-permute-start(bf16[64,4352]{1,0:T(8,128)(2,1)} %collective-permute-done.16.refs_6_), channel_id=1, source_target_pairs={{0,2},{1,7},{2,4},{3,1},{4,6},{5,3},{6,0},{7,5},{8,10},{9,15},{10,... | collective-permute-start | bytes 1671176 | tf_op jit(solution)/shard_map/ppermute | solution.py:40
  85.1 1.9 %collective-permute-done.28.refs_11_ = bf16[64,4864]{1,0:T(8,128)(2,1)S(1)} collective-permute-done((bf16[64,4864]{1,0:T(8,128)(2,1)}, bf16[64,4864]{1,0:T(8,128)(2,1)S(1)}, u32[]{:S(2)}, u32[]{:S(2)}) %collective-permute-start.28) | collective-permute-done | bytes 622624 | tf_op jit(solution)/shard_map/ppermute | solution.py:40
  87.0 3.1 %copy-done = bf16[256,14336]{1,0:T(8,128)(2,1)S(1)} copy-done((bf16[256,14336]{1,0:T(8,128)(2,1)S(1)}, bf16[256,14336]{1,0:T(8,128)(2,1)}, u32[]{:S(2)}) %copy-start) | copy-done | bytes 7340056
  90.1 7.2 %shard_map.82 = (f32[512,256]{1,0:T(8,128)S(1)}, f32[512,256]{1,0:T(8,128)S(1)}) custom-call(s32[5]{0:T(128)S(1)} %stack.61.where, bf16[256,4096]{1,0:T(8,128)(2,1)S(1)} %copy-done.1, bf16[256,4096]{1,0:T(8,128)(2,1)} %collective-permute-done.9.refs_1_, bf16[256,14336]{1,0:T(8,128)(2,1)S(1)} %copy-done, bf16[256,14336]{1,0:T(8,128)(2,1)} %collective-permute-done.10.refs_3_, ...), custom_call_target="tpu_custom_call" | custom-call | flops 2415919104 | bytes 14155776 | tf_op jit(solution)/shard_map/pallas_call | solution.py:164
  97.3 7.8 %shard_map.83 = (f32[8,16]{1,0:T(8,128)S(1)}, f32[8,16]{1,0:T(8,128)S(1)}, f32[8,16]{1,0:T(8,128)S(1)}, f32[8,16]{1,0:T(8,128)S(1)}) custom-call(s32[5]{0:T(128)S(1)} %stack.61.where, bf16[256,4096]{1,0:T(8,128)(2,1)S(1)} %copy-done.1, bf16[256,4096]{1,0:T(8,128)(2,1)} %collective-permute-done.9.refs_1_, bf16[256,14336]{1,0:T(8,128)(2,1)S(1)} %copy-done, ...), custom_call_target="tpu_custom_call" | custom-call | flops 2415919104 | bytes 14155776 | tf_op jit(solution)/shard_map/pallas_call | solution.py:164
  105.2 3.0 %collective-permute-start.29 = (f32[8,16]{1,0:T(8,128)S(1)}, f32[8,16]{1,0:T(8,128)S(1)}, u32[]{:S(2)}, u32[]{:S(2)}) collective-permute-start(f32[8,16]{1,0:T(8,128)S(1)} %get-tuple-element.32), channel_id=1, source_target_pairs={{0,1},{1,0},{2,3},{3,2},{4,5},{5,4},{6,7},{7,6},{8,9},{9,8},{10,11... | collective-permute-start | bytes 1544 | tf_op jit(solution)/shard_map/ppermute | solution.py:252
  108.2 1.7 %collective-permute-start.31 = (f32[8,16]{1,0:T(8,128)S(1)}, f32[8,16]{1,0:T(8,128)S(1)}, u32[]{:S(2)}, u32[]{:S(2)}) collective-permute-start(f32[8,16]{1,0:T(8,128)S(1)} %get-tuple-element.34), channel_id=1, source_target_pairs={{0,3},{1,2},{2,1},{3,0},{4,7},{5,6},{6,5},{7,4},{8,11},{9,10},{10,... | collective-permute-start | bytes 1544 | tf_op jit(solution)/shard_map/ppermute | solution.py:252
  109.9 0.7 collective-permute-done.30
  110.7 0.8 collective-permute-done.31
  (67 shorter events, 6.3 us)
Async XLA Ops:
  0.0 87.0 %copy-start.1 = (bf16[256,4096]{1,0:T(8,128)(2,1)S(1)}, bf16[256,4096]{1,0:T(8,128)(2,1)}, u32[]{:S(2)}) copy-start(bf16[256,4096]{1,0:T(8,128)(2,1)} %refs_0_.1) | copy-start | bytes 6291460
  0.0 81.9 %copy-start.2 = (s32[1,8]{1,0:T(1,128)S(1)}, s32[1,8]{1,0:T(1,128)}, u32[]{:S(2)}) copy-start(s32[1,8]{1,0:T(1,128)} %param.15) | copy-start | bytes 100
  0.0 8.0 %collective-permute-start.1 = (s32[256]{0:T(256)}, s32[256]{0:T(256)S(1)}, u32[]{:S(2)}, u32[]{:S(2)}) collective-permute-start(s32[256]{0:T(256)} %bitcast.36), channel_id=1, source_target_pairs={{0,1},{1,0},{2,3},{3,2},{4,5},{5,4},{6,7},{7,6},{8,9},{9,8},{10,11... | collective-permute-start | bytes 3080 | tf_op jit(solution)/shard_map/ppermute | solution.py:44
  7.7 1.3 %collective-permute-start = (bf16[4,4608]{1,0:T(4,128)(2,1)S(1)}, bf16[4,4608]{1,0:T(4,128)(2,1)S(1)}, u32[]{:S(2)}, u32[]{:S(2)}) collective-permute-start(bf16[4,4608]{1,0:T(4,128)(2,1)S(1)} %get-tuple-element.38), channel_id=1, source_target_pairs={{0,1},{1,0},{2,3},{3,2},{4,5},{5,4},{6,7},{7,6},{8,9},{9,8},{10,11... | collective-permute-start | bytes 110600 | tf_op jit(solution)/shard_map/ppermute | solution.py:44
  9.2 19.5 %collective-permute-start.10 = (bf16[256,14336]{1,0:T(8,128)(2,1)}, bf16[256,14336]{1,0:T(8,128)(2,1)}, u32[]{:S(2)}, u32[]{:S(2)}) collective-permute-start(bf16[256,14336]{1,0:T(8,128)(2,1)} %refs_2_.1), channel_id=1, source_target_pairs={{0,1},{1,0},{2,3},{3,2},{4,5},{5,4},{6,7},{7,6},{8,9},{9,8},{10,11... | collective-permute-start | bytes 22020104 | tf_op jit(solution)/shard_map/ppermute | solution.py:44
  9.5 6.3 %collective-permute-start.2 = (bf16[8,4608]{1,0:T(8,128)(2,1)S(1)}, bf16[8,4608]{1,0:T(8,128)(2,1)S(1)}, u32[]{:S(2)}, u32[]{:S(2)}) collective-permute-start(bf16[8,4608]{1,0:T(8,128)(2,1)S(1)} %select_n.58), channel_id=1, source_target_pairs={{0,8},{1,57},{2,10},{3,59},{4,12},{5,61},{6,14},{7,63},{8,16},{9,1... | collective-permute-start | bytes 221192 | tf_op jit(solution)/shard_map/ppermute | solution.py:40
  13.3 4.4 %collective-permute-start.4 = (bf16[8,4608]{1,0:T(8,128)(2,1)S(1)}, bf16[8,4608]{1,0:T(8,128)(2,1)S(1)}, u32[]{:S(2)}, u32[]{:S(2)}) collective-permute-start(bf16[8,4608]{1,0:T(8,128)(2,1)S(1)} %select_n.58), channel_id=1, source_target_pairs={{0,16},{1,49},{2,18},{3,51},{4,20},{5,53},{6,22},{7,55},{8,24},{9,... | collective-permute-start | bytes 221192 | tf_op jit(solution)/shard_map/ppermute | solution.py:40
  14.5 6.5 %collective-permute-start.6 = (bf16[8,4608]{1,0:T(8,128)(2,1)S(1)}, bf16[8,4608]{1,0:T(8,128)(2,1)S(1)}, u32[]{:S(2)}, u32[]{:S(2)}) collective-permute-start(bf16[8,4608]{1,0:T(8,128)(2,1)S(1)} %select_n.58), channel_id=1, source_target_pairs={{0,56},{1,9},{2,58},{3,11},{4,60},{5,13},{6,62},{7,15},{8,0},{9,17... | collective-permute-start | bytes 221192 | tf_op jit(solution)/shard_map/ppermute | solution.py:40
  15.2 11.7 %collective-permute-start.8 = (bf16[8,4608]{1,0:T(8,128)(2,1)S(1)}, bf16[8,4608]{1,0:T(8,128)(2,1)S(1)}, u32[]{:S(2)}, u32[]{:S(2)}) collective-permute-start(bf16[8,4608]{1,0:T(8,128)(2,1)S(1)} %select_n.58), channel_id=1, source_target_pairs={{0,48},{1,17},{2,50},{3,19},{4,52},{5,21},{6,54},{7,23},{8,56},{9,... | collective-permute-start | bytes 221192 | tf_op jit(solution)/shard_map/ppermute | solution.py:40
  15.8 5.2 %collective-permute-start.3 = (s32[2,256]{1,0:T(2,128)S(1)}, s32[2,256]{1,0:T(2,128)S(1)}, u32[]{:S(2)}, u32[]{:S(2)}) collective-permute-start(s32[2,256]{1,0:T(2,128)S(1)} %add_select_fusion.1), channel_id=1, source_target_pairs={{0,2},{2,0},{1,3},{3,1},{4,6},{6,4},{5,7},{7,5},{8,10},{10,8},{9,1... | collective-permute-start | bytes 6152 | tf_op jit(solution)/shard_map/ppermute | solution.py:212
  17.7 6.6 %collective-permute-start.5 = (bf16[16,4608]{1,0:T(8,128)(2,1)S(1)}, bf16[16,4608]{1,0:T(8,128)(2,1)S(1)}, u32[]{:S(2)}, u32[]{:S(2)}) collective-permute-start(bf16[16,4608]{1,0:T(8,128)(2,1)S(1)} %pad_maximum_fusion), channel_id=1, source_target_pairs={{0,16},{1,49},{2,18},{3,51},{4,20},{5,53},{6,22},{7,55},{8,24},{9,... | collective-permute-start | bytes 442376 | tf_op jit(solution)/shard_map/ppermute | solution.py:40
  21.0 7.7 %collective-permute-start.9 = (bf16[256,4096]{1,0:T(8,128)(2,1)}, bf16[256,4096]{1,0:T(8,128)(2,1)}, u32[]{:S(2)}, u32[]{:S(2)}) collective-permute-start(bf16[256,4096]{1,0:T(8,128)(2,1)} %refs_0_.1), channel_id=1, source_target_pairs={{0,1},{1,0},{2,3},{3,2},{4,5},{5,4},{6,7},{7,6},{8,9},{9,8},{10,11... | collective-permute-start | bytes 6291464 | tf_op jit(solution)/shard_map/ppermute | solution.py:44
  21.0 5.9 %collective-permute-start.7 = (bf16[8,4608]{1,0:T(8,128)(2,1)S(1)}, bf16[8,4608]{1,0:T(8,128)(2,1)S(1)}, u32[]{:S(2)}, u32[]{:S(2)}) collective-permute-start(bf16[8,4608]{1,0:T(8,128)(2,1)S(1)} %collective-permute-done.6), channel_id=1, source_target_pairs={{0,48},{1,17},{2,50},{3,19},{4,52},{5,21},{6,54},{7,23},{8,56},{9,... | collective-permute-start | bytes 221192 | tf_op jit(solution)/shard_map/ppermute | solution.py:40
  29.7 21.2 %collective-permute-start.25 = (bf16[32,4864]{1,0:T(8,128)(2,1)}, bf16[32,4864]{1,0:T(8,128)(2,1)S(1)}, u32[]{:S(2)}, u32[]{:S(2)}) collective-permute-start(bf16[32,4864]{1,0:T(8,128)(2,1)} %reshape.88), channel_id=1, source_target_pairs={{0,4},{1,5},{2,6},{3,7},{4,0},{5,1},{6,2},{7,3},{8,12},{9,13},{10,... | collective-permute-start | bytes 933896 | tf_op jit(solution)/shard_map/ppermute | solution.py:40
  32.7 9.7 %collective-permute-start.13 = (bf16[32,4352]{1,0:T(8,128)(2,1)}, bf16[32,4352]{1,0:T(8,128)(2,1)S(1)}, u32[]{:S(2)}, u32[]{:S(2)}) collective-permute-start(bf16[32,4352]{1,0:T(8,128)(2,1)} %reshape.87), channel_id=1, source_target_pairs={{0,128},{1,129},{2,130},{3,131},{4,132},{5,133},{6,134},{7,135},{8... | collective-permute-start | bytes 835592 | tf_op jit(solution)/shard_map/ppermute | solution.py:40
  35.7 12.8 %collective-permute-start.14 = (bf16[32,4352]{1,0:T(8,128)(2,1)}, bf16[32,4352]{1,0:T(8,128)(2,1)S(1)}, u32[]{:S(2)}, u32[]{:S(2)}) collective-permute-start(bf16[32,4352]{1,0:T(8,128)(2,1)} %reshape.87), channel_id=1, source_target_pairs={{0,192},{1,65},{2,194},{3,67},{4,196},{5,69},{6,198},{7,71},{8,200... | collective-permute-start | bytes 835592 | tf_op jit(solution)/shard_map/ppermute | solution.py:40
  37.8 15.3 %collective-permute-start.11 = (bf16[32,4352]{1,0:T(8,128)(2,1)}, bf16[32,4352]{1,0:T(8,128)(2,1)S(1)}, u32[]{:S(2)}, u32[]{:S(2)}) collective-permute-start(bf16[32,4352]{1,0:T(8,128)(2,1)} %reshape.87), channel_id=1, source_target_pairs={{0,64},{1,193},{2,66},{3,195},{4,68},{5,197},{6,70},{7,199},{8,72}... | collective-permute-start | bytes 835592 | tf_op jit(solution)/shard_map/ppermute | solution.py:40
  40.0 11.2 %collective-permute-start.20 = (bf16[32,4864]{1,0:T(8,128)(2,1)}, bf16[32,4864]{1,0:T(8,128)(2,1)S(1)}, u32[]{:S(2)}, u32[]{:S(2)}) collective-permute-start(bf16[32,4864]{1,0:T(8,128)(2,1)} %reshape.88), channel_id=1, source_target_pairs={{0,2},{1,7},{2,4},{3,1},{4,6},{5,3},{6,0},{7,5},{8,10},{9,15},{10,... | collective-permute-start | bytes 933896 | tf_op jit(solution)/shard_map/ppermute | solution.py:40
  42.4 8.8 %collective-permute-start.21 = (bf16[32,4864]{1,0:T(8,128)(2,1)}, bf16[32,4864]{1,0:T(8,128)(2,1)S(1)}, u32[]{:S(2)}, u32[]{:S(2)}) collective-permute-start(bf16[32,4864]{1,0:T(8,128)(2,1)} %reshape.88), channel_id=1, source_target_pairs={{0,6},{1,3},{2,0},{3,5},{4,2},{5,7},{6,4},{7,1},{8,14},{9,11},{10,... | collective-permute-start | bytes 933896 | tf_op jit(solution)/shard_map/ppermute | solution.py:40
  49.2 19.5 %collective-permute-start.15 = (bf16[64,4352]{1,0:T(8,128)(2,1)}, bf16[64,4352]{1,0:T(8,128)(2,1)}, u32[]{:S(2)}, u32[]{:S(2)}) collective-permute-start(bf16[64,4352]{1,0:T(8,128)(2,1)} %constant_dynamic-update-slice_fusion.9.refs_5_), channel_id=1, source_target_pairs={{0,2},{1,7},{2,4},{3,1},{4,6},{5,3},{6,0},{7,5},{8,10},{9,15},{10,... | collective-permute-start | bytes 1671176 | tf_op jit(solution)/shard_map/ppermute | solution.py:40
  50.9 9.6 %collective-permute-start.26 = (bf16[64,4864]{1,0:T(8,128)(2,1)S(1)}, bf16[64,4864]{1,0:T(8,128)(2,1)}, u32[]{:S(2)}, u32[]{:S(2)}) collective-permute-start(bf16[64,4864]{1,0:T(8,128)(2,1)S(1)} %constant_dynamic-update-slice_fusion.13.refs_8_), channel_id=1, source_target_pairs={{0,64},{1,193},{2,66},{3,195},{4,68},{5,197},{6,70},{7,199},{8,72}... | collective-permute-start | bytes 1867784 | tf_op jit(solution)/shard_map/ppermute | solution.py:40
  51.3 15.8 %collective-permute-start.22 = (bf16[64,4864]{1,0:T(8,128)(2,1)S(1)}, bf16[64,4864]{1,0:T(8,128)(2,1)}, u32[]{:S(2)}, u32[]{:S(2)}) collective-permute-start(bf16[64,4864]{1,0:T(8,128)(2,1)S(1)} %constant_dynamic-update-slice_fusion.11.refs_8_), channel_id=1, source_target_pairs={{0,64},{1,193},{2,66},{3,195},{4,68},{5,197},{6,70},{7,199},{8,72}... | collective-permute-start | bytes 1867784 | tf_op jit(solution)/shard_map/ppermute | solution.py:40
  53.8 15.0 %collective-permute-start.12 = (bf16[64,4352]{1,0:T(8,128)(2,1)}, bf16[64,4352]{1,0:T(8,128)(2,1)}, u32[]{:S(2)}, u32[]{:S(2)}) collective-permute-start(bf16[64,4352]{1,0:T(8,128)(2,1)} %constant_dynamic-update-slice_fusion.7.refs_4_), channel_id=1, source_target_pairs={{0,2},{1,7},{2,4},{3,1},{4,6},{5,3},{6,0},{7,5},{8,10},{9,15},{10,... | collective-permute-start | bytes 1671176 | tf_op jit(solution)/shard_map/ppermute | solution.py:40
  60.5 13.3 %collective-permute-start.27 = (bf16[64,4864]{1,0:T(8,128)(2,1)}, bf16[64,4864]{1,0:T(8,128)(2,1)}, u32[]{:S(2)}, u32[]{:S(2)}) collective-permute-start(bf16[64,4864]{1,0:T(8,128)(2,1)} %collective-permute-done.26.refs_9_), channel_id=1, source_target_pairs={{0,64},{1,193},{2,66},{3,195},{4,68},{5,197},{6,70},{7,199},{8,72}... | collective-permute-start | bytes 1867784 | tf_op jit(solution)/shard_map/ppermute | solution.py:40
  67.1 13.3 %collective-permute-start.23 = (bf16[64,4864]{1,0:T(8,128)(2,1)}, bf16[64,4864]{1,0:T(8,128)(2,1)}, u32[]{:S(2)}, u32[]{:S(2)}) collective-permute-start(bf16[64,4864]{1,0:T(8,128)(2,1)} %collective-permute-done.22.refs_9_), channel_id=1, source_target_pairs={{0,64},{1,193},{2,66},{3,195},{4,68},{5,197},{6,70},{7,199},{8,72}... | collective-permute-start | bytes 1867784 | tf_op jit(solution)/shard_map/ppermute | solution.py:40
  68.7 13.3 %collective-permute-start.18 = (bf16[64,4352]{1,0:T(8,128)(2,1)}, bf16[64,4352]{1,0:T(8,128)(2,1)}, u32[]{:S(2)}, u32[]{:S(2)}) collective-permute-start(bf16[64,4352]{1,0:T(8,128)(2,1)} %collective-permute-done.15.refs_5_), channel_id=1, source_target_pairs={{0,2},{1,7},{2,4},{3,1},{4,6},{5,3},{6,0},{7,5},{8,10},{9,15},{10,... | collective-permute-start | bytes 1671176 | tf_op jit(solution)/shard_map/ppermute | solution.py:40
  68.8 14.9 %collective-permute-start.16 = (bf16[64,4352]{1,0:T(8,128)(2,1)}, bf16[64,4352]{1,0:T(8,128)(2,1)}, u32[]{:S(2)}, u32[]{:S(2)}) collective-permute-start(bf16[64,4352]{1,0:T(8,128)(2,1)} %collective-permute-done.12.refs_4_), channel_id=1, source_target_pairs={{0,2},{1,7},{2,4},{3,1},{4,6},{5,3},{6,0},{7,5},{8,10},{9,15},{10,... | collective-permute-start | bytes 1671176 | tf_op jit(solution)/shard_map/ppermute | solution.py:40
  73.8 13.2 %collective-permute-start.28 = (bf16[64,4864]{1,0:T(8,128)(2,1)}, bf16[64,4864]{1,0:T(8,128)(2,1)S(1)}, u32[]{:S(2)}, u32[]{:S(2)}) collective-permute-start(bf16[64,4864]{1,0:T(8,128)(2,1)} %collective-permute-done.27.refs_10_), channel_id=1, source_target_pairs={{0,64},{1,193},{2,66},{3,195},{4,68},{5,197},{6,70},{7,199},{8,72}... | collective-permute-start | bytes 1867784 | tf_op jit(solution)/shard_map/ppermute | solution.py:40
  80.5 16.9 %collective-permute-start.24 = (bf16[64,4864]{1,0:T(8,128)(2,1)}, bf16[64,4864]{1,0:T(8,128)(2,1)S(1)}, u32[]{:S(2)}, u32[]{:S(2)}) collective-permute-start(bf16[64,4864]{1,0:T(8,128)(2,1)} %collective-permute-done.23.refs_10_), channel_id=1, source_target_pairs={{0,64},{1,193},{2,66},{3,195},{4,68},{5,197},{6,70},{7,199},{8,72}... | collective-permute-start | bytes 1867784 | tf_op jit(solution)/shard_map/ppermute | solution.py:40
  81.9 15.4 %collective-permute-start.19 = (bf16[64,4352]{1,0:T(8,128)(2,1)}, bf16[64,4352]{1,0:T(8,128)(2,1)S(1)}, u32[]{:S(2)}, u32[]{:S(2)}) collective-permute-start(bf16[64,4352]{1,0:T(8,128)(2,1)} %collective-permute-done.18.refs_7_), channel_id=1, source_target_pairs={{0,2},{1,7},{2,4},{3,1},{4,6},{5,3},{6,0},{7,5},{8,10},{9,15},{10,... | collective-permute-start | bytes 1671176 | tf_op jit(solution)/shard_map/ppermute | solution.py:40
  83.7 13.6 %collective-permute-start.17 = (bf16[64,4352]{1,0:T(8,128)(2,1)}, bf16[64,4352]{1,0:T(8,128)(2,1)S(1)}, u32[]{:S(2)}, u32[]{:S(2)}) collective-permute-start(bf16[64,4352]{1,0:T(8,128)(2,1)} %collective-permute-done.16.refs_6_), channel_id=1, source_target_pairs={{0,2},{1,7},{2,4},{3,1},{4,6},{5,3},{6,0},{7,5},{8,10},{9,15},{10,... | collective-permute-start | bytes 1671176 | tf_op jit(solution)/shard_map/ppermute | solution.py:40
  87.0 3.1 %copy-start = (bf16[256,14336]{1,0:T(8,128)(2,1)S(1)}, bf16[256,14336]{1,0:T(8,128)(2,1)}, u32[]{:S(2)}) copy-start(bf16[256,14336]{1,0:T(8,128)(2,1)} %refs_2_.1) | copy-start | bytes 22020100
  105.2 4.8 %collective-permute-start.29 = (f32[8,16]{1,0:T(8,128)S(1)}, f32[8,16]{1,0:T(8,128)S(1)}, u32[]{:S(2)}, u32[]{:S(2)}) collective-permute-start(f32[8,16]{1,0:T(8,128)S(1)} %get-tuple-element.32), channel_id=1, source_target_pairs={{0,1},{1,0},{2,3},{3,2},{4,5},{5,4},{6,7},{7,6},{8,9},{9,8},{10,11... | collective-permute-start | bytes 1544 | tf_op jit(solution)/shard_map/ppermute | solution.py:252
  108.2 2.5 %collective-permute-start.30 = (f32[8,16]{1,0:T(8,128)S(1)}, f32[8,16]{1,0:T(8,128)S(1)}, u32[]{:S(2)}, u32[]{:S(2)}) collective-permute-start(f32[8,16]{1,0:T(8,128)S(1)} %get-tuple-element.33), channel_id=1, source_target_pairs={{0,2},{1,3},{2,0},{3,1},{4,6},{5,7},{6,4},{7,5},{8,10},{9,11},{10,... | collective-permute-start | bytes 1544 | tf_op jit(solution)/shard_map/ppermute | solution.py:252
  108.2 3.3 %collective-permute-start.31 = (f32[8,16]{1,0:T(8,128)S(1)}, f32[8,16]{1,0:T(8,128)S(1)}, u32[]{:S(2)}, u32[]{:S(2)}) collective-permute-start(f32[8,16]{1,0:T(8,128)S(1)} %get-tuple-element.34), channel_id=1, source_target_pairs={{0,3},{1,2},{2,1},{3,0},{4,7},{5,6},{6,5},{7,4},{8,11},{9,10},{10,... | collective-permute-start | bytes 1544 | tf_op jit(solution)/shard_map/ppermute | solution.py:252
